TPU v7x, 32 devices: a whole 2x2x4 slice. The times are simulated.
32 devices in a mesh: seq: 8 (over z, x), chan: 4 (over y, core).
Axes of the slice: x: 2, y: 2, z: 4, core: 2. Of those that a mesh axis runs over, the one named last changes fastest.
Arguments:
- block_input: float32 [8, 2048, 768], P(None, 'seq'), may hold values from -6 to 6
- lengths: int32 [8], replicated, may hold values from 256 to 2048, as said below
- ln1_gain: float32 [768], replicated, may hold values from 0.5 to 1.5
- ln1_bias: float32 [768], replicated, may hold values from -1.75 to 1.75
- input_weight: float32 [768, 3, 768], P(None, None, 'chan'), may hold values from -0.21875 to 0.21875
- input_bias: float32 [3, 768], P(None, 'chan'), may hold values from -1.75 to 1.75
- conv_w: float32 [3, 3, 768], P(None, None, 'chan'), may hold values from -3.5 to 3.5
- conv_b: float32 [3, 768], P(None, 'chan'), may hold values from -1.75 to 1.75
- filt_w1: float32 [33, 64], replicated, may hold values from -6 to 6
- filt_b1: float32 [64], replicated, may hold values from -3.140625 to 3.140625
- filt_w2: float32 [64, 64], replicated, may hold values from -7.5 to 7.5
- filt_b2: float32 [64], replicated, may hold values from -3.140625 to 3.140625
- filt_w3: float32 [64, 768], P(None, 'chan'), may hold values from -0.125 to 0.125
- decay: float32 [768], P('chan'), may hold values from 0.00024414062 to 0.06
- skip: float32 [768], P('chan'), may hold values from -6 to 6
- output_weight: float32 [768, 768], P('chan'), may hold values from -0.21875 to 0.21875
- output_bias: float32 [768], replicated, may hold values from -1.75 to 1.75
- ln2_gain: float32 [768], replicated, may hold values from 0.5 to 1.5
- ln2_bias: float32 [768], replicated, may hold values from -1.75 to 1.75
- up_weight: float32 [768, 3072], P(None, 'chan'), may hold values from -0.21875 to 0.21875
- up_bias: float32 [3072], P('chan'), may hold values from -1.75 to 1.75
- down_weight: float32 [3072, 768], P('chan'), may hold values from -0.109375 to 0.109375
- down_bias: float32 [768], replicated, may hold values from -1.75 to 1.75
- cotangent: float32 [8, 2048, 768], P(None, 'seq'), may hold values from -6 to 6
Outputs:
- output: float32 [8, 2048, 768], P(None, 'seq')
- grad_x: float32 [8, 2048, 768], P(None, 'seq')
- grad_ln1_gain: float32 [768], replicated
- grad_ln1_bias: float32 [768], replicated
- grad_w_in: float32 [768, 3, 768], P(None, None, 'chan')
- grad_b_in: float32 [3, 768], P(None, 'chan')
- grad_conv_w: float32 [3, 3, 768], P(None, None, 'chan')
- grad_conv_b: float32 [3, 768], P(None, 'chan')
- grad_filt_w1: float32 [33, 64], replicated
- grad_filt_b1: float32 [64], replicated
- grad_filt_w2: float32 [64, 64], replicated
- grad_filt_b2: float32 [64], replicated
- grad_filt_w3: float32 [64, 768], P(None, 'chan')
- grad_decay: float32 [768], P('chan')
- grad_skip: float32 [768], P('chan')
- grad_w_out: float32 [768, 768], P('chan')
- grad_b_out: float32 [768], replicated
- grad_ln2_gain: float32 [768], replicated
- grad_ln2_bias: float32 [768], replicated
- grad_w_fc1: float32 [768, 3072], P(None, 'chan')
- grad_b_fc1: float32 [3072], P('chan')
- grad_w_fc2: float32 [3072, 768], P('chan')
- grad_b_fc2: float32 [768], replicated
Inputs may be any that keep to these rules, and one draw needn't show every extreme that they name: `lengths`: each sequence is valid up to its length; exactly one sequence has the full length 2048, the others are shorter.
All inputs are finite; a program needn't handle non-finite values.
Results may differ from a plain program's by a relative error of at most 0.0003.
Values sent between devices are 32-bit elements; how exact they have to be, the bound alone decides.
No kernel may reach another device: no remote copies, remote signals or barrier semaphores. Data moves between devices by JAX's collectives and lax.ppermute only.
A program may use at most 256 MiB of HBM per device.

v0:
```python
from functools import partial
import math

import jax
import jax.numpy as jnp
from jax import lax
from jax.sharding import PartitionSpec as P

EPSILON = 1e-05
HIGH_ACCURACY = lax.Precision.HIGHEST


def shifted(block, axis, distance):
    devices = range(lax.axis_size(axis))
    route = [(i - distance, i) for i in devices if i - distance in devices]
    return lax.ppermute(block, axis, route)


def layer_norm(values, gain, offset):
    average = jnp.mean(values, -1, keepdims=True)
    centered = values - average
    variance = jnp.mean(centered * centered, -1, keepdims=True)
    return centered * lax.rsqrt(variance + EPSILON) * gain + offset


def position_features(place_values, seq_length, emb_width):
    band_count = (emb_width - 1) // 2
    frequency = jnp.linspace(0.0001, band_count - 1, band_count).astype(jnp.float32)
    phases = 2.0 * math.pi * place_values[:, None] * frequency[None, :] / seq_length
    return jnp.concatenate(
        [(place_values / (seq_length - 1))[:, None], jnp.cos(phases), -jnp.sin(phases)], 1
    )


def implicit_filter(features, place_values, filt_w1, filt_b1, filt_w2, filt_b2, filt_w3, decay):
    first_layer = jnp.sin(jnp.dot(features, filt_w1, precision=HIGH_ACCURACY) + filt_b1)
    second_layer = jnp.sin(jnp.dot(first_layer, filt_w2, precision=HIGH_ACCURACY) + filt_b2)
    raw_kernel = jnp.dot(second_layer, filt_w3, precision=HIGH_ACCURACY)
    return raw_kernel * jnp.exp(-decay[None, :] * place_values[:, None])


def exact_gelu(values):
    return jax.nn.gelu(values, approximate=False)


def tables(count_rows, count_cols):
    turns = (
        jnp.arange(count_rows, dtype=jnp.int32)[:, None]
        * jnp.arange(count_cols, dtype=jnp.int32)[None, :]
        % count_rows
    )
    phases = turns.astype(jnp.float32) * (2.0 * math.pi / count_rows)
    return (jnp.cos(phases), jnp.sin(phases))


def rotate(cos_tab, sin_tab, real, imag, sign, form):
    first_part = jnp.einsum(form, cos_tab, real, precision=HIGH_ACCURACY)
    second_part = jnp.einsum(form, sin_tab, imag, precision=HIGH_ACCURACY)
    third_part = jnp.einsum(form, cos_tab, imag, precision=HIGH_ACCURACY)
    fourth_part = jnp.einsum(form, sin_tab, real, precision=HIGH_ACCURACY)
    return (first_part - sign * second_part, third_part + sign * fourth_part)


def to_spectrum(cos_tab, sin_tab, signal):
    real = jnp.einsum("wp,spc->swc", cos_tab, signal, precision=HIGH_ACCURACY)
    imag = -jnp.einsum("wp,spc->swc", sin_tab, signal, precision=HIGH_ACCURACY)
    return (real, imag)


def time_domain(cos_tab, sin_tab, real, imag):
    return jnp.einsum("wp,swc->spc", cos_tab, real, precision=HIGH_ACCURACY) - jnp.einsum(
        "wp,swc->spc", sin_tab, imag, precision=HIGH_ACCURACY
    )


def earlier_block(values):
    return jnp.pad(values, ((0, 0), (1, 0), (0, 0), (0, 0)))[:, :-1]


def later_block(values):
    return jnp.pad(values, ((0, 0), (0, 1), (0, 0), (0, 0)))[:, 1:]


def on_device(
    block_input,
    lengths,
    ln1_gain,
    ln1_bias,
    input_weight,
    input_bias,
    conv_w,
    conv_b,
    filt_w1,
    filt_b1,
    filt_w2,
    filt_b2,
    filt_w3,
    decay,
    skip,
    output_weight,
    output_bias,
    ln2_gain,
    ln2_bias,
    up_weight,
    up_bias,
    down_weight,
    down_bias,
    cotangent,
):
    block = block_input.shape[1]
    blocks = lax.axis_size("seq")
    share = 2 * block // blocks
    seq_index = lax.axis_index("seq")
    places = seq_index * block + jnp.arange(block, dtype=jnp.int32)
    place_values = places.astype(jnp.float32)
    mask = (places[None, :] < lengths[:, None]).astype(jnp.float32)[:, :, None]
    first_normed, norm1_pull = jax.vjp(layer_norm, block_input, ln1_gain, ln1_bias)
    input_projected = (
        jnp.einsum("spd,dkc->spkc", first_normed, input_weight, precision=HIGH_ACCURACY)
        + input_bias
    )
    rims = shifted(input_projected[:, block - 2 :], "seq", 1)
    extended = jnp.concatenate([rims, input_projected], 1)
    short = (
        conv_w[0] * extended[:, :block]
        + conv_w[1] * extended[:, 1 : block + 1]
        + conv_w[2] * extended[:, 2:]
        + conv_b
    )
    gate_out = short[:, :, 0]
    gate_in = short[:, :, 1]
    values = short[:, :, 2]
    signal = values * gate_in * mask
    cos_tab, sin_tab = tables(2 * block, block)
    block_cos, block_sin = tables(2 * blocks, blocks)
    own_freq = seq_index * share + jnp.arange(share, dtype=jnp.int32)
    parity = (1 - 2 * (own_freq % 2)).astype(jnp.float32)[:, None]
    features = position_features(place_values, blocks * block, filt_w1.shape[0])
    kernel, filter_pull = jax.vjp(
        partial(implicit_filter, features, place_values),
        filt_w1,
        filt_b1,
        filt_w2,
        filt_b2,
        filt_w3,
        decay,
    )
    signal_re, signal_im = to_spectrum(cos_tab, sin_tab, signal)
    kernel_re, kernel_im = to_spectrum(cos_tab, sin_tab, kernel[None])
    signal_re, signal_im, kernel_re, kernel_im = (
        lax.all_to_all(signal_re[:, None], "seq", split_axis=2, concat_axis=1, tiled=True),
        lax.all_to_all(signal_im[:, None], "seq", split_axis=2, concat_axis=1, tiled=True),
        lax.all_to_all(kernel_re[:, None], "seq", split_axis=2, concat_axis=1, tiled=True),
        lax.all_to_all(kernel_im[:, None], "seq", split_axis=2, concat_axis=1, tiled=True),
    )
    zq_re, zq_im = rotate(block_cos, block_sin, signal_re, signal_im, -1.0, "qk,skfc->sqfc")
    hq_re, hq_im = rotate(block_cos, block_sin, kernel_re, kernel_im, -1.0, "qk,skfc->sqfc")
    prod_re = zq_re * hq_re - zq_im * hq_im
    prod_im = zq_re * hq_im + zq_im * hq_re
    joined_re, joined_im = rotate(block_cos, block_sin, prod_re, prod_im, 1.0, "qj,sqfc->sjfc")
    joined_re = joined_re / (2 * blocks)
    joined_im = joined_im / (2 * blocks)
    folded_re = joined_re + parity * earlier_block(joined_re)
    folded_im = joined_im + parity * earlier_block(joined_im)
    folded_re, folded_im = (
        lax.all_to_all(folded_re, "seq", split_axis=1, concat_axis=2, tiled=True),
        lax.all_to_all(folded_im, "seq", split_axis=1, concat_axis=2, tiled=True),
    )
    convolved = time_domain(cos_tab, sin_tab, folded_re[:, 0], folded_im[:, 0]) / (2 * block)
    conv_sum = convolved + skip * signal
    mixer_output = conv_sum * gate_out
    partial_mix = jnp.einsum("spc,cd->spd", mixer_output, output_weight, precision=HIGH_ACCURACY)
    hidden_state = block_input + lax.psum(partial_mix, "chan") + output_bias
    second_normed2 = layer_norm(hidden_state, ln2_gain, ln2_bias)
    before = jnp.einsum("spd,df->spf", second_normed2, up_weight, precision=HIGH_ACCURACY) + up_bias
    active_units, gelu_pull = jax.vjp(exact_gelu, before)
    feed = lax.psum(
        jnp.einsum("spf,fd->spd", active_units, down_weight, precision=HIGH_ACCURACY), "chan"
    )
    output = hidden_state + feed + down_bias
    grad_b_fc2 = jnp.sum(cotangent, (0, 1))
    grad_w_fc2 = jnp.einsum("spf,spd->fd", active_units, cotangent, precision=HIGH_ACCURACY)
    grad_active = jnp.einsum("spd,fd->spf", cotangent, down_weight, precision=HIGH_ACCURACY)
    grad_before = gelu_pull(grad_active)[0]
    grad_w_fc1 = jnp.einsum("spd,spf->df", second_normed2, grad_before, precision=HIGH_ACCURACY)
    grad_b_fc1 = jnp.sum(grad_before, (0, 1))
    grad_normed2 = lax.psum(
        jnp.einsum("spf,df->spd", grad_before, up_weight, precision=HIGH_ACCURACY), "chan"
    )
    norm2_pull = jax.vjp(layer_norm, hidden_state, ln2_gain, ln2_bias)[1]
    grad_hidden_norm, grad_ln2_gain, grad_ln2_bias = norm2_pull(grad_normed2)
    grad_hidden = cotangent + grad_hidden_norm
    grad_b_out = jnp.sum(grad_hidden, (0, 1))
    grad_w_out = jnp.einsum("spc,spd->cd", mixer_output, grad_hidden, precision=HIGH_ACCURACY)
    grad_mixed = jnp.einsum("spd,cd->spc", grad_hidden, output_weight, precision=HIGH_ACCURACY)
    grad_conv = grad_mixed * gate_out
    grad_gate_out = grad_mixed * conv_sum
    grad_skip = jnp.sum(grad_conv * signal, (0, 1))
    back_re, back_im = to_spectrum(cos_tab, sin_tab, grad_conv)
    back_re = back_re / (2 * block)
    back_im = back_im / (2 * block)
    back_re, back_im = (
        lax.all_to_all(back_re[:, None], "seq", split_axis=2, concat_axis=1, tiled=True),
        lax.all_to_all(back_im[:, None], "seq", split_axis=2, concat_axis=1, tiled=True),
    )
    unfold_re = back_re + parity * later_block(back_re)
    unfold_im = back_im + parity * later_block(back_im)
    dprod_re, dprod_im = rotate(block_cos, block_sin, unfold_re, unfold_im, -1.0, "qj,sjfc->sqfc")
    dprod_re = dprod_re / (2 * blocks)
    dprod_im = dprod_im / (2 * blocks)
    dzq_re = hq_re * dprod_re + hq_im * dprod_im
    dzq_im = hq_re * dprod_im - hq_im * dprod_re
    dhq_re = jnp.sum(zq_re * dprod_re + zq_im * dprod_im, 0, keepdims=True)
    dhq_im = jnp.sum(zq_re * dprod_im - zq_im * dprod_re, 0, keepdims=True)
    dsig_re, dsig_im = rotate(block_cos, block_sin, dzq_re, dzq_im, 1.0, "qk,sqfc->skfc")
    dker_re, dker_im = rotate(block_cos, block_sin, dhq_re, dhq_im, 1.0, "qk,sqfc->skfc")
    dsig_re, dsig_im, dker_re, dker_im = (
        lax.all_to_all(dsig_re, "seq", split_axis=1, concat_axis=2, tiled=True),
        lax.all_to_all(dsig_im, "seq", split_axis=1, concat_axis=2, tiled=True),
        lax.all_to_all(dker_re, "seq", split_axis=1, concat_axis=2, tiled=True),
        lax.all_to_all(dker_im, "seq", split_axis=1, concat_axis=2, tiled=True),
    )
    grad_signal = time_domain(cos_tab, sin_tab, dsig_re[:, 0], dsig_im[:, 0]) + grad_conv * skip
    grad_kernel = time_domain(cos_tab, sin_tab, dker_re[:, 0], dker_im[:, 0])[0]
    grad_fw1, grad_fb1, grad_fw2, grad_fb2, grad_fw3, grad_decay = filter_pull(grad_kernel)
    grad_short = jnp.stack(
        [grad_gate_out, grad_signal * values * mask, grad_signal * gate_in * mask], 2
    )
    grad_conv_b = jnp.sum(grad_short, (0, 1))
    grad_conv_w = jnp.stack(
        [jnp.sum(grad_short * extended[:, offset : offset + block], (0, 1)) for offset in range(3)]
    )
    grad_extended = (
        jnp.pad(conv_w[0] * grad_short, ((0, 0), (0, 2), (0, 0), (0, 0)))
        + jnp.pad(conv_w[1] * grad_short, ((0, 0), (1, 1), (0, 0), (0, 0)))
        + jnp.pad(conv_w[2] * grad_short, ((0, 0), (2, 0), (0, 0), (0, 0)))
    )
    returned = shifted(grad_extended[:, :2], "seq", -1)
    grad_proj = grad_extended[:, 2:] + jnp.pad(returned, ((0, 0), (block - 2, 0), (0, 0), (0, 0)))
    grad_b_in = jnp.sum(grad_proj, (0, 1))
    grad_w_in = jnp.einsum("spd,spkc->dkc", first_normed, grad_proj, precision=HIGH_ACCURACY)
    grad_normed = lax.psum(
        jnp.einsum("spkc,dkc->spd", grad_proj, input_weight, precision=HIGH_ACCURACY), "chan"
    )
    grad_x_norm, grad_ln1_gain, grad_ln1_bias = norm1_pull(grad_normed)
    grad_x = grad_hidden + grad_x_norm
    (
        grad_ln1_gain,
        grad_ln1_bias,
        grad_w_in,
        grad_b_in,
        grad_conv_w,
        grad_conv_b,
        grad_fw3,
        grad_decay,
        grad_skip,
        grad_w_out,
        grad_b_out,
        grad_ln2_gain,
        grad_ln2_bias,
        grad_w_fc1,
        grad_b_fc1,
        grad_w_fc2,
        grad_b_fc2,
    ) = lax.psum(
        (
            grad_ln1_gain,
            grad_ln1_bias,
            grad_w_in,
            grad_b_in,
            grad_conv_w,
            grad_conv_b,
            grad_fw3,
            grad_decay,
            grad_skip,
            grad_w_out,
            grad_b_out,
            grad_ln2_gain,
            grad_ln2_bias,
            grad_w_fc1,
            grad_b_fc1,
            grad_w_fc2,
            grad_b_fc2,
        ),
        "seq",
    )
    grad_fw1, grad_fb1, grad_fw2, grad_fb2 = lax.psum(
        (grad_fw1, grad_fb1, grad_fw2, grad_fb2), ("seq", "chan")
    )
    return (
        output,
        grad_x,
        grad_ln1_gain,
        grad_ln1_bias,
        grad_w_in,
        grad_b_in,
        grad_conv_w,
        grad_conv_b,
        grad_fw1,
        grad_fb1,
        grad_fw2,
        grad_fb2,
        grad_fw3,
        grad_decay,
        grad_skip,
        grad_w_out,
        grad_b_out,
        grad_ln2_gain,
        grad_ln2_bias,
        grad_w_fc1,
        grad_b_fc1,
        grad_w_fc2,
        grad_b_fc2,
    )


def solution(mesh):
    in_specs = (
        P(None, "seq", None),
        P(),
        P(),
        P(),
        P(None, None, "chan"),
        P(None, "chan"),
        P(None, None, "chan"),
        P(None, "chan"),
        P(),
        P(),
        P(),
        P(),
        P(None, "chan"),
        P("chan"),
        P("chan"),
        P("chan", None),
        P(),
        P(),
        P(),
        P(None, "chan"),
        P("chan"),
        P("chan", None),
        P(),
        P(None, "seq", None),
    )
    out_specs = (
        P(None, "seq", None),
        P(None, "seq", None),
        P(),
        P(),
        P(None, None, "chan"),
        P(None, "chan"),
        P(None, None, "chan"),
        P(None, "chan"),
        P(),
        P(),
        P(),
        P(),
        P(None, "chan"),
        P("chan"),
        P("chan"),
        P("chan", None),
        P(),
        P(),
        P(),
        P(None, "chan"),
        P("chan"),
        P("chan", None),
        P(),
    )
    return jax.shard_map(
        on_device, mesh=mesh, in_specs=in_specs, out_specs=out_specs, check_vma=False
    )
```

profile of v0, /device:TPU:0, one launch (start us, length us, event | category | flops | bytes accessed | tf_op | source)
XLA Modules:
  0.0 2053.2 jit_solution(15090760110083479990)
XLA Ops:
  32.0 14.5 broadcast_add_fusion
  110.1 79.4 %all-to-all-done.1 = f32[8,1,512,192]{3,0,1,2:T(8,128)} async-done(((f32[8,1,512,192]{3,0,1,2:T(8,128)}), f32[8,1,512,192]{3,0,1,2:T(8,128)}, u32[]{:S(2)}, u32[]{:S(2)}) %all-to-all-start.1) | async-done | bytes 3145760 | tf_op jit(solution)/shard_map/all_to_all | solution.py:152
  228.2 58.9 %all-to-all-done = f32[8,1,512,192]{3,0,1,2:T(8,128)} async-done(((f32[8,1,512,192]{3,0,1,2:T(8,128)}), f32[8,1,512,192]{3,0,1,2:T(8,128)}, u32[]{:S(2)}, u32[]{:S(2)}) %all-to-all-start) | async-done | bytes 3145760 | tf_op jit(solution)/shard_map/all_to_all | solution.py:151
  300.0 14.4 multiply_subtract_fusion.1
  367.9 87.0 %all-to-all-done.4 = f32[8,8,64,192]{3,2,0,1:T(8,128)} async-done(((f32[8,8,64,192]{3,2,0,1:T(8,128)}), f32[8,8,64,192]{3,2,0,1:T(8,128)}, u32[]{:S(2)}, u32[]{:S(2)}) %all-to-all-start.4) | async-done | bytes 3145760 | tf_op jit(solution)/shard_map/all_to_all | solution.py:166
  471.7 80.3 %all-to-all-done.5 = f32[8,8,64,192]{3,2,0,1:T(8,128)} async-done(((f32[8,8,64,192]{3,2,0,1:T(8,128)}), f32[8,8,64,192]{3,2,0,1:T(8,128)}, u32[]{:S(2)}, u32[]{:S(2)}) %all-to-all-start.5) | async-done | bytes 3145760 | tf_op jit(solution)/shard_map/all_to_all | solution.py:167
  578.9 118.3 %all-reduce.18.cloned.1.call-done = f32[8,256,768]{2,1,0:T(8,128)} async-done(((f32[8,256,768]{2,1,0:T(8,128)}), f32[8,256,768]{2,1,0:T(8,128)}) %all-reduce.18.cloned.1.call-update) | async-done | bytes 6291472 | tf_op jit(solution)/shard_map/psum | solution.py:173
  703.6 19.6 fusion.87
  737.4 20.2 fusion.395
  760.3 17.2 fusion.64
  777.5 119.9 %all-reduce.20.cloned.1.call-done = f32[8,256,768]{2,1,0:T(8,128)} async-done(((f32[8,256,768]{2,1,0:T(8,128)}), f32[8,256,768]{2,1,0:T(8,128)}) %all-reduce.20.cloned.1.call-update) | async-done | bytes 6291472 | tf_op jit(solution)/shard_map/psum | solution.py:187
  956.0 81.9 %all-to-all-done.7 = f32[8,1,512,192]{3,0,1,2:T(8,128)} async-done(((f32[8,1,512,192]{3,0,1,2:T(8,128)}), f32[8,1,512,192]{3,0,1,2:T(8,128)}, u32[]{:S(2)}, u32[]{:S(2)}) %all-to-all-start.7) | async-done | bytes 3145760 | tf_op jit(solution)/shard_map/all_to_all | solution.py:204
  1049.1 86.0 %all-to-all-done.6 = f32[8,1,512,192]{3,0,1,2:T(8,128)} async-done(((f32[8,1,512,192]{3,0,1,2:T(8,128)}), f32[8,1,512,192]{3,0,1,2:T(8,128)}, u32[]{:S(2)}, u32[]{:S(2)}) %all-to-all-start.6) | async-done | bytes 3145760 | tf_op jit(solution)/shard_map/all_to_all | solution.py:203
  1166.7 22.4 %fusion.7 = (f32[16,64,192]{2,0,1:T(8,128)}, f32[16,64,192]{2,0,1:T(8,128)}, f32[8,64,192,16]{2,3,1,0:T(8,128)}) fusion(f32[8,64,192,16]{2,3,1,0:T(8,128)} %copy-done.2, f32[8,64,192,16]{2,3,1,0:T(8,128)} %copy-done.3, f32[8,64,192,16]{2,3,1,0:T(8,128)} %multiply_add_fusion, f32[8,64,192,16]{2,3,1,0:T(8,128)} %fusion.181, f32[8,8,64,192]{3,1,2,0:T(8,128)} %copy.130, ...), kind=kOutput, calls=%fused_computation.20 | convolution fusion | flops 171050752 | bytes 36176128 | tf_op jit(solution)/shard_map/qj,sjfc->sqfc/dot_general | solution.py:58
  1238.6 70.4 %all-to-all-done.8 = f32[8,8,64,192]{3,2,0,1:T(8,128)} async-done(((f32[8,8,64,192]{3,2,0,1:T(8,128)}), f32[8,8,64,192]{3,2,0,1:T(8,128)}, u32[]{:S(2)}, u32[]{:S(2)}) %all-to-all-start.8) | async-done | bytes 3145760 | tf_op jit(solution)/shard_map/all_to_all | solution.py:218
  1313.7 20.0 fusion.62
  1345.8 60.4 %all-to-all-done.9 = f32[8,8,64,192]{3,2,0,1:T(8,128)} async-done(((f32[8,8,64,192]{3,2,0,1:T(8,128)}), f32[8,8,64,192]{3,2,0,1:T(8,128)}, u32[]{:S(2)}, u32[]{:S(2)}) %all-to-all-start.9) | async-done | bytes 3145760 | tf_op jit(solution)/shard_map/all_to_all | solution.py:219
  1450.3 23.2 %convolution_bitcast_fusion = f32[8,256,768]{2,1,0:T(8,128)} fusion(f32[768,3,192]{0,2,1:T(8,128)} %param.28, f32[8,258,3,192]{1,3,2,0:T(8,128)} %pad_add_fusion, f32[8,2,3,192]{1,3,2,0:T(8,128)S(1)} %copy.141), kind=kOutput, calls=%fused_computation.125 | convolution fusion | flops 10872815616 | bytes 12816384 | tf_op jit(solution)/shard_map/spkc,dkc->spd/dot_general | solution.py:243
  1473.6 21.1 %fusion.72 = f32[768,768]{1,0:T(8,128)} fusion(f32[8,256,768]{2,1,0:T(8,128)} %param.47, f32[8,256,768]{2,1,0:T(8,128)} %copy-done.9, f32[8,256,768]{2,1,0:T(8,128)} %copy-done.8, f32[768]{0:T(1024)S(1)} %copy-done.49), kind=kOutput, calls=%fused_computation.141 | convolution fusion | flops 14500233216 | bytes 21236736 | tf_op jit(solution)/shard_map/spf,spd->fd/dot_general | solution.py:182
  1502.7 21.0 %fusion.73 = f32[768,768]{1,0:T(8,128)} fusion(f32[8,256,768]{2,1,0:T(8,128)} %copy-done.37, f32[8,256,768]{2,1,0:T(8,128)} %copy-done.5, f32[768]{0:T(1024)S(1)} %copy-done.95, f32[768]{0:T(1024)S(1)} %copy-done.68, f32[8,256]{1,0:T(8,128)S(1)} %fusion.165, f32[8,256]{1,0:T(8,128)S(1)} %broadcast_multiply_fusion.5), kind=kOutput, calls=%fused_computation.142 | convolution fusion | flops 14501806080 | bytes 14964736 | tf_op jit(solution)/shard_map/spd,spf->df/dot_general | solution.py:185
  1557.9 137.7 %all-reduce.26.cloned.1.call-done = (f32[8,256,768]{2,1,0:T(8,128)}, f32[8,256,768]{2,1,0:T(8,128)}) async-done(((f32[8,256,768]{2,1,0:T(8,128)}, f32[8,256,768]{2,1,0:T(8,128)}), (f32[8,256,768]{2,1,0:T(8,128)}, f32[8,256,768]{2,1,0:T(8,128)})) %all-reduce.26.cloned.1.call-update) | async-done | bytes 12582928 | tf_op jit(solution)/shard_map/psum | solution.py:177
  1707.2 23.4 %fusion.88 = f32[768,3,192]{0,2,1:T(8,128)} fusion(f32[8,256,768]{2,1,0:T(8,128)} %param.24, f32[768]{0:T(1024)S(1)} %copy-done.97, f32[768]{0:T(1024)S(1)} %copy-done.72, f32[8,256]{1,0:T(8,128)S(1)} %copy-done.65, f32[8,256]{1,0:T(8,128)S(1)} %copy-done.54, f32[8,258,3,192]{1,3,2,0:T(8,128)} %pad_add_fusion, f32[8,2,3,192]{1,3,2,0:T(8,128)S(1)} %copy-done.33), kind=kOutput, calls=%fused_computation.159 | convolution fusion | flops 10879107072 | bytes 12838912 | tf_op jit(solution)/shard_map/spd,spkc->dkc/dot_general | solution.py:241
  1733.0 41.0 %all-reduce.8 = (f32[33,64]{1,0:T(8,128)}, f32[64]{0:T(128)}, f32[64,64]{1,0:T(8,128)}, f32[64]{0:T(128)}) all-reduce(f32[33,64]{1,0:T(8,128)S(1)} %fusion.162, f32[64]{0:T(128)S(1)} %get-tuple-element.95, f32[64,64]{1,0:T(8,128)S(1)} %fusion.403, f32[64]{0:T(128)S(1)} %get-tuple-element.97), channel_id=1, replica_groups=mesh['seq'=8,'chan'=4] {'seq','chan'}, use_global_device_ids=true, to_apply=%region_27.28 | all-reduce | flops 6336 | bytes 50688 | tf_op jit(solution)/shard_map/psum | solution.py:287
  1792.4 230.8 %all-reduce.24.cloned.1.call-done = (f32[768,3,192]{0,2,1:T(8,128)}, f32[192,768]{1,0:T(8,128)}, f32[768,768]{1,0:T(8,128)}, f32[768,768]{1,0:T(8,128)}) async-done(((f32[768,3,192]{0,2,1:T(8,128)}, f32[192,768]{1,0:T(8,128)}, f32[768,768]{1,0:T(8,128)}, f32[768,768]{1,0:T(8,128)}), (f32[768,3,192]{0,2,1:T(8,128)}, f32[192,768]{1,0:T(8,128)}, f32[768,768]{1,0:T(8,128)}, ...) | async-done | bytes 7077904 | tf_op jit(solution)/shard_map/psum | solution.py:265
  (369 shorter events, 568.8 us)
Async XLA Ops:
  7.2 696.4 %copy-start = (f32[768,768]{1,0:T(8,128)S(1)}, f32[768,768]{1,0:T(8,128)}, u32[]{:S(2)}) copy-start(f32[768,768]{1,0:T(8,128)} %param.43) | copy-start | bytes 7077892
  17.5 47.3 %all-to-all-start.3 = ((f32[1,1,512,192]{3,1,0,2:T(1,128)}), f32[1,1,512,192]{3,1,0,2:T(1,128)S(1)}, u32[]{:S(2)}, u32[]{:S(2)}) async-start(f32[1,1,512,192]{3,1,0,2:T(1,128)} %copy.111), calls=%async_computation.3 | async-start | bytes 1048576 | tf_op jit(solution)/shard_map/all_to_all | solution.py:154
  53.3 8.6 collective-permute-start
  64.8 26.8 %all-to-all-start.2 = ((f32[1,1,512,192]{3,1,0,2:T(1,128)}), f32[1,1,512,192]{3,1,0,2:T(1,128)S(1)}, u32[]{:S(2)}, u32[]{:S(2)}) async-start(f32[1,1,512,192]{3,1,0,2:T(1,128)} %copy.109), calls=%async_computation.2 | async-start | bytes 1048576 | tf_op jit(solution)/shard_map/all_to_all | solution.py:153
  91.7 97.9 %all-to-all-start.1 = ((f32[8,1,512,192]{3,0,1,2:T(8,128)}), f32[8,1,512,192]{3,0,1,2:T(8,128)}, u32[]{:S(2)}, u32[]{:S(2)}) async-start(f32[8,1,512,192]{3,0,1,2:T(8,128)} %copy.106), calls=%async_computation.1 | async-start | bytes 8388608 | tf_op jit(solution)/shard_map/all_to_all | solution.py:152
  189.6 97.5 %all-to-all-start = ((f32[8,1,512,192]{3,0,1,2:T(8,128)}), f32[8,1,512,192]{3,0,1,2:T(8,128)}, u32[]{:S(2)}, u32[]{:S(2)}) async-start(f32[8,1,512,192]{3,0,1,2:T(8,128)} %copy.103), calls=%async_computation | async-start | bytes 8388608 | tf_op jit(solution)/shard_map/all_to_all | solution.py:151
  357.8 97.1 %all-to-all-start.4 = ((f32[8,8,64,192]{3,2,0,1:T(8,128)}), f32[8,8,64,192]{3,2,0,1:T(8,128)}, u32[]{:S(2)}, u32[]{:S(2)}) async-start(f32[8,8,64,192]{3,2,0,1:T(8,128)} %copy.117), calls=%async_computation.4 | async-start | bytes 8388608 | tf_op jit(solution)/shard_map/all_to_all | solution.py:166
  454.9 97.1 %all-to-all-start.5 = ((f32[8,8,64,192]{3,2,0,1:T(8,128)}), f32[8,8,64,192]{3,2,0,1:T(8,128)}, u32[]{:S(2)}, u32[]{:S(2)}) async-start(f32[8,8,64,192]{3,2,0,1:T(8,128)} %copy.120), calls=%async_computation.5 | async-start | bytes 8388608 | tf_op jit(solution)/shard_map/all_to_all | solution.py:167
  459.5 237.8 %all-reduce.18.cloned.1.call-start = ((), (), s32[]{:S(2)}) async-start(), calls=%async_computation.12 | async-start | bytes 12582912 | tf_op jit(solution)/shard_map/psum | solution.py:173
  565.3 132.0 %copy-start.83 = (f32[768]{0:T(1024)S(1)}, f32[768]{0:T(1024)}, u32[]{:S(2)}) copy-start(f32[768]{0:T(1024)} %param.40) | copy-start | bytes 9220
  578.5 319.0 %all-reduce.20.cloned.1.call-start = ((), (), s32[]{:S(2)}) async-start(), calls=%async_computation.13 | async-start | bytes 12582912 | tf_op jit(solution)/shard_map/psum | solution.py:187
  939.2 98.6 %all-to-all-start.7 = ((f32[8,1,512,192]{3,0,1,2:T(8,128)}), f32[8,1,512,192]{3,0,1,2:T(8,128)}, u32[]{:S(2)}, u32[]{:S(2)}) async-start(f32[8,1,512,192]{3,0,1,2:T(8,128)} %copy.127), calls=%async_computation.7 | async-start | bytes 8388608 | tf_op jit(solution)/shard_map/all_to_all | solution.py:204
  1037.8 97.3 %all-to-all-start.6 = ((f32[8,1,512,192]{3,0,1,2:T(8,128)}), f32[8,1,512,192]{3,0,1,2:T(8,128)}, u32[]{:S(2)}, u32[]{:S(2)}) async-start(f32[8,1,512,192]{3,0,1,2:T(8,128)} %copy.123), calls=%async_computation.6 | async-start | bytes 8388608 | tf_op jit(solution)/shard_map/all_to_all | solution.py:203
  1212.0 97.1 %all-to-all-start.8 = ((f32[8,8,64,192]{3,2,0,1:T(8,128)}), f32[8,8,64,192]{3,2,0,1:T(8,128)}, u32[]{:S(2)}, u32[]{:S(2)}) async-start(f32[8,8,64,192]{3,2,0,1:T(8,128)} %copy.131), calls=%async_computation.8 | async-start | bytes 8388608 | tf_op jit(solution)/shard_map/all_to_all | solution.py:218
  1309.1 97.1 %all-to-all-start.9 = ((f32[8,8,64,192]{3,2,0,1:T(8,128)}), f32[8,8,64,192]{3,2,0,1:T(8,128)}, u32[]{:S(2)}, u32[]{:S(2)}) async-start(f32[8,8,64,192]{3,2,0,1:T(8,128)} %copy.134), calls=%async_computation.9 | async-start | bytes 8388608 | tf_op jit(solution)/shard_map/all_to_all | solution.py:219
  1313.7 381.9 %all-reduce.26.cloned.1.call-start = ((), (), s32[]{:S(2)}) async-start(), calls=%async_computation.16 | async-start | bytes 25165824 | tf_op jit(solution)/shard_map/psum | solution.py:177
  1439.3 10.3 collective-permute-start.1
  1497.1 29.0 %all-to-all-start.10 = ((f32[1,8,64,192]{3,2,0,1:T(8,128)}), f32[1,8,64,192]{3,2,0,1:T(8,128)}, u32[]{:S(2)}, u32[]{:S(2)}) async-start(f32[1,8,64,192]{3,2,0,1:T(8,128)} %copy.143), calls=%async_computation.10 | async-start | bytes 1048576 | tf_op jit(solution)/shard_map/all_to_all | solution.py:220
  1526.1 19.9 all-to-all-start.11
  1532.1 260.3 %all-reduce.22.cloned.1.call-start = ((), (), s32[]{:S(2)}) async-start(), calls=%async_computation.14 | async-start | bytes 233472 | tf_op jit(solution)/shard_map/psum | solution.py:265
  1541.3 154.3 %copy-start.54 = (f32[8,256]{1,0:T(8,128)S(1)}, f32[8,256]{1,0:T(8,128)}, u32[]{:S(2)}) copy-start(f32[8,256]{1,0:T(8,128)} %copy-done.53) | copy-start | bytes 24580
  1541.3 154.3 %copy-start.72 = (f32[768]{0:T(1024)S(1)}, f32[768]{0:T(1024)}, u32[]{:S(2)}) copy-start(f32[768]{0:T(1024)} %param.26) | copy-start | bytes 9220
  1707.2 316.0 %all-reduce.24.cloned.1.call-start = ((), (), s32[]{:S(2)}) async-start(), calls=%async_computation.15 | async-start | bytes 14155776 | tf_op jit(solution)/shard_map/psum | solution.py:265
  1792.4 251.3 %copy-start.88 = (f32[768]{0:T(1024)S(1)}, f32[768]{0:T(1024)}, u32[]{:S(2)}) copy-start(f32[768]{0:T(1024)} %get-tuple-element.121) | copy-start | bytes 9220
  (99 other events, 1556.6 us)
Sparse Core Ops, SparseCore 0:
  578.6 118.6 all-reduce.17
  777.6 119.7 all-reduce.19
  1473.7 221.7 all-reduce.25
  1707.3 73.3 all-reduce.21
  1787.3 235.8 all-reduce.23
where the time goes:
time: 2060 us; the launch traced here: 2050 us
  waiting for transfers between devices  1210 us (59%)
  matrix products  482 us (23%)
  other arithmetic  124 us (6%)
  local copies, waits for them, and re-layouts  111 us (5%)
  starting transfers between devices  69.6 us (3%)
  blocking collectives  41 us (2%)
    psum x2, waiting for transfers between devices, on_device(): lax.psum((grad_ln1_gain, grad_ln1_bias, grad_w_in, grad_b_in, grad_conv_w...  231 us
    psum x1, waiting for transfers between devices, on_device(): lax.psum(jnp.einsum('spf,fd->spd', active_units, down_weight, precision=H...  138 us
    psum x1, waiting for transfers between devices, on_device(): lax.psum(jnp.einsum('spf,df->spd', grad_before, up_weight, precision=HIGH...  120 us
    psum x1, waiting for transfers between devices, on_device(): hidden_state = block_input + lax.psum(partial_mix, 'chan') + output_bias  118 us
    all_to_all x1, waiting for transfers between devices, on_device(): lax.all_to_all(folded_re, 'seq', split_axis=1, concat_axis=2, tiled=True)  87 us
    all_to_all x1, waiting for transfers between devices, on_device(): lax.all_to_all(back_re[:, None], 'seq', split_axis=2, concat_axis=1, tile...  86 us
    all_to_all x1, waiting for transfers between devices, on_device(): lax.all_to_all(back_im[:, None], 'seq', split_axis=2, concat_axis=1, tile...  81.9 us
    all_to_all x1, waiting for transfers between devices, on_device(): lax.all_to_all(folded_im, 'seq', split_axis=1, concat_axis=2, tiled=True)  80.3 us
  transfers between devices with their start and end apart: 19, of which 12 were waited for; matrix products, arithmetic and copies ran while one was open for 15% of the time, Pallas kernels for 0%

commit v1 on v0

--- a/solution.py
+++ b/solution.py
@@ -3,7 +3,11 @@
 
 import jax
 import jax.numpy as jnp
+import ml_dtypes
+import numpy as np
 from jax import lax
+from jax.experimental import pallas as pl
+from jax.experimental.pallas import tpu as pltpu
 from jax.sharding import PartitionSpec as P
 
 EPSILON = 1e-05
@@ -81,7 +85,7 @@
     return jnp.pad(values, ((0, 0), (0, 1), (0, 0), (0, 0)))[:, 1:]
 
 
-def on_device(
+def spectral_device(
     block_input,
     lengths,
     ln1_gain,
@@ -314,6 +318,813 @@
     )
 
 
+F32 = jnp.float32
+BF16 = jnp.bfloat16
+NN = (((1,), (0,)), ((), ()))
+NT = (((1,), (1,)), ((), ()))
+TN = (((0,), (0,)), ((), ()))
+VMEM_BYTES = 56 * 2**20
+
+
+def parts_of(values):
+    high = values.astype(BF16)
+    return high, (values - high.astype(F32)).astype(BF16)
+
+
+def dot_parts(left, right, dims):
+    def one(a, b):
+        return lax.dot_general(a, b, dims, preferred_element_type=F32)
+
+    return one(left[0], right[0]) + (one(left[0], right[1]) + one(left[1], right[0]))
+
+
+def normalise(values):
+    average = jnp.mean(values, -1, keepdims=True)
+    centered = values - average
+    variance = jnp.mean(centered * centered, -1, keepdims=True)
+    scale = lax.rsqrt(variance + EPSILON)
+    return centered * scale, scale
+
+
+def norm_back(unit, scale, gain, grad):
+    lifted = grad * gain
+    mean_one = jnp.mean(lifted, -1, keepdims=True)
+    mean_two = jnp.mean(lifted * unit, -1, keepdims=True)
+    return scale * (lifted - mean_one - unit * mean_two)
+
+
+def column_sum(values):
+    return jnp.sum(values, 0, keepdims=True)
+
+
+def whole(array):
+    return pl.BlockSpec(array.shape, lambda *_: (0,) * len(array.shape))
+
+
+def scalar_spec():
+    return pl.BlockSpec(memory_space=pltpu.SMEM)
+
+
+def struct(shape, kind=F32):
+    return jax.ShapeDtypeStruct(tuple(shape), kind)
+
+
+def run_kernel(body, name, grid, in_specs, out_specs, out_shape, scratch, args, flops):
+    moved = sum(math.prod(a.shape) * a.dtype.itemsize for a in args)
+    moved += sum(math.prod(a.shape) * a.dtype.itemsize for a in out_shape)
+    return pl.pallas_call(
+        body,
+        name=name,
+        grid=grid,
+        in_specs=in_specs,
+        out_specs=out_specs,
+        out_shape=out_shape,
+        scratch_shapes=scratch,
+        compiler_params=pltpu.CompilerParams(
+            dimension_semantics=("arbitrary",) * len(grid), vmem_limit_bytes=VMEM_BYTES
+        ),
+        cost_estimate=pl.CostEstimate(flops=int(flops), bytes_accessed=int(moved), transcendentals=0),
+    )(*args)
+
+
+def wave_tables(block):
+    angles = np.pi * np.outer(2 * np.arange(block) + 1, np.arange(block)) / (2 * block)
+    table = np.concatenate([np.cos(angles), -np.sin(angles)], 0)
+
+    def both(values):
+        high = values.astype(ml_dtypes.bfloat16)
+        low = (values - high.astype(np.float64)).astype(ml_dtypes.bfloat16)
+        return jnp.asarray(high), jnp.asarray(low)
+
+    return both(table) + both(table.T / block)
+
+
+def parity_of(rows):
+    odd = lax.broadcasted_iota(jnp.int32, (rows, 1), 0) % 2
+    return (1 - 2 * odd).astype(F32)
+
+
+def filter_spectrum(kernel, tables):
+    blocks, block, width = kernel.shape
+    table_high, table_low = tables[:2]
+
+    def body(kernel_ref, high_ref, low_ref, out_ref, before_ref):
+        @pl.when(pl.program_id(0) == 0)
+        def _():
+            before_ref[...] = jnp.zeros_like(before_ref)
+
+        spectrum = dot_parts((high_ref[...], low_ref[...]), parts_of(kernel_ref[0]), NN)
+        sign = parity_of(block)
+        out_ref[0, :block] = spectrum[:block] - sign * before_ref[block:]
+        out_ref[0, block:] = spectrum[block:] + sign * before_ref[:block]
+        before_ref[...] = spectrum
+
+    return run_kernel(
+        body,
+        "filter_spectrum",
+        (blocks,),
+        [pl.BlockSpec((1, block, width), lambda b: (b, 0, 0)), whole(table_high), whole(table_low)],
+        [pl.BlockSpec((1, 2 * block, width), lambda b: (b, 0, 0))],
+        [struct((blocks, 2 * block, width))],
+        [pltpu.VMEM((2 * block, width), F32)],
+        [kernel, table_high, table_low],
+        12 * blocks * block * block * width,
+    )[0]
+
+
+def mixer_forward(own, length, x_parts, gain, offset, weight, bias, conv_w, conv_b, skip, spectrum, tables):
+    blocks, quarter, model = x_parts[0].shape
+    count = len(x_parts)
+    block = quarter * count
+    width = weight.shape[2]
+    tile = min(32, block)
+
+    def body(*refs):
+        own_ref, length_ref = refs[:2]
+        x_refs = refs[2 : 2 + count]
+        refs = refs[2 + count :]
+        gain_ref, offset_ref, weight_ref, bias_ref, conv_w_ref, conv_b_ref, skip_ref, k_ref = refs[:8]
+        th_ref, tl_ref, ih_ref, il_ref = refs[8:12]
+        nh_ref, nl_ref, proj_ref, conv_ref, s_ref = refs[12:17]
+        m_refs = refs[17 : 17 + count]
+        wh_ref, wl_ref, ext_ref, o_ref, mixed_ref = refs[17 + count :]
+        b = pl.program_id(0)
+        me = own_ref[0]
+
+        @pl.when(b == 0)
+        def _():
+            for k in range(3):
+                wh_ref[k], wl_ref[k] = parts_of(weight_ref[k])
+            ext_ref[:, :8] = jnp.zeros((3, 8, width), F32)
+
+        for k in range(count):
+            normed = normalise(x_refs[k][0])[0] * gain_ref[...] + offset_ref[...]
+            start = pl.multiple_of((me ^ k) * quarter, quarter)
+            high, low = parts_of(normed)
+            nh_ref[0, pl.ds(start, quarter), :] = high
+            nl_ref[0, pl.ds(start, quarter), :] = low
+        normed = (nh_ref[0], nl_ref[0])
+        short = []
+        for k in range(3):
+            proj = dot_parts(normed, (wh_ref[k], wl_ref[k]), NN) + bias_ref[k : k + 1, :]
+            proj_ref[0, k] = proj
+            ext_ref[k, 8 : 8 + block] = proj
+            short.append(
+                conv_w_ref[0, k : k + 1, :] * ext_ref[k, 6 : 6 + block]
+                + conv_w_ref[1, k : k + 1, :] * ext_ref[k, 7 : 7 + block]
+                + conv_w_ref[2, k : k + 1, :] * proj
+                + conv_b_ref[k : k + 1, :]
+            )
+            ext_ref[k, :8] = ext_ref[k, block : block + 8]
+        places = b * block + lax.broadcasted_iota(jnp.int32, (block, 1), 0)
+        mask = (places < length_ref[0]).astype(F32)
+        signal = short[2] * short[1] * mask
+        s_ref[b] = dot_parts((th_ref[...], tl_ref[...]), parts_of(signal), NN)
+        for r in range(0, block, tile):
+            lo = slice(r, r + tile)
+            hi = slice(block + r, block + r + tile)
+
+            def product(i, total, lo=lo, hi=hi):
+                s_re, s_im = s_ref[i, lo], s_ref[i, hi]
+                k_re, k_im = k_ref[b - i, lo], k_ref[b - i, hi]
+                return total[0] + s_re * k_re - s_im * k_im, total[1] + s_re * k_im + s_im * k_re
+
+            zero = jnp.zeros((tile, width), F32)
+            o_ref[lo], o_ref[hi] = lax.fori_loop(0, b + 1, product, (zero, zero))
+        conv = dot_parts((ih_ref[...], il_ref[...]), parts_of(o_ref[...]), NN) + skip_ref[...] * signal
+        conv_ref[0] = conv
+        mixed_ref[...] = conv * short[0]
+        for k in range(count):
+            start = pl.multiple_of((me ^ k) * quarter, quarter)
+            m_refs[k][0] = mixed_ref[pl.ds(start, quarter), :]
+
+    by_block = lambda *shape: pl.BlockSpec((1,) + shape, lambda b: (b,) + (0,) * len(shape))
+    args = [own, length, *x_parts, gain, offset, weight, bias, conv_w, conv_b, skip, spectrum, *tables]
+    in_specs = [scalar_spec(), scalar_spec()] + [by_block(quarter, model)] * count
+    in_specs += [whole(a) for a in args[2 + count :]]
+    s_shape = struct((blocks, 2 * block, width))
+    outs = run_kernel(
+        body,
+        "mixer_forward",
+        (blocks,),
+        in_specs,
+        [by_block(block, model)] * 2
+        + [by_block(3, block, width), by_block(block, width), whole(s_shape)]
+        + [by_block(quarter, width)] * count,
+        [struct((blocks, block, model), BF16)] * 2
+        + [struct((blocks, 3, block, width)), struct((blocks, block, width)), s_shape]
+        + [struct((blocks, quarter, width))] * count,
+        [
+            pltpu.VMEM((3, model, width), BF16),
+            pltpu.VMEM((3, model, width), BF16),
+            pltpu.VMEM((3, block + 8, width), F32),
+            pltpu.VMEM((2 * block, width), F32),
+            pltpu.VMEM((block, width), F32),
+        ],
+        args,
+        6 * blocks * block * width * (3 * model + 4 * block),
+    )
+    return outs[:5], outs[5:]
+
+
+def hidden_forward(m_parts, weights, x_own, cotangent, bias, gain, offset):
+    rows, width = m_parts[0].shape
+    model = x_own.shape[1]
+    count = len(m_parts)
+    step = min(128, rows)
+
+    def body(*refs):
+        m_refs, w_refs = refs[:count], refs[count : 2 * count]
+        x_ref, c_ref, bias_ref, gain_ref, offset_ref = refs[2 * count : 2 * count + 5]
+        h_ref, nh_ref, nl_ref, th_ref, tl_ref, ch_ref, cl_ref = refs[2 * count + 5 : 2 * count + 12]
+        wh_ref, wl_ref = refs[2 * count + 12 :]
+
+        @pl.when(pl.program_id(0) == 0)
+        def _():
+            for k in range(count):
+                wh_ref[k], wl_ref[k] = parts_of(w_refs[k][...])
+
+        hidden = x_ref[...] + bias_ref[...]
+        for k in range(count):
+            hidden = hidden + dot_parts(parts_of(m_refs[k][...]), (wh_ref[k], wl_ref[k]), NN)
+        h_ref[...] = hidden
+        normed = normalise(hidden)[0] * gain_ref[...] + offset_ref[...]
+        nh_ref[...], nl_ref[...] = parts_of(normed)
+        th_ref[...], tl_ref[...] = parts_of(normed.T)
+        ch_ref[...], cl_ref[...] = parts_of(c_ref[...])
+
+    row_spec = lambda n: pl.BlockSpec((step, n), lambda r: (r, 0))
+    turned = pl.BlockSpec((model, step), lambda r: (0, r))
+    args = [*m_parts, *weights, x_own, cotangent, bias, gain, offset]
+    return run_kernel(
+        body,
+        "hidden_forward",
+        (rows // step,),
+        [row_spec(width)] * count
+        + [whole(w) for w in weights]
+        + [row_spec(model)] * 2
+        + [whole(bias), whole(gain), whole(offset)],
+        [row_spec(model)] * 3 + [turned] * 2 + [row_spec(model)] * 2,
+        [struct((rows, model))]
+        + [struct((rows, model), BF16)] * 2
+        + [struct((model, rows), BF16)] * 2
+        + [struct((rows, model), BF16)] * 2,
+        [pltpu.VMEM((count, width, model), BF16)] * 2,
+        args,
+        6 * rows * model * width * count,
+    )
+
+
+def feed_forward(normed, turned, cotangent, up, up_bias, down, sums):
+    rows, model = normed[0].shape
+    units = up.shape[1]
+    step = min(256, units)
+    first = sums is None
+
+    def body(*refs):
+        nh_ref, nl_ref, th_ref, tl_ref, ch_ref, cl_ref, up_ref, bias_ref, down_ref = refs[:9]
+        feed_in, grad_in = (None, None) if first else refs[9:11]
+        feed_ref, grad_ref, gup_ref, gdown_ref, gbias_ref = refs[9 if first else 11 :]
+
+        @pl.when(pl.program_id(0) == 0)
+        def _():
+            if first:
+                feed_ref[...] = jnp.zeros_like(feed_ref)
+                grad_ref[...] = jnp.zeros_like(grad_ref)
+            else:
+                feed_ref[...] = feed_in[...]
+                grad_ref[...] = grad_in[...]
+
+        own_normed = (nh_ref[...], nl_ref[...])
+        own_cotangent = (ch_ref[...], cl_ref[...])
+        up_parts = parts_of(up_ref[...])
+        down_parts = parts_of(down_ref[...])
+        before = dot_parts(own_normed, up_parts, NN) + bias_ref[...]
+        grad_active = dot_parts(own_cotangent, down_parts, NT)
+        below = 0.5 + 0.5 * lax.erf(before * math.sqrt(0.5))
+        slope = below + before * (jnp.exp(-0.5 * before * before) * (1.0 / math.sqrt(2.0 * math.pi)))
+        active = before * below
+        grad_before = grad_active * slope
+        gbias_ref[...] = column_sum(grad_before)
+        active_parts = parts_of(active)
+        grad_parts = parts_of(grad_before)
+        feed_ref[...] += dot_parts(active_parts, down_parts, NN)
+        grad_ref[...] += dot_parts(grad_parts, up_parts, NT)
+        gup_ref[...] = dot_parts((th_ref[...], tl_ref[...]), grad_parts, NN)
+        gdown_ref[...] = dot_parts(active_parts, own_cotangent, TN)
+
+    total = struct((rows, model))
+    args = [*normed, *turned, *cotangent, up, up_bias, down] + ([] if first else list(sums))
+    columns = pl.BlockSpec((model, step), lambda t: (0, t))
+    one_row = pl.BlockSpec((1, step), lambda t: (0, t))
+    some_rows = pl.BlockSpec((step, model), lambda t: (t, 0))
+    outs = run_kernel(
+        body,
+        "feed_forward",
+        (units // step,),
+        [whole(a) for a in args[:6]] + [columns, one_row, some_rows] + [whole(a) for a in args[9:]],
+        [whole(total), whole(total), columns, some_rows, one_row],
+        [total, total, struct(up.shape), struct(down.shape), struct(up_bias.shape)],
+        [],
+        args,
+        36 * rows * model * units,
+    )
+    return outs[:2], outs[2:]
+
+
+def hidden_backward(hidden, feed, grad_normed, cotangent, m_parts, weights, gain, bias):
+    rows, model = hidden.shape
+    width = m_parts[0].shape[1]
+    count = len(m_parts)
+    step = min(128, rows)
+
+    def body(*refs):
+        h_ref, f_ref, g_ref, c_ref = refs[:4]
+        m_refs, w_refs = refs[4 : 4 + count], refs[4 + count : 4 + 2 * count]
+        gain_ref, bias_ref, out_ref, gh_ref, sum_ref = refs[4 + 2 * count : 9 + 2 * count]
+        gm_refs = refs[9 + 2 * count : 9 + 3 * count]
+        gw_refs = refs[9 + 3 * count : 9 + 4 * count]
+        wh_ref, wl_ref = refs[9 + 4 * count :]
+
+        @pl.when(pl.program_id(0) == 0)
+        def _():
+            sum_ref[...] = jnp.zeros_like(sum_ref)
+            for k in range(count):
+                wh_ref[k], wl_ref[k] = parts_of(w_refs[k][...])
+                gw_refs[k][...] = jnp.zeros_like(gw_refs[k])
+
+        hidden_rows, grad, above = h_ref[...], g_ref[...], c_ref[...]
+        out_ref[...] = hidden_rows + f_ref[...] + bias_ref[...]
+        unit, scale = normalise(hidden_rows)
+        grad_hidden = above + norm_back(unit, scale, gain_ref[...], grad)
+        gh_ref[...] = grad_hidden
+        sum_ref[0:1] += column_sum(grad * unit)
+        sum_ref[1:2] += column_sum(grad)
+        sum_ref[2:3] += column_sum(grad_hidden)
+        sum_ref[3:4] += column_sum(above)
+        parts = parts_of(grad_hidden)
+        for k in range(count):
+            gm_refs[k][...] = dot_parts(parts, (wh_ref[k], wl_ref[k]), NT)
+            gw_refs[k][...] += dot_parts(parts_of(m_refs[k][...]), parts, TN)
+
+    row_spec = lambda n: pl.BlockSpec((step, n), lambda r: (r, 0))
+    args = [hidden, feed, grad_normed, cotangent, *m_parts, *weights, gain, bias]
+    sums = struct((8, model))
+    outs = run_kernel(
+        body,
+        "hidden_backward",
+        (rows // step,),
+        [row_spec(model)] * 4 + [row_spec(width)] * count + [whole(w) for w in weights] + [whole(gain), whole(bias)],
+        [row_spec(model)] * 2 + [whole(sums)] + [row_spec(width)] * count + [whole(w) for w in weights],
+        [struct((rows, model))] * 2
+        + [sums]
+        + [struct((rows, width))] * count
+        + [struct(w.shape) for w in weights],
+        [pltpu.VMEM((count, width, model), BF16)] * 2,
+        args,
+        12 * rows * model * width * count,
+    )
+    return outs[:3], outs[3 : 3 + count], outs[3 + count :]
+
+
+def mixer_backward(own, length, gm_parts, proj, conv, s_spec, k_spec, conv_w, conv_b, skip, weight, tables):
+    blocks, quarter, width = gm_parts[0].shape
+    count = len(gm_parts)
+    block = quarter * count
+    model = weight.shape[1]
+    tile = min(32, block)
+
+    def body(*refs):
+        own_ref, length_ref = refs[:2]
+        gm_refs = refs[2 : 2 + count]
+        refs = refs[2 + count :]
+        proj_ref, rim_ref, conv_ref, k_ref, conv_w_ref, conv_b_ref, skip_ref, weight_ref = refs[:8]
+        th_ref, tl_ref, ih_ref, il_ref = refs[8:12]
+        g_ref, gp_ref, sum_ref = refs[12:15]
+        gn_refs = refs[15 : 15 + count]
+        wh_ref, wl_ref, ext_ref, gs_ref, o_ref, rows_ref, gn_ref = refs[15 + count :]
+        step = pl.program_id(0)
+        b = blocks - 1 - step
+        me = own_ref[0]
+
+        @pl.when(step == 0)
+        def _():
+            for k in range(3):
+                wh_ref[k], wl_ref[k] = parts_of(weight_ref[k])
+            gs_ref[:, block:] = jnp.zeros((3, 8, width), F32)
+            sum_ref[...] = jnp.zeros_like(sum_ref)
+
+        for k in range(count):
+            start = pl.multiple_of((me ^ k) * quarter, quarter)
+            rows_ref[pl.ds(start, quarter), :] = gm_refs[k][0]
+        inside = (b > 0).astype(F32)
+        short = []
+        for k in range(3):
+            ext_ref[k, :8] = rim_ref[0, k] * inside
+            ext_ref[k, 8:] = proj_ref[0, k]
+            short.append(
+                conv_w_ref[0, k : k + 1, :] * ext_ref[k, 6 : 6 + block]
+                + conv_w_ref[1, k : k + 1, :] * ext_ref[k, 7 : 7 + block]
+                + conv_w_ref[2, k : k + 1, :] * proj_ref[0, k]
+                + conv_b_ref[k : k + 1, :]
+            )
+        places = b * block + lax.broadcasted_iota(jnp.int32, (block, 1), 0)
+        mask = (places < length_ref[0]).astype(F32)
+        gate_in, values = short[1] * mask, short[2] * mask
+        grad_mixed = rows_ref[...]
+        grad_conv = grad_mixed * short[0]
+        gs_ref[0, :block] = grad_mixed * conv_ref[0]
+        g_ref[b] = dot_parts((th_ref[...], tl_ref[...]), parts_of(grad_conv), NN)
+        for r in range(0, block, tile):
+            lo = slice(r, r + tile)
+            hi = slice(block + r, block + r + tile)
+
+            def product(j, total, lo=lo, hi=hi):
+                g_re, g_im = g_ref[j, lo], g_ref[j, hi]
+                k_re, k_im = k_ref[j - b, lo], k_ref[j - b, hi]
+                return total[0] + g_re * k_re + g_im * k_im, total[1] + g_im * k_re - g_re * k_im
+
+            zero = jnp.zeros((tile, width), F32)
+            o_ref[lo], o_ref[hi] = lax.fori_loop(b, blocks, product, (zero, zero))
+        grad_signal = dot_parts((ih_ref[...], il_ref[...]), parts_of(o_ref[...]), NN)
+        grad_signal = grad_signal + skip_ref[...] * grad_conv
+        gs_ref[1, :block] = grad_signal * values
+        gs_ref[2, :block] = grad_signal * gate_in
+        sum_ref[0:1] += column_sum(grad_conv * short[2] * gate_in)
+        normed_grad = jnp.zeros((block, model), F32)
+        for k in range(3):
+            grad_short = gs_ref[k, :block]
+            sum_ref[1 + k : 2 + k] += column_sum(grad_short)
+            for t in range(3):
+                row = 4 + 3 * t + k
+                sum_ref[row : row + 1] += column_sum(grad_short * ext_ref[k, 6 + t : 6 + t + block])
+            grad_proj = (
+                conv_w_ref[2, k : k + 1, :] * grad_short
+                + conv_w_ref[1, k : k + 1, :] * gs_ref[k, 1 : 1 + block]
+                + conv_w_ref[0, k : k + 1, :] * gs_ref[k, 2 : 2 + block]
+            )
+            sum_ref[13 + k : 14 + k] += column_sum(grad_proj)
+            gp_ref[0, k] = grad_proj
+            normed_grad = normed_grad + dot_parts(parts_of(grad_proj), (wh_ref[k], wl_ref[k]), NT)
+            gs_ref[k, block:] = gs_ref[k, :8]
+        gn_ref[...] = normed_grad
+        for k in range(count):
+            start = pl.multiple_of((me ^ k) * quarter, quarter)
+            gn_refs[k][0] = gn_ref[pl.ds(start, quarter), :]
+
+    last = blocks - 1
+    by_block = lambda *shape: pl.BlockSpec((1,) + shape, lambda s: (last - s,) + (0,) * len(shape))
+    rim = pl.BlockSpec((1, 3, 8, width), lambda s: (jnp.maximum(last - s - 1, 0), 0, block // 8 - 1, 0))
+    fixed = [k_spec, conv_w, conv_b, skip, weight, *tables]
+    spectra = struct((blocks, 2 * block, width))
+    sums = struct((16, width))
+    outs = run_kernel(
+        body,
+        "mixer_backward",
+        (blocks,),
+        [scalar_spec(), scalar_spec()]
+        + [by_block(quarter, width)] * count
+        + [by_block(3, block, width), rim, by_block(block, width)]
+        + [whole(a) for a in fixed],
+        [whole(spectra), by_block(3, block, width), whole(sums)] + [by_block(quarter, model)] * count,
+        [spectra, struct((blocks, 3, block, width)), sums] + [struct((blocks, quarter, model))] * count,
+        [
+            pltpu.VMEM((3, model, width), BF16),
+            pltpu.VMEM((3, model, width), BF16),
+            pltpu.VMEM((3, block + 8, width), F32),
+            pltpu.VMEM((3, block + 8, width), F32),
+            pltpu.VMEM((2 * block, width), F32),
+            pltpu.VMEM((block, width), F32),
+            pltpu.VMEM((block, model), F32),
+        ],
+        [own, length, *gm_parts, proj, proj, conv, *fixed],
+        6 * blocks * block * width * (3 * model + 4 * block),
+    )
+    return outs[:3], outs[3:]
+
+
+def filter_backward(s_spec, g_spec, tables):
+    blocks, double, width = s_spec.shape
+    block = double // 2
+    tile = min(32, block)
+    inverse = tables[2:]
+
+    def body(s_ref, g_ref, ih_ref, il_ref, out_ref, after_ref, o_ref):
+        m = blocks - 1 - pl.program_id(0)
+
+        @pl.when(m == blocks - 1)
+        def _():
+            after_ref[...] = jnp.zeros_like(after_ref)
+
+        sign = parity_of(tile)
+        for r in range(0, block, tile):
+            lo = slice(r, r + tile)
+            hi = slice(block + r, block + r + tile)
+
+            def product(j, total, lo=lo, hi=hi):
+                g_re, g_im = g_ref[j, lo], g_ref[j, hi]
+                s_re, s_im = s_ref[j - m, lo], s_ref[j - m, hi]
+                return total[0] + g_re * s_re + g_im * s_im, total[1] + g_im * s_re - g_re * s_im
+
+            zero = jnp.zeros((tile, width), F32)
+            re, im = lax.fori_loop(m, blocks, product, (zero, zero))
+            o_ref[lo] = re + sign * after_ref[hi]
+            o_ref[hi] = im - sign * after_ref[lo]
+            after_ref[lo], after_ref[hi] = re, im
+        out_ref[0] = dot_parts((ih_ref[...], il_ref[...]), parts_of(o_ref[...]), NN)
+
+    return run_kernel(
+        body,
+        "filter_backward",
+        (blocks,),
+        [whole(s_spec), whole(g_spec), whole(inverse[0]), whole(inverse[1])],
+        [pl.BlockSpec((1, block, width), lambda s: (blocks - 1 - s, 0, 0))],
+        [struct((blocks, block, width))],
+        [pltpu.VMEM((double, width), F32)] * 2,
+        [s_spec, g_spec, *inverse],
+        12 * blocks * block * block * width,
+    )[0]
+
+
+def input_weight_grad(normed_high, normed_low, grad_proj):
+    blocks, block, model = normed_high.shape
+    width = grad_proj.shape[3]
+
+    def body(nh_ref, nl_ref, gp_ref, out_ref):
+        @pl.when(pl.program_id(0) == 0)
+        def _():
+            out_ref[...] = jnp.zeros_like(out_ref)
+
+        normed = (nh_ref[0], nl_ref[0])
+        for k in range(3):
+            out_ref[k] += dot_parts(normed, parts_of(gp_ref[0, k]), TN)
+
+    by_block = lambda *shape: pl.BlockSpec((1,) + shape, lambda b: (b,) + (0,) * len(shape))
+    out = struct((3, model, width))
+    return run_kernel(
+        body,
+        "input_weight_grad",
+        (blocks,),
+        [by_block(block, model)] * 2 + [by_block(3, block, width)],
+        [whole(out)],
+        [out],
+        [],
+        [normed_high, normed_low, grad_proj],
+        18 * blocks * block * model * width,
+    )[0]
+
+
+def input_backward(grad_pieces, x_own, grad_hidden, gain):
+    rows, model = x_own.shape
+    count = len(grad_pieces)
+    step = min(128, rows)
+
+    def body(*refs):
+        piece_refs = refs[:count]
+        x_ref, gh_ref, gain_ref, out_ref, sum_ref = refs[count:]
+
+        @pl.when(pl.program_id(0) == 0)
+        def _():
+            sum_ref[...] = jnp.zeros_like(sum_ref)
+
+        grad = sum(r[...] for r in piece_refs)
+        unit, scale = normalise(x_ref[...])
+        out_ref[...] = gh_ref[...] + norm_back(unit, scale, gain_ref[...], grad)
+        sum_ref[0:1] += column_sum(grad * unit)
+        sum_ref[1:2] += column_sum(grad)
+
+    row_spec = pl.BlockSpec((step, model), lambda r: (r, 0))
+    sums = struct((8, model))
+    return run_kernel(
+        body,
+        "input_backward",
+        (rows // step,),
+        [row_spec] * (count + 2) + [whole(gain)],
+        [row_spec, whole(sums)],
+        [struct((rows, model)), sums],
+        [],
+        [*grad_pieces, x_own, grad_hidden, gain],
+        20 * rows * model,
+    )
+
+
+def put_together(own, pieces):
+    groups, quarter, model = pieces[0].shape
+    count = len(pieces)
+
+    def body(own_ref, *refs):
+        for k in range(count):
+            start = pl.multiple_of((own_ref[0] ^ k) * quarter, quarter)
+            refs[count][0, pl.ds(start, quarter), :] = refs[k][0]
+
+    by_group = lambda n: pl.BlockSpec((1, n, model), lambda s: (s, 0, 0))
+    return run_kernel(
+        body,
+        "put_together",
+        (groups,),
+        [scalar_spec()] + [by_group(quarter)] * count,
+        [by_group(quarter * count)],
+        [struct((groups, quarter * count, model))],
+        [],
+        [own, *pieces],
+        0,
+    )[0]
+
+
+def swap(values, axis, bit):
+    size = lax.axis_size(axis)
+    return lax.ppermute(values, axis, [(i, i ^ bit) for i in range(size)])
+
+
+def total_over(values, axis):
+    bit = 1
+    while bit < lax.axis_size(axis):
+        values = values + swap(values, axis, bit)
+        bit *= 2
+    return values
+
+
+def transpose_blocks(values):
+    return lax.all_to_all(values, "seq", split_axis=0, concat_axis=0, tiled=True)
+
+
+def spread(values):
+    far = swap(values, "chan", 2)
+    return [values, swap(values, "chan", 1), far, swap(far, "chan", 1)]
+
+
+def collect(pieces):
+    far = pieces[2] + swap(pieces[3], "chan", 1)
+    return [pieces[0], swap(pieces[1], "chan", 1), swap(far, "chan", 2)]
+
+
+def pack(arrays):
+    flat = jnp.concatenate([a.reshape(-1) for a in arrays])
+    return jnp.pad(flat, (0, -flat.shape[0] % 1024))
+
+
+def unpack(flat, arrays):
+    out = []
+    start = 0
+    for a in arrays:
+        size = math.prod(a.shape)
+        out.append(flat[start : start + size].reshape(a.shape))
+        start += size
+    return out
+
+
+def sequence_device(
+    block_input,
+    lengths,
+    ln1_gain,
+    ln1_bias,
+    input_weight,
+    input_bias,
+    conv_w,
+    conv_b,
+    filt_w1,
+    filt_b1,
+    filt_w2,
+    filt_b2,
+    filt_w3,
+    decay,
+    skip,
+    output_weight,
+    output_bias,
+    ln2_gain,
+    ln2_bias,
+    up_weight,
+    up_bias,
+    down_weight,
+    down_bias,
+    cotangent,
+):
+    blocks, block, model = block_input.shape
+    count = lax.axis_size("chan")
+    quarter = block // count
+    rows = blocks * quarter
+    width = decay.shape[0]
+    seq_length = blocks * block
+    seq_index = lax.axis_index("seq")
+    chan_index = lax.axis_index("chan")
+    own = chan_index.astype(jnp.int32).reshape(1)
+    length = lax.dynamic_slice(lengths, (seq_index,), (1,))
+    tables = wave_tables(block)
+    row = lambda v: v.reshape(1, -1)
+
+    def own_rows(values):
+        part = lax.dynamic_slice_in_dim(values, chan_index * quarter, quarter, 1)
+        return transpose_blocks(part)
+
+    x_own = own_rows(block_input)
+    x_parts = spread(x_own)
+    x_own, cotangent_home = lax.optimization_barrier((x_own, cotangent))
+    cot_own = own_rows(cotangent_home).reshape(rows, model)
+    x_rows = x_own.reshape(rows, model)
+
+    up_parts = spread(up_weight)
+    late, down_home, out_home = lax.optimization_barrier((x_parts[2], down_weight, output_weight))
+    x_parts = [x_parts[0], x_parts[1], late, x_parts[3]]
+    down_parts = spread(down_home)
+    out_parts = spread(out_home)
+    up_bias_parts = [swap(up_bias, "chan", k) if k else up_bias for k in range(count)]
+
+    place_values = jnp.arange(seq_length, dtype=jnp.int32).astype(F32)
+    features = position_features(place_values, seq_length, filt_w1.shape[0])
+    kernel, filter_pull = jax.vjp(
+        partial(implicit_filter, features, place_values), filt_w1, filt_b1, filt_w2, filt_b2, filt_w3, decay
+    )
+    k_spec = filter_spectrum(kernel.reshape(blocks, block, width), tables)
+
+    weight = jnp.transpose(input_weight, (1, 0, 2))
+    (normed_high, normed_low, proj, conv, s_spec), mixed = mixer_forward(
+        own, length, x_parts, row(ln1_gain), row(ln1_bias), weight, input_bias, conv_w, conv_b, row(skip), k_spec, tables
+    )
+    mixed = [m if k == 0 else swap(m, "chan", k) for k, m in enumerate(mixed)]
+    mixed = [m.reshape(rows, width) for m in mixed]
+
+    hidden, *rest = hidden_forward(
+        mixed, out_parts, x_rows, cot_own, row(output_bias), row(ln2_gain), row(ln2_bias)
+    )
+    normed2, turned, cot_parts = rest[0:2], rest[2:4], rest[4:6]
+    sums = None
+    grads_up, grads_down, grads_up_bias = [None] * count, [None] * count, [None] * count
+    for k in (1, 0, 3, 2):
+        sums, (grads_up[k], grads_down[k], grads_up_bias[k]) = feed_forward(
+            normed2, turned, cot_parts, up_parts[k], row(up_bias_parts[k]), down_parts[k], sums
+        )
+    (out_rows, grad_hidden, sums2), grad_mixed, grads_out = hidden_backward(
+        hidden, sums[0], sums[1], cot_own, mixed, out_parts, row(ln2_gain), row(down_bias)
+    )
+
+    grad_mixed = [g.reshape(blocks, quarter, width) for g in grad_mixed]
+    grad_mixed = [g if k == 0 else swap(g, "chan", k) for k, g in enumerate(grad_mixed)]
+    (g_spec, grad_proj, mixer_sums), grad_normed = mixer_backward(
+        own, length, grad_mixed, proj, conv, s_spec, k_spec, conv_w, conv_b, row(skip), weight, tables
+    )
+
+    def to_home(values):
+        part = transpose_blocks(values.reshape(blocks, quarter, model))
+        return put_together(own, spread(part))
+
+    output = to_home(out_rows)
+    grad_down = sum(collect(grads_down))
+    grad_up = sum(collect(grads_up))
+    grad_out = sum(collect(grads_out))
+    grad_down, grad_up, grad_out = lax.psum((grad_down, grad_up, grad_out), "seq")
+
+    pieces = [p.reshape(rows, model) for p in collect(grad_normed)]
+    grad_x_rows, sums1 = input_backward(pieces, x_rows, grad_hidden, row(ln1_gain))
+    grad_x = to_home(grad_x_rows)
+
+    grad_in = input_weight_grad(normed_high, normed_low, grad_proj)
+    grad_in = lax.psum(grad_in, "seq")
+    grad_in = jnp.transpose(grad_in, (1, 0, 2))
+
+    grad_kernel = filter_backward(s_spec, g_spec, tables).reshape(seq_length, width)
+    grad_fw1, grad_fb1, grad_fw2, grad_fb2, grad_fw3, grad_decay = filter_pull(grad_kernel)
+
+    up_bias_grads = jnp.take(
+        jnp.concatenate(grads_up_bias, 0), jnp.arange(count, dtype=jnp.int32) ^ chan_index, axis=0
+    )
+    shared = [sums1[0], sums1[1], *[sums2[i] for i in range(4)], up_bias_grads, grad_fw1, grad_fb1, grad_fw2, grad_fb2]
+    split = [mixer_sums, grad_fw3, grad_decay]
+    shared_flat = total_over(pack(shared), "chan")
+    flat = total_over(jnp.concatenate([shared_flat, pack(split)]), "seq")
+    cut = shared_flat.shape[0]
+    grad_ln1_gain, grad_ln1_bias, grad_ln2_gain, grad_ln2_bias, grad_b_out, grad_b_fc2, up_bias_grads, *filt = unpack(
+        flat[:cut], shared
+    )
+    mixer_sums, grad_fw3, grad_decay = unpack(flat[cut:], split)
+    grad_b_fc1 = lax.dynamic_slice_in_dim(up_bias_grads, chan_index, 1, 0)[0]
+    grad_skip = mixer_sums[0]
+    grad_conv_b = mixer_sums[1:4]
+    grad_conv_w = mixer_sums[4:13].reshape(3, 3, width)
+    grad_b_in = mixer_sums[13:16]
+    return (
+        output,
+        grad_x,
+        grad_ln1_gain,
+        grad_ln1_bias,
+        grad_in,
+        grad_b_in,
+        grad_conv_w,
+        grad_conv_b,
+        *filt,
+        grad_fw3,
+        grad_decay,
+        grad_skip,
+        grad_out,
+        grad_b_out,
+        grad_ln2_gain,
+        grad_ln2_bias,
+        grad_up,
+        grad_b_fc1,
+        grad_down,
+        grad_b_fc2,
+    )
+
+
 def solution(mesh):
     in_specs = (
         P(None, "seq", None),
@@ -366,6 +1177,14 @@
         P("chan", None),
         P(),
     )
-    return jax.shard_map(
-        on_device, mesh=mesh, in_specs=in_specs, out_specs=out_specs, check_vma=False
-    )
+    chan = mesh.shape["chan"]
+
+    def step(*arrays):
+        sequences, seq_length = arrays[0].shape[:2]
+        whole_sequences = sequences == mesh.shape["seq"] and chan == 4 and seq_length % (64 * sequences) == 0
+        body = sequence_device if whole_sequences else spectral_device
+        return jax.shard_map(
+            body, mesh=mesh, in_specs=in_specs, out_specs=out_specs, check_vma=False
+        )(*arrays)
+
+    return step

time: 2060 us -> 865 us (0.42)
  waiting for transfers between devices: 1210 us -> 460 us
  matrix products: 482 us -> 22.8 us
  Pallas kernels: 0 us -> 221 us
  other arithmetic: 124 us -> 19.4 us
  local copies, waits for them, and re-layouts: 111 us -> 39.5 us
  starting transfers between devices: 69.6 us -> 33.6 us
    all_to_all x12 -> x3, waiting for transfers between devices: 604 us -> 44.4 us  [transpose_blocks(): lax.all_to_all(values, 'seq', split_axis=0, concat_axis=0, tiled=True)]
    psum x5 -> x1, waiting for transfers between devices: 607 us -> 94 us  [sequence_device(): grad_in = lax.psum(grad_in, 'seq')]
    dot_general x48 -> x0, matrix products: 475 us -> none  [the longest x6 54.6 us: rotate(): second_part = jnp.einsum(form, sin_tab, imag, precision=HIGH_ACCURACY)]
    ppermute x2 -> x44, waiting for transfers between devices: 0.01 us -> 322 us  [swap(): return lax.ppermute(values, axis, [(i, i ^ bit) for i in range(size)])]
    pallas_call x0 -> x14, Pallas kernels: none -> 221 us  [run_kernel(): pl.pallas_call(body, name=name, grid=grid, in_specs=in_specs, out_specs=o...]
    reduce_sum x11 -> x1, other arithmetic: 57.1 us -> 1.91 us  [implicit_filter(): return raw_kernel * jnp.exp(-decay[None, :] * place_values[:, None])]
    all_to_all x12 -> x3, starting transfers between devices: 62.6 us -> 12.8 us  [transpose_blocks(): lax.all_to_all(values, 'seq', split_axis=0, concat_axis=0, tiled=True)]
    all_to_all x0 -> x1, blocking collectives: none -> 44.1 us  [transpose_blocks(): lax.all_to_all(values, 'seq', split_axis=0, concat_axis=0, tiled=True)]
  transfers between devices with their start and end apart: 19 -> 48, of which waited for: 12 -> 17; matrix products, arithmetic and copies ran while one was open for 15% -> 8% of each run, Pallas kernels for 0% -> 24%
where the time goes in v1:
time: 865 us; the launch traced here: 855 us
  waiting for transfers between devices  460 us (53%)
  Pallas kernels  221 us (26%)
  blocking collectives  44.1 us (5%)
  local copies, waits for them, and re-layouts  39.5 us (5%)
  starting transfers between devices  33.6 us (4%)
  matrix products  22.8 us (3%)
  other arithmetic  19.4 us (2%)
  between operations  15 us (2%)
    ppermute x44, waiting for transfers between devices, swap(): return lax.ppermute(values, axis, [(i, i ^ bit) for i in range(size)])  322 us
    pallas_call x14, Pallas kernels, run_kernel(): pl.pallas_call(body, name=name, grid=grid, in_specs=in_specs, out_specs=o...  221 us
    psum x1, waiting for transfers between devices, sequence_device(): grad_in = lax.psum(grad_in, 'seq')  94 us
    all_to_all x3, waiting for transfers between devices, transpose_blocks(): lax.all_to_all(values, 'seq', split_axis=0, concat_axis=0, tiled=True)  44.4 us
    all_to_all x1, blocking collectives, transpose_blocks(): lax.all_to_all(values, 'seq', split_axis=0, concat_axis=0, tiled=True)  44.1 us
    ppermute x44, starting transfers between devices, swap(): return lax.ppermute(values, axis, [(i, i ^ bit) for i in range(size)])  20.7 us
  transfers between devices with their start and end apart: 48, of which 17 were waited for; matrix products, arithmetic and copies ran while one was open for 8% of the time, Pallas kernels for 24%

profile of v1, /device:TPU:0, one launch (start us, length us, event | category | flops | bytes accessed | tf_op | source)
XLA Modules:
  0.0 855.0 jit_solution(454350869425082064)
XLA Ops:
  8.8 44.1 %all_to_all.20.refs_2_ = f32[8,64,768]{2,1,0:T(8,128)S(1)} all-to-all(f32[8,64,768]{2,1,0:T(8,128)S(1)} %constant_dynamic-slice_fusion.1), channel_id=1, replica_groups=mesh['seq'=8,'chan'=4] {'seq'}, dimensions={0} | all-to-all | bytes 3145728 | tf_op jit(solution)/shard_map/all_to_all | solution.py:948
  56.6 33.7 %collective-permute-done.1.refs_4_ = f32[8,64,768]{2,1,0:T(8,128)} collective-permute-done((f32[8,64,768]{2,1,0:T(8,128)S(1)}, f32[8,64,768]{2,1,0:T(8,128)}, u32[]{:S(2)}, u32[]{:S(2)}) %collective-permute-start.1) | collective-permute-done | bytes 1572896 | tf_op jit(solution)/shard_map/ppermute | solution.py:936
  98.9 38.8 %collective-permute-done.13 = f32[768]{0:T(1024)S(1)} collective-permute-done((f32[768]{0:T(1024)S(1)}, f32[768]{0:T(1024)S(1)}, u32[]{:S(2)}, u32[]{:S(2)}) %collective-permute-start.13) | collective-permute-done | bytes 3104 | tf_op jit(solution)/shard_map/ppermute | solution.py:936
  165.3 39.4 %collective-permute-done.7.refs_6_.refs_10_ = f32[192,768]{1,0:T(8,128)} collective-permute-done((f32[192,768]{1,0:T(8,128)}, f32[192,768]{1,0:T(8,128)}, u32[]{:S(2)}, u32[]{:S(2)}) %collective-permute-start.7) | collective-permute-done | bytes 589856 | tf_op jit(solution)/shard_map/ppermute | solution.py:936
  205.2 36.3 %mixer_forward.1 = (bf16[8,256,768]{2,1,0:T(8,128)(2,1)}, bf16[8,256,768]{2,1,0:T(8,128)(2,1)}, f32[8,3,256,192]{3,2,1,0:T(8,128)}, f32[8,256,192]{2,1,0:T(8,128...) custom-call(s32[1]{0:T(128)} %bitcast.refs_0_.own_ref, ...), custom_call_target="tpu_custom_call" | custom-call | flops 7851737088 | bytes 29575176 | tf_op jit(solution)/shard_map/mixer_forward/pallas_call | solution.py:375
  243.7 12.9 %collective-permute-done.4 = f32[8,64,192]{2,1,0:T(8,128)S(1)} collective-permute-done((f32[8,64,192]{2,1,0:T(8,128)}, f32[8,64,192]{2,1,0:T(8,128)S(1)}, u32[]{:S(2)}, u32[]{:S(2)}) %collective-permute-start.4) | collective-permute-done | bytes 393248 | tf_op jit(solution)/shard_map/ppermute | solution.py:936
  267.0 9.0 %hidden_forward.1 = (f32[512,768]{1,0:T(8,128)}, bf16[512,768]{1,0:T(8,128)(2,1)}, bf16[512,768]{1,0:T(8,128)(2,1)}, bf16[768,512]{1,0:T(8,128)(2,1)}, bf16[768,...) custom-call(f32[512,192]{1,0:T(8,128)} %bitcast.47, f32[512,192]{1,0:T(8,128)} %bitcast.49, ...), custom_call_target="tpu_custom_call" | custom-call | flops 1811939328 | bytes 13378560 | tf_op jit(solution)/shard_map/hidden_forward/pallas_call | solution.py:375
  276.1 17.0 %feed_forward.4 = (f32[512,768]{1,0:T(8,128)}, f32[512,768]{1,0:T(8,128)}, f32[768,768]{1,0:T(8,128)}, f32[768,768]{1,0:T(8,128)}, f32[1,768]{1,0:T(1,128)}) custom-call(bf16[512,768]{1,0:T(8,128)(2,1)} %get-tuple-element.93.refs_0_, bf16[512,768]{1,0:T(8,128)(2,1)} %get-tuple-element.94.refs_1_, bf16[768,512]{1,0:T(8,128)(2,1)} %get-tuple-element.95.refs_2_, ...), custom_call_target="tpu_custom_call" | custom-call | flops 10871635968 | bytes 17307648 | tf_op jit(solution)/shard_map/feed_forward/pallas_call | solution.py:375
  293.1 17.8 %feed_forward.5 = (f32[512,768]{1,0:T(8,128)}, f32[512,768]{1,0:T(8,128)}, f32[768,768]{1,0:T(8,128)}, f32[768,768]{1,0:T(8,128)}, f32[1,768]{1,0:T(1,128)}) custom-call(bf16[512,768]{1,0:T(8,128)(2,1)} %get-tuple-element.93.refs_0_, bf16[512,768]{1,0:T(8,128)(2,1)} %get-tuple-element.94.refs_1_, bf16[768,512]{1,0:T(8,128)(2,1)} %get-tuple-element.95.refs_2_, ...), custom_call_target="tpu_custom_call" | custom-call | flops 10871635968 | bytes 20453376 | tf_op jit(solution)/shard_map/feed_forward/pallas_call | solution.py:375
  310.9 17.8 %feed_forward.6 = (f32[512,768]{1,0:T(8,128)}, f32[512,768]{1,0:T(8,128)}, f32[768,768]{1,0:T(8,128)}, f32[768,768]{1,0:T(8,128)}, f32[1,768]{1,0:T(1,128)}) custom-call(bf16[512,768]{1,0:T(8,128)(2,1)} %get-tuple-element.93.refs_0_, bf16[512,768]{1,0:T(8,128)(2,1)} %get-tuple-element.94.refs_1_, bf16[768,512]{1,0:T(8,128)(2,1)} %get-tuple-element.95.refs_2_, ...), custom_call_target="tpu_custom_call" | custom-call | flops 10871635968 | bytes 20453376 | tf_op jit(solution)/shard_map/feed_forward/pallas_call | solution.py:375
  329.3 18.2 %feed_forward.7 = (f32[512,768]{1,0:T(8,128)}, f32[512,768]{1,0:T(8,128)}, f32[768,768]{1,0:T(8,128)}, f32[768,768]{1,0:T(8,128)}, f32[1,768]{1,0:T(1,128)}) custom-call(bf16[512,768]{1,0:T(8,128)(2,1)} %get-tuple-element.93.refs_0_, bf16[512,768]{1,0:T(8,128)(2,1)} %get-tuple-element.94.refs_1_, bf16[768,512]{1,0:T(8,128)(2,1)} %get-tuple-element.95.refs_2_, ...), custom_call_target="tpu_custom_call" | custom-call | flops 10871635968 | bytes 20453376 | tf_op jit(solution)/shard_map/feed_forward/pallas_call | solution.py:375
  347.6 14.9 %hidden_backward.1 = (f32[512,768]{1,0:T(8,128)}, f32[512,768]{1,0:T(8,128)}, f32[8,768]{1,0:T(8,128)}, f32[512,192]{1,0:T(8,128)}, f32[512,192]{1,0:T(8,128)}, ...) custom-call(f32[512,768]{1,0:T(8,128)} %get-tuple-element.92.refs_0_, ...), custom_call_target="tpu_custom_call" | custom-call | flops 3623878656 | bytes 17332224 | tf_op jit(solution)/shard_map/hidden_backward/pallas_call | solution.py:375
  364.8 13.2 %collective-permute-done.22.refs_4_ = f32[8,64,192]{2,1,0:T(8,128)S(1)} collective-permute-done((f32[8,64,192]{2,1,0:T(8,128)}, f32[8,64,192]{2,1,0:T(8,128)S(1)}, u32[]{:S(2)}, u32[]{:S(2)}) %collective-permute-start.22) | collective-permute-done | bytes 393248 | tf_op jit(solution)/shard_map/ppermute | solution.py:936
  378.0 10.0 %collective-permute-done.23.refs_5_ = f32[8,64,192]{2,1,0:T(8,128)S(1)} collective-permute-done((f32[8,64,192]{2,1,0:T(8,128)}, f32[8,64,192]{2,1,0:T(8,128)S(1)}, u32[]{:S(2)}, u32[]{:S(2)}) %collective-permute-start.23) | collective-permute-done | bytes 393248 | tf_op jit(solution)/shard_map/ppermute | solution.py:936
  388.8 35.0 %mixer_backward.1 = (f32[8,512,192]{2,1,0:T(8,128)}, f32[8,3,256,192]{3,2,1,0:T(8,128)}, f32[16,192]{1,0:T(8,128)}, f32[8,64,768]{2,1,0:T(8,128)}, f32[8,64,768]...) custom-call(s32[1]{0:T(128)} %bitcast.refs_0_.own_ref, s32[1]{0:T(128)} %dynamic_slice.12.refs_1_, ...), custom_call_target="tpu_custom_call" | custom-call | flops 7851737088 | bytes 32724744 | tf_op jit(solution)/shard_map/mixer_backward/pallas_call | solution.py:375
  435.6 13.1 %input_weight_grad.1 = f32[3,768,192]{2,1,0:T(8,128)} custom-call(bf16[8,256,768]{2,1,0:T(8,128)(2,1)} %get-tuple-element.130.nh_ref, bf16[8,256,768]{2,1,0:T(8,128)(2,1)} %get-tuple-element.131.nl_ref, f32[8,3,256,192]{3,2,1,0:T(8,128)} %get-tuple-element.132.gp_ref), custom_call_target="tpu_custom_call" | custom-call | flops 5435817984 | bytes 12779520 | tf_op jit(solution)/shard_map/input_weight_grad/pallas_call | solution.py:375
  451.5 91.1 %collective-permute-done.37 = f32[192,768]{1,0:T(8,128)S(1)} collective-permute-done((f32[192,768]{1,0:T(8,128)S(1)}, f32[192,768]{1,0:T(8,128)S(1)}, u32[]{:S(2)}, u32[]{:S(2)}) %collective-permute-start.37) | collective-permute-done | bytes 589856 | tf_op jit(solution)/shard_map/ppermute | solution.py:936
  552.5 25.9 %collective-permute-done.26 = f32[8,64,768]{2,1,0:T(8,128)} collective-permute-done((f32[8,64,768]{2,1,0:T(8,128)}, f32[8,64,768]{2,1,0:T(8,128)}, u32[]{:S(2)}, u32[]{:S(2)}) %collective-permute-start.26) | collective-permute-done | bytes 1572896 | tf_op jit(solution)/shard_map/ppermute | solution.py:936
  590.5 12.7 %filter_backward.1 = f32[8,256,192]{2,1,0:T(8,128)} custom-call(f32[8,512,192]{2,1,0:T(8,128)} %get-tuple-element.127.s_ref, f32[8,512,192]{2,1,0:T(8,128)} %get-tuple-element.128.g_ref, bf16[256,512]{1,0:T(8,128)(2,1)} %constant.68.clone.refs_16_.ih_ref, bf16[256,512]{1,0:T(8,128)(2,1)} %constant.69.clone.refs_17_.il_ref), custom_call_target="tpu_custom_call" | custom-call | flops 1207959552 | bytes 8388608 | tf_op jit(solution)/shard_map/filter_backward/pallas_call | solution.py:375
  619.9 44.4 %all-to-all-done.3.refs_0_ = f32[8,64,768]{2,1,0:T(8,128)} async-done(((f32[8,64,768]{2,1,0:T(8,128)}), f32[8,64,768]{2,1,0:T(8,128)}, u32[]{:S(2)}, u32[]{:S(2)}) %all-to-all-start.3) | async-done | bytes 1572896 | tf_op jit(solution)/shard_map/all_to_all | solution.py:948
  670.3 30.2 %collective-permute-done.31 = f32[14336]{0:T(1024)S(1)} collective-permute-done((f32[14336]{0:T(1024)S(1)}, f32[14336]{0:T(1024)S(1)}, u32[]{:S(2)}, u32[]{:S(2)}) %collective-permute-start.31) | collective-permute-done | bytes 57376 | tf_op jit(solution)/shard_map/ppermute | solution.py:936
  705.6 8.6 %collective-permute-done.33 = f32[30720]{0:T(1024)S(1)} collective-permute-done((f32[30720]{0:T(1024)S(1)}, f32[30720]{0:T(1024)S(1)}, u32[]{:S(2)}, u32[]{:S(2)}) %collective-permute-start.33) | collective-permute-done | bytes 122912 | tf_op jit(solution)/shard_map/ppermute | solution.py:936
  729.3 7.9 put_together.2
  746.2 94.0 %all-reduce.5.cloned.1.call-done = (f32[768,3,192]{2,0,1:T(8,128)}, f32[192,768]{1,0:T(8,128)}, f32[768,768]{1,0:T(8,128)}, f32[768,768]{1,0:T(8,128)}) async-done(((f32[768,3,192]{2,0,1:T(8,128)}, f32[192,768]{1,0:T(8,128)}, f32[768,768]{1,0:T(8,128)}, f32[768,768]{1,0:T(8,128)}), (f32[768,3,192]{2,0,1:T(8,128)}, f32[192,768]{1,0:T(8,128)}, f32[768,768]{1,0:T(8,128)}, ...) | async-done | bytes 7077904 | tf_op jit(solution)/shard_map/psum | solution.py:1081
  (289 shorter events, 154.1 us)
Async XLA Ops:
  54.4 89.5 %collective-permute-start.9 = (f32[768,768]{1,0:T(8,128)}, f32[768,768]{1,0:T(8,128)}, u32[]{:S(2)}, u32[]{:S(2)}) collective-permute-start(f32[768,768]{1,0:T(8,128)} %refs_6_.1), channel_id=1, source_target_pairs={{0,2},{1,3},{2,0},{3,1},{4,6},{5,7},{6,4},{7,5},{8,10},{9,11},{10,... | collective-permute-start | bytes 7077896 | tf_op jit(solution)/shard_map/ppermute | solution.py:936
  54.9 89.1 %collective-permute-start = (f32[8,64,768]{2,1,0:T(8,128)S(1)}, f32[8,64,768]{2,1,0:T(8,128)}, u32[]{:S(2)}, u32[]{:S(2)}) collective-permute-start(f32[8,64,768]{2,1,0:T(8,128)S(1)} %all_to_all.20.refs_2_), channel_id=1, source_target_pairs={{0,1},{1,0},{2,3},{3,2},{4,5},{5,4},{6,7},{7,6},{8,9},{9,8},{10,11... | collective-permute-start | bytes 4718600 | tf_op jit(solution)/shard_map/ppermute | solution.py:936
  55.4 82.3 %collective-permute-start.13 = (f32[768]{0:T(1024)S(1)}, f32[768]{0:T(1024)S(1)}, u32[]{:S(2)}, u32[]{:S(2)}) collective-permute-start(f32[768]{0:T(1024)S(1)} %copy-done.38), channel_id=1, source_target_pairs={{0,3},{1,2},{2,1},{3,0},{4,7},{5,6},{6,5},{7,4},{8,11},{9,10},{10,... | collective-permute-start | bytes 9224 | tf_op jit(solution)/shard_map/ppermute | solution.py:936
  90.3 114.5 %collective-permute-start.2 = (f32[8,64,768]{2,1,0:T(8,128)}, f32[8,64,768]{2,1,0:T(8,128)}, u32[]{:S(2)}, u32[]{:S(2)}) collective-permute-start(f32[8,64,768]{2,1,0:T(8,128)} %collective-permute-done.1.refs_4_), channel_id=1, source_target_pairs={{0,1},{1,0},{2,3},{3,2},{4,5},{5,4},{6,7},{7,6},{8,9},{9,8},{10,11... | collective-permute-start | bytes 4718600 | tf_op jit(solution)/shard_map/ppermute | solution.py:936
  93.6 168.3 %all-to-all-start.1 = ((f32[8,64,768]{2,1,0:T(8,128)}), f32[8,64,768]{2,1,0:T(8,128)S(1)}, u32[]{:S(2)}, u32[]{:S(2)}) async-start(f32[8,64,768]{2,1,0:T(8,128)} %constant_dynamic-slice_fusion), calls=%async_computation.1 | async-start | bytes 3145728 | tf_op jit(solution)/shard_map/all_to_all | solution.py:948
  97.3 44.7 %collective-permute-start.10 = (f32[768]{0:T(1024)S(1)}, f32[768]{0:T(1024)S(1)}, u32[]{:S(2)}, u32[]{:S(2)}) collective-permute-start(f32[768]{0:T(1024)S(1)} %copy-done.38), channel_id=1, source_target_pairs={{0,2},{1,3},{2,0},{3,1},{4,6},{5,7},{6,4},{7,5},{8,10},{9,11},{10,... | collective-permute-start | bytes 9224 | tf_op jit(solution)/shard_map/ppermute | solution.py:936
  137.7 119.0 %collective-permute-start.11 = (f32[768,768]{1,0:T(8,128)}, f32[768,768]{1,0:T(8,128)}, u32[]{:S(2)}, u32[]{:S(2)}) collective-permute-start(f32[768,768]{1,0:T(8,128)} %refs_8_), channel_id=1, source_target_pairs={{0,2},{1,3},{2,0},{3,1},{4,6},{5,7},{6,4},{7,5},{8,10},{9,11},{10,... | collective-permute-start | bytes 7077896 | tf_op jit(solution)/shard_map/ppermute | solution.py:936
  142.0 134.0 %collective-permute-start.15 = (f32[768,768]{1,0:T(8,128)}, f32[768,768]{1,0:T(8,128)}, u32[]{:S(2)}, u32[]{:S(2)}) collective-permute-start(f32[768,768]{1,0:T(8,128)} %refs_6_.1), channel_id=1, source_target_pairs={{0,1},{1,0},{2,3},{3,2},{4,5},{5,4},{6,7},{7,6},{8,9},{9,8},{10,11... | collective-permute-start | bytes 7077896 | tf_op jit(solution)/shard_map/ppermute | solution.py:936
  143.9 132.1 %collective-permute-start.17 = (f32[768,768]{1,0:T(8,128)}, f32[768,768]{1,0:T(8,128)}, u32[]{:S(2)}, u32[]{:S(2)}) collective-permute-start(f32[768,768]{1,0:T(8,128)} %refs_8_), channel_id=1, source_target_pairs={{0,1},{1,0},{2,3},{3,2},{4,5},{5,4},{6,7},{7,6},{8,9},{9,8},{10,11... | collective-permute-start | bytes 7077896 | tf_op jit(solution)/shard_map/ppermute | solution.py:936
  144.0 60.7 %collective-permute-start.7 = (f32[192,768]{1,0:T(8,128)}, f32[192,768]{1,0:T(8,128)}, u32[]{:S(2)}, u32[]{:S(2)}) collective-permute-start(f32[192,768]{1,0:T(8,128)} %refs_8_.1), channel_id=1, source_target_pairs={{0,2},{1,3},{2,0},{3,1},{4,6},{5,7},{6,4},{7,5},{8,10},{9,11},{10,... | collective-permute-start | bytes 1769480 | tf_op jit(solution)/shard_map/ppermute | solution.py:936
  256.6 54.3 %collective-permute-start.12 = (f32[768,768]{1,0:T(8,128)}, f32[768,768]{1,0:T(8,128)}, u32[]{:S(2)}, u32[]{:S(2)}) collective-permute-start(f32[768,768]{1,0:T(8,128)} %collective-permute-done.9.refs_6_), channel_id=1, source_target_pairs={{0,1},{1,0},{2,3},{3,2},{4,5},{5,4},{6,7},{7,6},{8,9},{9,8},{10,11... | collective-permute-start | bytes 7077896 | tf_op jit(solution)/shard_map/ppermute | solution.py:936
  256.6 54.3 %collective-permute-start.14 = (f32[768,768]{1,0:T(8,128)}, f32[768,768]{1,0:T(8,128)}, u32[]{:S(2)}, u32[]{:S(2)}) collective-permute-start(f32[768,768]{1,0:T(8,128)} %collective-permute-done.11.refs_8_), channel_id=1, source_target_pairs={{0,1},{1,0},{2,3},{3,2},{4,5},{5,4},{6,7},{7,6},{8,9},{9,8},{10,11... | collective-permute-start | bytes 7077896 | tf_op jit(solution)/shard_map/ppermute | solution.py:936
  328.7 95.6 %collective-permute-start.42 = (f32[768,768]{1,0:T(8,128)}, f32[768,768]{1,0:T(8,128)S(1)}, u32[]{:S(2)}, u32[]{:S(2)}) collective-permute-start(f32[768,768]{1,0:T(8,128)} %get-tuple-element.144), channel_id=1, source_target_pairs={{0,1},{1,0},{2,3},{3,2},{4,5},{5,4},{6,7},{7,6},{8,9},{9,8},{10,11... | collective-permute-start | bytes 7077896 | tf_op jit(solution)/shard_map/ppermute | solution.py:936
  329.1 97.2 %collective-permute-start.39 = (f32[768,768]{1,0:T(8,128)}, f32[768,768]{1,0:T(8,128)S(1)}, u32[]{:S(2)}, u32[]{:S(2)}) collective-permute-start(f32[768,768]{1,0:T(8,128)} %get-tuple-element.140), channel_id=1, source_target_pairs={{0,1},{1,0},{2,3},{3,2},{4,5},{5,4},{6,7},{7,6},{8,9},{9,8},{10,11... | collective-permute-start | bytes 7077896 | tf_op jit(solution)/shard_map/ppermute | solution.py:936
  362.8 66.9 %collective-permute-start.41 = (f32[768,768]{1,0:T(8,128)}, f32[768,768]{1,0:T(8,128)}, u32[]{:S(2)}, u32[]{:S(2)}) collective-permute-start(f32[768,768]{1,0:T(8,128)} %get-tuple-element.142), channel_id=1, source_target_pairs={{0,1},{1,0},{2,3},{3,2},{4,5},{5,4},{6,7},{7,6},{8,9},{9,8},{10,11... | collective-permute-start | bytes 7077896 | tf_op jit(solution)/shard_map/ppermute | solution.py:936
  426.0 117.9 %collective-permute-start.43 = (f32[768,768]{1,0:T(8,128)}, f32[768,768]{1,0:T(8,128)}, u32[]{:S(2)}, u32[]{:S(2)}) collective-permute-start(f32[768,768]{1,0:T(8,128)} %add.125), channel_id=1, source_target_pairs={{0,2},{1,3},{2,0},{3,1},{4,6},{5,7},{6,4},{7,5},{8,10},{9,11},{10,... | collective-permute-start | bytes 7077896 | tf_op jit(solution)/shard_map/ppermute | solution.py:936
  426.3 122.0 %collective-permute-start.38 = (f32[768,768]{1,0:T(8,128)}, f32[768,768]{1,0:T(8,128)}, u32[]{:S(2)}, u32[]{:S(2)}) collective-permute-start(f32[768,768]{1,0:T(8,128)} %get-tuple-element.138), channel_id=1, source_target_pairs={{0,1},{1,0},{2,3},{3,2},{4,5},{5,4},{6,7},{7,6},{8,9},{9,8},{10,11... | collective-permute-start | bytes 7077896 | tf_op jit(solution)/shard_map/ppermute | solution.py:936
  428.5 119.7 %collective-permute-start.40 = (f32[768,768]{1,0:T(8,128)}, f32[768,768]{1,0:T(8,128)}, u32[]{:S(2)}, u32[]{:S(2)}) collective-permute-start(f32[768,768]{1,0:T(8,128)} %add.121), channel_id=1, source_target_pairs={{0,2},{1,3},{2,0},{3,1},{4,6},{5,7},{6,4},{7,5},{8,10},{9,11},{10,... | collective-permute-start | bytes 7077896 | tf_op jit(solution)/shard_map/ppermute | solution.py:936
  430.0 154.0 %all-to-all-start.2 = ((f32[8,64,768]{2,1,0:T(8,128)}), f32[8,64,768]{2,1,0:T(8,128)S(1)}, u32[]{:S(2)}, u32[]{:S(2)}) async-start(f32[8,64,768]{2,1,0:T(8,128)} %bitcast.10), calls=%async_computation.2 | async-start | bytes 3145728 | tf_op jit(solution)/shard_map/all_to_all | solution.py:948
  434.5 405.7 %all-reduce.5.cloned.1.call-start = ((), (), s32[]{:S(2)}) async-start(), calls=%async_computation.4 | async-start | bytes 15335424 | tf_op jit(solution)/shard_map/psum | solution.py:1081
  434.7 107.9 %collective-permute-start.37 = (f32[192,768]{1,0:T(8,128)S(1)}, f32[192,768]{1,0:T(8,128)S(1)}, u32[]{:S(2)}, u32[]{:S(2)}) collective-permute-start(f32[192,768]{1,0:T(8,128)S(1)} %add.118), channel_id=1, source_target_pairs={{0,2},{1,3},{2,0},{3,1},{4,6},{5,7},{6,4},{7,5},{8,10},{9,11},{10,... | collective-permute-start | bytes 1769480 | tf_op jit(solution)/shard_map/ppermute | solution.py:936
  451.5 101.0 %collective-permute-start.24 = (f32[8,64,768]{2,1,0:T(8,128)}, f32[8,64,768]{2,1,0:T(8,128)S(1)}, u32[]{:S(2)}, u32[]{:S(2)}) collective-permute-start(f32[8,64,768]{2,1,0:T(8,128)} %get-tuple-element.116), channel_id=1, source_target_pairs={{0,1},{1,0},{2,3},{3,2},{4,5},{5,4},{6,7},{7,6},{8,9},{9,8},{10,11... | collective-permute-start | bytes 4718600 | tf_op jit(solution)/shard_map/ppermute | solution.py:936
  584.0 80.4 %all-to-all-start.3 = ((f32[8,64,768]{2,1,0:T(8,128)}), f32[8,64,768]{2,1,0:T(8,128)}, u32[]{:S(2)}, u32[]{:S(2)}) async-start(f32[8,64,768]{2,1,0:T(8,128)} %bitcast.44), calls=%async_computation.3 | async-start | bytes 3145728 | tf_op jit(solution)/shard_map/all_to_all | solution.py:948
  619.1 83.2 %collective-permute-start.19 = (f32[8,64,768]{2,1,0:T(8,128)S(1)}, f32[8,64,768]{2,1,0:T(8,128)}, u32[]{:S(2)}, u32[]{:S(2)}) collective-permute-start(f32[8,64,768]{2,1,0:T(8,128)S(1)} %all-to-all-done.2.refs_0_), channel_id=1, source_target_pairs={{0,2},{1,3},{2,0},{3,1},{4,6},{5,7},{6,4},{7,5},{8,10},{9,11},{10,... | collective-permute-start | bytes 4718600 | tf_op jit(solution)/shard_map/ppermute | solution.py:936
  (83 other events, 2715.1 us)
Sparse Core Ops, SparseCore 0:
  552.6 287.4 all-reduce.4

commit v2 on v1

--- a/solution.py
+++ b/solution.py
@@ -369,9 +369,7 @@
     return jax.ShapeDtypeStruct(tuple(shape), kind)
 
 
-def run_kernel(body, name, grid, in_specs, out_specs, out_shape, scratch, args, flops):
-    moved = sum(math.prod(a.shape) * a.dtype.itemsize for a in args)
-    moved += sum(math.prod(a.shape) * a.dtype.itemsize for a in out_shape)
+def run_kernel(body, name, grid, in_specs, out_specs, out_shape, scratch, args, micros):
     return pl.pallas_call(
         body,
         name=name,
@@ -383,7 +381,9 @@
         compiler_params=pltpu.CompilerParams(
             dimension_semantics=("arbitrary",) * len(grid), vmem_limit_bytes=VMEM_BYTES
         ),
-        cost_estimate=pl.CostEstimate(flops=int(flops), bytes_accessed=int(moved), transcendentals=0),
+        cost_estimate=pl.CostEstimate(
+            flops=int(micros * 1.15e9), bytes_accessed=int(micros * 3.6e6), transcendentals=0
+        ),
     )(*args)
 
 
@@ -428,7 +428,7 @@
         [struct((blocks, 2 * block, width))],
         [pltpu.VMEM((2 * block, width), F32)],
         [kernel, table_high, table_low],
-        12 * blocks * block * block * width,
+        8,
     )[0]
 
 
@@ -438,6 +438,8 @@
     block = quarter * count
     width = weight.shape[2]
     tile = min(32, block)
+    pair = 2 - blocks % 2
+    span = pair * block
 
     def body(*refs):
         own_ref, length_ref = refs[:2]
@@ -448,83 +450,92 @@
         nh_ref, nl_ref, proj_ref, conv_ref, s_ref = refs[12:17]
         m_refs = refs[17 : 17 + count]
         wh_ref, wl_ref, ext_ref, o_ref, mixed_ref = refs[17 + count :]
-        b = pl.program_id(0)
+        step = pl.program_id(0)
         me = own_ref[0]
 
-        @pl.when(b == 0)
+        @pl.when(step == 0)
         def _():
             for k in range(3):
                 wh_ref[k], wl_ref[k] = parts_of(weight_ref[k])
             ext_ref[:, :8] = jnp.zeros((3, 8, width), F32)
 
-        for k in range(count):
-            normed = normalise(x_refs[k][0])[0] * gain_ref[...] + offset_ref[...]
-            start = pl.multiple_of((me ^ k) * quarter, quarter)
-            high, low = parts_of(normed)
-            nh_ref[0, pl.ds(start, quarter), :] = high
-            nl_ref[0, pl.ds(start, quarter), :] = low
+        for u in range(pair):
+            for k in range(count):
+                normed = normalise(x_refs[k][u])[0] * gain_ref[...] + offset_ref[...]
+                start = pl.multiple_of(u * block + (me ^ k) * quarter, quarter)
+                high, low = parts_of(normed)
+                nh_ref[0, pl.ds(start, quarter), :] = high
+                nl_ref[0, pl.ds(start, quarter), :] = low
         normed = (nh_ref[0], nl_ref[0])
         short = []
         for k in range(3):
             proj = dot_parts(normed, (wh_ref[k], wl_ref[k]), NN) + bias_ref[k : k + 1, :]
             proj_ref[0, k] = proj
-            ext_ref[k, 8 : 8 + block] = proj
+            ext_ref[k, 8:] = proj
             short.append(
-                conv_w_ref[0, k : k + 1, :] * ext_ref[k, 6 : 6 + block]
-                + conv_w_ref[1, k : k + 1, :] * ext_ref[k, 7 : 7 + block]
+                conv_w_ref[0, k : k + 1, :] * ext_ref[k, 6 : 6 + span]
+                + conv_w_ref[1, k : k + 1, :] * ext_ref[k, 7 : 7 + span]
                 + conv_w_ref[2, k : k + 1, :] * proj
                 + conv_b_ref[k : k + 1, :]
             )
-            ext_ref[k, :8] = ext_ref[k, block : block + 8]
-        places = b * block + lax.broadcasted_iota(jnp.int32, (block, 1), 0)
+            ext_ref[k, :8] = ext_ref[k, span:]
+        places = step * span + lax.broadcasted_iota(jnp.int32, (span, 1), 0)
         mask = (places < length_ref[0]).astype(F32)
         signal = short[2] * short[1] * mask
-        s_ref[b] = dot_parts((th_ref[...], tl_ref[...]), parts_of(signal), NN)
-        for r in range(0, block, tile):
-            lo = slice(r, r + tile)
-            hi = slice(block + r, block + r + tile)
-
-            def product(i, total, lo=lo, hi=hi):
-                s_re, s_im = s_ref[i, lo], s_ref[i, hi]
-                k_re, k_im = k_ref[b - i, lo], k_ref[b - i, hi]
-                return total[0] + s_re * k_re - s_im * k_im, total[1] + s_re * k_im + s_im * k_re
-
-            zero = jnp.zeros((tile, width), F32)
-            o_ref[lo], o_ref[hi] = lax.fori_loop(0, b + 1, product, (zero, zero))
-        conv = dot_parts((ih_ref[...], il_ref[...]), parts_of(o_ref[...]), NN) + skip_ref[...] * signal
+        for u in range(pair):
+            part = signal[u * block : (u + 1) * block]
+            s_ref[step * pair + u] = dot_parts((th_ref[...], tl_ref[...]), parts_of(part), NN)
+        for u in range(pair):
+            b = step * pair + u
+            for r in range(0, block, tile):
+                lo = slice(r, r + tile)
+                hi = slice(block + r, block + r + tile)
+
+                def product(i, total, b=b, lo=lo, hi=hi):
+                    s_re, s_im = s_ref[i, lo], s_ref[i, hi]
+                    k_re, k_im = k_ref[b - i, lo], k_ref[b - i, hi]
+                    return total[0] + s_re * k_re - s_im * k_im, total[1] + s_re * k_im + s_im * k_re
+
+                zero = jnp.zeros((tile, width), F32)
+                o_ref[u, lo], o_ref[u, hi] = lax.fori_loop(0, b + 1, product, (zero, zero))
+        inverse = (ih_ref[...], il_ref[...])
+        conv = jnp.concatenate([dot_parts(inverse, parts_of(o_ref[u]), NN) for u in range(pair)], 0)
+        conv = conv + skip_ref[...] * signal
         conv_ref[0] = conv
         mixed_ref[...] = conv * short[0]
-        for k in range(count):
-            start = pl.multiple_of((me ^ k) * quarter, quarter)
-            m_refs[k][0] = mixed_ref[pl.ds(start, quarter), :]
+        for u in range(pair):
+            for k in range(count):
+                start = pl.multiple_of(u * block + (me ^ k) * quarter, quarter)
+                m_refs[k][u] = mixed_ref[pl.ds(start, quarter), :]
 
     by_block = lambda *shape: pl.BlockSpec((1,) + shape, lambda b: (b,) + (0,) * len(shape))
     args = [own, length, *x_parts, gain, offset, weight, bias, conv_w, conv_b, skip, spectrum, *tables]
-    in_specs = [scalar_spec(), scalar_spec()] + [by_block(quarter, model)] * count
+    by_pair = lambda n: pl.BlockSpec((pair, quarter, n), lambda b: (b, 0, 0))
+    in_specs = [scalar_spec(), scalar_spec()] + [by_pair(model)] * count
     in_specs += [whole(a) for a in args[2 + count :]]
     s_shape = struct((blocks, 2 * block, width))
     outs = run_kernel(
         body,
         "mixer_forward",
-        (blocks,),
+        (blocks // pair,),
         in_specs,
-        [by_block(block, model)] * 2
-        + [by_block(3, block, width), by_block(block, width), whole(s_shape)]
-        + [by_block(quarter, width)] * count,
-        [struct((blocks, block, model), BF16)] * 2
-        + [struct((blocks, 3, block, width)), struct((blocks, block, width)), s_shape]
+        [by_block(span, model)] * 2
+        + [by_block(3, span, width), by_block(span, width), whole(s_shape)]
+        + [by_pair(width)] * count,
+        [struct((blocks // pair, span, model), BF16)] * 2
+        + [struct((blocks // pair, 3, span, width)), struct((blocks // pair, span, width)), s_shape]
         + [struct((blocks, quarter, width))] * count,
         [
             pltpu.VMEM((3, model, width), BF16),
             pltpu.VMEM((3, model, width), BF16),
-            pltpu.VMEM((3, block + 8, width), F32),
-            pltpu.VMEM((2 * block, width), F32),
-            pltpu.VMEM((block, width), F32),
+            pltpu.VMEM((3, span + 8, width), F32),
+            pltpu.VMEM((pair, 2 * block, width), F32),
+            pltpu.VMEM((span, width), F32),
         ],
         args,
-        6 * blocks * block * width * (3 * model + 4 * block),
-    )
-    return outs[:5], outs[5:]
+        36,
+    )
+    return outs[:5], list(outs[5:])
 
 
 def hidden_forward(m_parts, weights, x_own, cotangent, bias, gain, offset):
@@ -571,20 +582,23 @@
         + [struct((rows, model), BF16)] * 2,
         [pltpu.VMEM((count, width, model), BF16)] * 2,
         args,
-        6 * rows * model * width * count,
-    )
-
-
-def feed_forward(normed, turned, cotangent, up, up_bias, down, sums):
+        9,
+    )
+
+
+def feed_forward(side, normed, turned, cotangent, up, up_bias, down, sums):
     rows, model = normed[0].shape
-    units = up.shape[1]
+    units = up_bias.shape[1]
     step = min(256, units)
     first = sums is None
-
-    def body(*refs):
-        nh_ref, nl_ref, th_ref, tl_ref, ch_ref, cl_ref, up_ref, bias_ref, down_ref = refs[:9]
-        feed_in, grad_in = (None, None) if first else refs[9:11]
-        feed_ref, grad_ref, gup_ref, gdown_ref, gbias_ref = refs[9 if first else 11 :]
+    pieces = len(up)
+
+    def body(side_ref, *refs):
+        nh_ref, nl_ref, th_ref, tl_ref, ch_ref, cl_ref, bias_ref = refs[:7]
+        up_refs, down_refs = refs[7 : 7 + pieces], refs[7 + pieces : 7 + 2 * pieces]
+        refs = refs[7 + 2 * pieces :]
+        feed_in, grad_in = (None, None) if first else refs[:2]
+        feed_ref, grad_ref, gup_ref, gdown_ref, gbias_ref = refs[0 if first else 2 :]
 
         @pl.when(pl.program_id(0) == 0)
         def _():
@@ -595,10 +609,17 @@
                 feed_ref[...] = feed_in[...]
                 grad_ref[...] = grad_in[...]
 
+        def in_order(halves, axis):
+            if pieces == 1:
+                return halves[0][...]
+            mine, other = halves[0][...], halves[1][...]
+            low = side_ref[0] == 0
+            return jnp.concatenate([jnp.where(low, mine, other), jnp.where(low, other, mine)], axis)
+
         own_normed = (nh_ref[...], nl_ref[...])
         own_cotangent = (ch_ref[...], cl_ref[...])
-        up_parts = parts_of(up_ref[...])
-        down_parts = parts_of(down_ref[...])
+        up_parts = parts_of(in_order(up_refs, 0))
+        down_parts = parts_of(in_order(down_refs, 1))
         before = dot_parts(own_normed, up_parts, NN) + bias_ref[...]
         grad_active = dot_parts(own_cotangent, down_parts, NT)
         below = 0.5 + 0.5 * lax.erf(before * math.sqrt(0.5))
@@ -614,20 +635,24 @@
         gdown_ref[...] = dot_parts(active_parts, own_cotangent, TN)
 
     total = struct((rows, model))
-    args = [*normed, *turned, *cotangent, up, up_bias, down] + ([] if first else list(sums))
-    columns = pl.BlockSpec((model, step), lambda t: (0, t))
-    one_row = pl.BlockSpec((1, step), lambda t: (0, t))
-    some_rows = pl.BlockSpec((step, model), lambda t: (t, 0))
+    args = [side, *normed, *turned, *cotangent, up_bias, *up, *down] + ([] if first else list(sums))
+    columns = lambda n: pl.BlockSpec((n, step), lambda t: (0, t))
+    some_rows = lambda n: pl.BlockSpec((step, n), lambda t: (t, 0))
     outs = run_kernel(
         body,
         "feed_forward",
         (units // step,),
-        [whole(a) for a in args[:6]] + [columns, one_row, some_rows] + [whole(a) for a in args[9:]],
-        [whole(total), whole(total), columns, some_rows, one_row],
-        [total, total, struct(up.shape), struct(down.shape), struct(up_bias.shape)],
+        [scalar_spec()]
+        + [whole(a) for a in args[1:7]]
+        + [columns(1)]
+        + [columns(model // pieces)] * pieces
+        + [some_rows(model // pieces)] * pieces
+        + [whole(a) for a in args[8 + 2 * pieces :]],
+        [whole(total), whole(total), columns(model), some_rows(model), columns(1)],
+        [total, total, struct((model, units)), struct((units, model)), struct(up_bias.shape)],
         [],
         args,
-        36 * rows * model * units,
+        18,
     )
     return outs[:2], outs[2:]
 
@@ -642,15 +667,15 @@
         h_ref, f_ref, g_ref, c_ref = refs[:4]
         m_refs, w_refs = refs[4 : 4 + count], refs[4 + count : 4 + 2 * count]
         gain_ref, bias_ref, out_ref, gh_ref, sum_ref = refs[4 + 2 * count : 9 + 2 * count]
-        gm_refs = refs[9 + 2 * count : 9 + 3 * count]
-        gw_refs = refs[9 + 3 * count : 9 + 4 * count]
-        wh_ref, wl_ref = refs[9 + 4 * count :]
+        gm_refs, refs = refs[9 + 2 * count : 9 + 3 * count], refs[9 + 3 * count :]
+        gw_refs, (wh_ref, wl_ref) = refs[:2], refs[2:]
 
         @pl.when(pl.program_id(0) == 0)
         def _():
             sum_ref[...] = jnp.zeros_like(sum_ref)
             for k in range(count):
                 wh_ref[k], wl_ref[k] = parts_of(w_refs[k][...])
+            for k in range(2):
                 gw_refs[k][...] = jnp.zeros_like(gw_refs[k])
 
         hidden_rows, grad, above = h_ref[...], g_ref[...], c_ref[...]
@@ -665,26 +690,26 @@
         parts = parts_of(grad_hidden)
         for k in range(count):
             gm_refs[k][...] = dot_parts(parts, (wh_ref[k], wl_ref[k]), NT)
-            gw_refs[k][...] += dot_parts(parts_of(m_refs[k][...]), parts, TN)
+            gw_refs[k // 2][k % 2] += dot_parts(parts_of(m_refs[k][...]), parts, TN)
 
     row_spec = lambda n: pl.BlockSpec((step, n), lambda r: (r, 0))
     args = [hidden, feed, grad_normed, cotangent, *m_parts, *weights, gain, bias]
-    sums = struct((8, model))
+    sums, pair = struct((8, model)), struct((2, width, model))
     outs = run_kernel(
         body,
         "hidden_backward",
         (rows // step,),
         [row_spec(model)] * 4 + [row_spec(width)] * count + [whole(w) for w in weights] + [whole(gain), whole(bias)],
-        [row_spec(model)] * 2 + [whole(sums)] + [row_spec(width)] * count + [whole(w) for w in weights],
-        [struct((rows, model))] * 2
-        + [sums]
-        + [struct((rows, width))] * count
-        + [struct(w.shape) for w in weights],
+        [row_spec(model)] * 2
+        + [whole(sums)]
+        + [row_spec(width)] * count
+        + [whole(pair)] * 2,
+        [struct((rows, model))] * 2 + [sums] + [struct((rows, width))] * count + [pair] * 2,
         [pltpu.VMEM((count, width, model), BF16)] * 2,
         args,
-        12 * rows * model * width * count,
-    )
-    return outs[:3], outs[3 : 3 + count], outs[3 + count :]
+        15,
+    )
+    return outs[:3], list(outs[3 : 3 + count]), outs[3 + count :]
 
 
 def mixer_backward(own, length, gm_parts, proj, conv, s_spec, k_spec, conv_w, conv_b, skip, weight, tables):
@@ -693,6 +718,8 @@
     block = quarter * count
     model = weight.shape[1]
     tile = min(32, block)
+    pair = 2 - blocks % 2
+    span = pair * block
 
     def body(*refs):
         own_ref, length_ref = refs[:2]
@@ -704,103 +731,111 @@
         gn_refs = refs[15 : 15 + count]
         wh_ref, wl_ref, ext_ref, gs_ref, o_ref, rows_ref, gn_ref = refs[15 + count :]
         step = pl.program_id(0)
-        b = blocks - 1 - step
+        slot = blocks // pair - 1 - step
         me = own_ref[0]
 
         @pl.when(step == 0)
         def _():
             for k in range(3):
                 wh_ref[k], wl_ref[k] = parts_of(weight_ref[k])
-            gs_ref[:, block:] = jnp.zeros((3, 8, width), F32)
+            gs_ref[:, span:] = jnp.zeros((3, 8, width), F32)
             sum_ref[...] = jnp.zeros_like(sum_ref)
 
-        for k in range(count):
-            start = pl.multiple_of((me ^ k) * quarter, quarter)
-            rows_ref[pl.ds(start, quarter), :] = gm_refs[k][0]
-        inside = (b > 0).astype(F32)
+        for u in range(pair):
+            for k in range(count):
+                start = pl.multiple_of(u * block + (me ^ k) * quarter, quarter)
+                rows_ref[pl.ds(start, quarter), :] = gm_refs[k][u]
+        inside = (slot > 0).astype(F32)
         short = []
         for k in range(3):
             ext_ref[k, :8] = rim_ref[0, k] * inside
             ext_ref[k, 8:] = proj_ref[0, k]
             short.append(
-                conv_w_ref[0, k : k + 1, :] * ext_ref[k, 6 : 6 + block]
-                + conv_w_ref[1, k : k + 1, :] * ext_ref[k, 7 : 7 + block]
+                conv_w_ref[0, k : k + 1, :] * ext_ref[k, 6 : 6 + span]
+                + conv_w_ref[1, k : k + 1, :] * ext_ref[k, 7 : 7 + span]
                 + conv_w_ref[2, k : k + 1, :] * proj_ref[0, k]
                 + conv_b_ref[k : k + 1, :]
             )
-        places = b * block + lax.broadcasted_iota(jnp.int32, (block, 1), 0)
+        places = slot * span + lax.broadcasted_iota(jnp.int32, (span, 1), 0)
         mask = (places < length_ref[0]).astype(F32)
         gate_in, values = short[1] * mask, short[2] * mask
         grad_mixed = rows_ref[...]
         grad_conv = grad_mixed * short[0]
-        gs_ref[0, :block] = grad_mixed * conv_ref[0]
-        g_ref[b] = dot_parts((th_ref[...], tl_ref[...]), parts_of(grad_conv), NN)
-        for r in range(0, block, tile):
-            lo = slice(r, r + tile)
-            hi = slice(block + r, block + r + tile)
-
-            def product(j, total, lo=lo, hi=hi):
-                g_re, g_im = g_ref[j, lo], g_ref[j, hi]
-                k_re, k_im = k_ref[j - b, lo], k_ref[j - b, hi]
-                return total[0] + g_re * k_re + g_im * k_im, total[1] + g_im * k_re - g_re * k_im
-
-            zero = jnp.zeros((tile, width), F32)
-            o_ref[lo], o_ref[hi] = lax.fori_loop(b, blocks, product, (zero, zero))
-        grad_signal = dot_parts((ih_ref[...], il_ref[...]), parts_of(o_ref[...]), NN)
+        gs_ref[0, :span] = grad_mixed * conv_ref[0]
+        for u in range(pair):
+            part = grad_conv[u * block : (u + 1) * block]
+            g_ref[slot * pair + u] = dot_parts((th_ref[...], tl_ref[...]), parts_of(part), NN)
+        for u in range(pair):
+            b = slot * pair + u
+            for r in range(0, block, tile):
+                lo = slice(r, r + tile)
+                hi = slice(block + r, block + r + tile)
+
+                def product(j, total, b=b, lo=lo, hi=hi):
+                    g_re, g_im = g_ref[j, lo], g_ref[j, hi]
+                    k_re, k_im = k_ref[j - b, lo], k_ref[j - b, hi]
+                    return total[0] + g_re * k_re + g_im * k_im, total[1] + g_im * k_re - g_re * k_im
+
+                zero = jnp.zeros((tile, width), F32)
+                o_ref[u, lo], o_ref[u, hi] = lax.fori_loop(b, blocks, product, (zero, zero))
+        inverse = (ih_ref[...], il_ref[...])
+        grad_signal = jnp.concatenate([dot_parts(inverse, parts_of(o_ref[u]), NN) for u in range(pair)], 0)
         grad_signal = grad_signal + skip_ref[...] * grad_conv
-        gs_ref[1, :block] = grad_signal * values
-        gs_ref[2, :block] = grad_signal * gate_in
+        gs_ref[1, :span] = grad_signal * values
+        gs_ref[2, :span] = grad_signal * gate_in
         sum_ref[0:1] += column_sum(grad_conv * short[2] * gate_in)
-        normed_grad = jnp.zeros((block, model), F32)
+        normed_grad = jnp.zeros((span, model), F32)
         for k in range(3):
-            grad_short = gs_ref[k, :block]
+            grad_short = gs_ref[k, :span]
             sum_ref[1 + k : 2 + k] += column_sum(grad_short)
             for t in range(3):
                 row = 4 + 3 * t + k
-                sum_ref[row : row + 1] += column_sum(grad_short * ext_ref[k, 6 + t : 6 + t + block])
+                sum_ref[row : row + 1] += column_sum(grad_short * ext_ref[k, 6 + t : 6 + t + span])
             grad_proj = (
                 conv_w_ref[2, k : k + 1, :] * grad_short
-                + conv_w_ref[1, k : k + 1, :] * gs_ref[k, 1 : 1 + block]
-                + conv_w_ref[0, k : k + 1, :] * gs_ref[k, 2 : 2 + block]
+                + conv_w_ref[1, k : k + 1, :] * gs_ref[k, 1 : 1 + span]
+                + conv_w_ref[0, k : k + 1, :] * gs_ref[k, 2 : 2 + span]
             )
             sum_ref[13 + k : 14 + k] += column_sum(grad_proj)
             gp_ref[0, k] = grad_proj
             normed_grad = normed_grad + dot_parts(parts_of(grad_proj), (wh_ref[k], wl_ref[k]), NT)
-            gs_ref[k, block:] = gs_ref[k, :8]
+            gs_ref[k, span:] = gs_ref[k, :8]
         gn_ref[...] = normed_grad
-        for k in range(count):
-            start = pl.multiple_of((me ^ k) * quarter, quarter)
-            gn_refs[k][0] = gn_ref[pl.ds(start, quarter), :]
-
-    last = blocks - 1
+        for u in range(pair):
+            for k in range(count):
+                start = pl.multiple_of(u * block + (me ^ k) * quarter, quarter)
+                gn_refs[k][u] = gn_ref[pl.ds(start, quarter), :]
+
+    last = blocks // pair - 1
     by_block = lambda *shape: pl.BlockSpec((1,) + shape, lambda s: (last - s,) + (0,) * len(shape))
-    rim = pl.BlockSpec((1, 3, 8, width), lambda s: (jnp.maximum(last - s - 1, 0), 0, block // 8 - 1, 0))
+    rim = pl.BlockSpec((1, 3, 8, width), lambda s: (jnp.maximum(last - s - 1, 0), 0, span // 8 - 1, 0))
+    by_pair = lambda n: pl.BlockSpec((pair, quarter, n), lambda s: (last - s, 0, 0))
     fixed = [k_spec, conv_w, conv_b, skip, weight, *tables]
     spectra = struct((blocks, 2 * block, width))
     sums = struct((16, width))
     outs = run_kernel(
         body,
         "mixer_backward",
-        (blocks,),
+        (blocks // pair,),
         [scalar_spec(), scalar_spec()]
-        + [by_block(quarter, width)] * count
-        + [by_block(3, block, width), rim, by_block(block, width)]
+        + [by_pair(width)] * count
+        + [by_block(3, span, width), rim, by_block(span, width)]
         + [whole(a) for a in fixed],
-        [whole(spectra), by_block(3, block, width), whole(sums)] + [by_block(quarter, model)] * count,
-        [spectra, struct((blocks, 3, block, width)), sums] + [struct((blocks, quarter, model))] * count,
+        [whole(spectra), by_block(3, span, width), whole(sums)] + [by_pair(model)] * count,
+        [spectra, struct((blocks // pair, 3, span, width)), sums] + [struct((blocks, quarter, model))] * count,
         [
             pltpu.VMEM((3, model, width), BF16),
             pltpu.VMEM((3, model, width), BF16),
-            pltpu.VMEM((3, block + 8, width), F32),
-            pltpu.VMEM((3, block + 8, width), F32),
-            pltpu.VMEM((2 * block, width), F32),
-            pltpu.VMEM((block, width), F32),
-            pltpu.VMEM((block, model), F32),
+            pltpu.VMEM((3, span + 8, width), F32),
+            pltpu.VMEM((3, span + 8, width), F32),
+            pltpu.VMEM((pair, 2 * block, width), F32),
+            pltpu.VMEM((span, width), F32),
+            pltpu.VMEM((span, model), F32),
         ],
         [own, length, *gm_parts, proj, proj, conv, *fixed],
-        6 * blocks * block * width * (3 * model + 4 * block),
-    )
-    return outs[:3], outs[3:]
+        35,
+    )
+    return outs[:3], list(outs[3:])
 
 
 def filter_backward(s_spec, g_spec, tables):
@@ -842,7 +877,7 @@
         [struct((blocks, block, width))],
         [pltpu.VMEM((double, width), F32)] * 2,
         [s_spec, g_spec, *inverse],
-        12 * blocks * block * block * width,
+        13,
     )[0]
 
 
@@ -857,10 +892,10 @@
 
         normed = (nh_ref[0], nl_ref[0])
         for k in range(3):
-            out_ref[k] += dot_parts(normed, parts_of(gp_ref[0, k]), TN)
+            out_ref[k] += dot_parts(parts_of(gp_ref[0, k]), normed, TN)
 
     by_block = lambda *shape: pl.BlockSpec((1,) + shape, lambda b: (b,) + (0,) * len(shape))
-    out = struct((3, model, width))
+    out = struct((3, width, model))
     return run_kernel(
         body,
         "input_weight_grad",
@@ -870,7 +905,7 @@
         [out],
         [],
         [normed_high, normed_low, grad_proj],
-        18 * blocks * block * model * width,
+        12,
     )[0]
 
 
@@ -904,7 +939,7 @@
         [struct((rows, model)), sums],
         [],
         [*grad_pieces, x_own, grad_hidden, gain],
-        20 * rows * model,
+        5,
     )
 
 
@@ -927,7 +962,7 @@
         [struct((groups, quarter * count, model))],
         [],
         [own, *pieces],
-        0,
+        8,
     )[0]
 
 
@@ -942,6 +977,23 @@
         values = values + swap(values, axis, bit)
         bit *= 2
     return values
+
+
+def meet(*values):
+    return lax.optimization_barrier(values)
+
+
+def split_rows(values, axis, bit):
+    mine = (lax.axis_index(axis) // bit) % 2
+    half = values.shape[0] // 2
+    leaving = lax.dynamic_slice_in_dim(values, (1 - mine) * half, half, 0)
+    staying = lax.dynamic_slice_in_dim(values, mine * half, half, 0)
+    return leaving, staying
+
+
+def join_rows(values, other, axis, bit):
+    first = (lax.axis_index(axis) // bit) % 2 == 0
+    return jnp.concatenate([jnp.where(first, values, other), jnp.where(first, other, values)], 0)
 
 
 def transpose_blocks(values):
@@ -1016,81 +1068,203 @@
         part = lax.dynamic_slice_in_dim(values, chan_index * quarter, quarter, 1)
         return transpose_blocks(part)
 
-    x_own = own_rows(block_input)
-    x_parts = spread(x_own)
-    x_own, cotangent_home = lax.optimization_barrier((x_own, cotangent))
-    cot_own = own_rows(cotangent_home).reshape(rows, model)
-    x_rows = x_own.reshape(rows, model)
-
-    up_parts = spread(up_weight)
-    late, down_home, out_home = lax.optimization_barrier((x_parts[2], down_weight, output_weight))
-    x_parts = [x_parts[0], x_parts[1], late, x_parts[3]]
-    down_parts = spread(down_home)
-    out_parts = spread(out_home)
-    up_bias_parts = [swap(up_bias, "chan", k) if k else up_bias for k in range(count)]
-
     place_values = jnp.arange(seq_length, dtype=jnp.int32).astype(F32)
     features = position_features(place_values, seq_length, filt_w1.shape[0])
     kernel, filter_pull = jax.vjp(
         partial(implicit_filter, features, place_values), filt_w1, filt_b1, filt_w2, filt_b2, filt_w3, decay
     )
     k_spec = filter_spectrum(kernel.reshape(blocks, block, width), tables)
-
     weight = jnp.transpose(input_weight, (1, 0, 2))
+
+    x_own = own_rows(block_input)
+    side = (seq_index % 2).astype(jnp.int32)
+
+    def half_of(values, axis):
+        half = values.shape[axis] // 2
+        return lax.dynamic_slice_in_dim(values, side * half, half, axis)
+
+    up_far = swap(half_of(up_weight, 0), "chan", 2)
+    up_bias_parts = [swap(up_bias, "chan", k) if k else up_bias for k in range(count)]
+    x_own, k_spec, weight, up_far, up_bias_parts, cotangent_home = meet(
+        x_own, k_spec, weight, up_far, up_bias_parts, cotangent
+    )
+    x_far = swap(x_own, "chan", 2)
+    x_parts = [x_own, swap(x_own, "chan", 1), x_far, swap(x_far, "chan", 1)]
+    cot_own = own_rows(cotangent_home)
+    x_rows = x_own.reshape(rows, model)
+    x_parts[2], out_home, down_home, up_far = meet(x_parts[2], output_weight, down_weight, up_far)
+    out_far = swap(out_home, "chan", 2)
+    down_far = swap(half_of(down_home, 1), "chan", 2)
+    up_other = swap(up_far, "seq", 1)
+    x_parts[0], cot_own = meet(x_parts[0], cot_own)
+    cot_own = cot_own.reshape(rows, model)
+
     (normed_high, normed_low, proj, conv, s_spec), mixed = mixer_forward(
         own, length, x_parts, row(ln1_gain), row(ln1_bias), weight, input_bias, conv_w, conv_b, row(skip), k_spec, tables
     )
+    *mixed, down_far, out_far, up_other = meet(*mixed, down_far, out_far, up_other)
     mixed = [m if k == 0 else swap(m, "chan", k) for k, m in enumerate(mixed)]
+    down_other = swap(down_far, "seq", 1)
+    out_3 = swap(out_far, "chan", 1)
+    *mixed, out_3 = meet(*mixed, out_3)
+    out_parts = [output_weight, swap(output_weight, "chan", 1), out_far, out_3]
+    up_parts = [[up_weight], [swap(up_weight, "chan", 1)], [up_far, up_other]]
+    up_parts.append([swap(u, "chan", 1) for u in up_parts[2]])
+    down_parts = [[down_weight], [swap(down_weight, "chan", 1)], [down_far, down_other]]
+    down_parts.append([swap(d, "chan", 1) for d in down_parts[2]])
     mixed = [m.reshape(rows, width) for m in mixed]
 
     hidden, *rest = hidden_forward(
         mixed, out_parts, x_rows, cot_own, row(output_bias), row(ln2_gain), row(ln2_bias)
     )
     normed2, turned, cot_parts = rest[0:2], rest[2:4], rest[4:6]
-    sums = None
-    grads_up, grads_down, grads_up_bias = [None] * count, [None] * count, [None] * count
-    for k in (1, 0, 3, 2):
-        sums, (grads_up[k], grads_down[k], grads_up_bias[k]) = feed_forward(
-            normed2, turned, cot_parts, up_parts[k], row(up_bias_parts[k]), down_parts[k], sums
+
+    def units(k, sums):
+        return feed_forward(
+            side.reshape(1), normed2, turned, cot_parts, up_parts[k], row(up_bias_parts[k]), down_parts[k], sums
         )
-    (out_rows, grad_hidden, sums2), grad_mixed, grads_out = hidden_backward(
+
+    bias_grads = [None] * count
+    sums, (up_3, down_3, bias_grads[3]) = units(3, None)
+    up_3, down_3 = swap(up_3, "chan", 1), swap(down_3, "chan", 1)
+    sums, (up_2, down_2, bias_grads[2]) = units(2, sums)
+    *sums, far_up, far_down = meet(*sums, up_2 + up_3, down_2 + down_3)
+
+    third = model // 3
+    half = far_down.shape[0] // 2
+    far_ups = [swap(far_up[:third], "chan", 2)]
+    leaving, staying = split_rows(far_down, "seq", 1)
+    came = [swap(leaving[: half // 2], "seq", 1)]
+    sums, (up_1, down_1, bias_grads[1]) = units(1, sums)
+    *sums, far_ups[0], came[0], up_1, down_1 = meet(*sums, far_ups[0], came[0], up_1, down_1)
+    up_1, down_1 = swap(up_1, "chan", 1), swap(down_1, "chan", 1)
+    far_ups.append(swap(far_up[third : 2 * third], "chan", 2))
+    came.append(swap(leaving[half // 2 :], "seq", 1))
+    sums, (up_0, down_0, bias_grads[0]) = units(0, sums)
+    *sums, far_ups[1], far_down, up_1, down_1 = meet(
+        *sums, far_ups[1], staying + jnp.concatenate(came, 0), up_1, down_1
+    )
+    far_ups.append(swap(far_up[2 * third :], "chan", 2))
+    leaving, far_staying = split_rows(far_down, "seq", 2)
+    far_came = swap(leaving, "seq", 2)
+    leaving_0, staying_0 = split_rows(down_0, "seq", 1)
+    leaving_1, staying_1 = split_rows(down_1, "seq", 1)
+    near_came = swap(leaving_0 + leaving_1, "seq", 1)
+    (out_rows, grad_hidden, sums2), grad_mixed, (out_near, out_far) = hidden_backward(
         hidden, sums[0], sums[1], cot_own, mixed, out_parts, row(ln2_gain), row(down_bias)
+    )
+    grad_hidden, far_ups[2], far_came, grad_mixed, out_rows = meet(
+        grad_hidden, far_ups[2], far_came, grad_mixed, out_rows
     )
 
     grad_mixed = [g.reshape(blocks, quarter, width) for g in grad_mixed]
     grad_mixed = [g if k == 0 else swap(g, "chan", k) for k, g in enumerate(grad_mixed)]
+    leaving, far_staying = split_rows(far_staying + far_came, "seq", 4)
+    far_came = swap(leaving, "seq", 4)
+    out_blocks = transpose_blocks(out_rows.reshape(blocks, quarter, model))
+    grad_up = up_0 + up_1 + jnp.concatenate(far_ups, 0)
+    grad_mixed, grad_up, out_far, near_came = meet(grad_mixed, grad_up, out_far, near_came)
+
+    up_leaving, up_staying = split_rows(grad_up, "seq", 1)
+    up_came = swap(up_leaving, "seq", 1)
+    leaving, near_staying = split_rows(staying_0 + staying_1 + near_came, "seq", 2)
+    near_came = swap(leaving, "seq", 2)
+    out_far = swap(out_far, "chan", 2)
     (g_spec, grad_proj, mixer_sums), grad_normed = mixer_backward(
         own, length, grad_mixed, proj, conv, s_spec, k_spec, conv_w, conv_b, row(skip), weight, tables
     )
-
-    def to_home(values):
-        part = transpose_blocks(values.reshape(blocks, quarter, model))
-        return put_together(own, spread(part))
-
-    output = to_home(out_rows)
-    grad_down = sum(collect(grads_down))
-    grad_up = sum(collect(grads_up))
-    grad_out = sum(collect(grads_out))
-    grad_down, grad_up, grad_out = lax.psum((grad_down, grad_up, grad_out), "seq")
-
-    pieces = [p.reshape(rows, model) for p in collect(grad_normed)]
+    grad_normed, grad_proj, out_far, near_came, up_came, out_blocks, far_came = meet(
+        grad_normed, grad_proj, out_far, near_came, up_came, out_blocks, far_came
+    )
+
+    grad_normed[3], grad_normed[1] = swap(grad_normed[3], "chan", 1), swap(grad_normed[1], "chan", 1)
+    far_down = swap(far_staying + far_came, "chan", 2)
+    leaving, near_staying = split_rows(near_staying + near_came, "seq", 4)
+    up_leaving, up_staying = split_rows(up_staying + up_came, "seq", 2)
+    far_normed, grad_proj, leaving, up_leaving = meet(
+        grad_normed[2] + grad_normed[3], grad_proj, leaving, up_leaving
+    )
+    far_normed = swap(far_normed, "chan", 2)
+    near_came, up_came = swap(leaving, "seq", 4), swap(up_leaving, "seq", 2)
+    grad_in = input_weight_grad(normed_high, normed_low, grad_proj)
+    grad_out = out_near[0] + out_far[0] + swap(out_near[1] + out_far[1], "chan", 1)
+    g_spec, grad_in, grad_out, near_came, far_down, up_came = meet(
+        g_spec, grad_in, grad_out, near_came, far_down, up_came
+    )
+
+    grad_down = near_staying + near_came + far_down
+    down_came = swap(grad_down, "seq", 4)
+    up_leaving, up_staying = split_rows(up_staying + up_came, "seq", 4)
+    up_came = swap(up_leaving, "seq", 4)
+    mixer_leaving, mixer_staying = split_rows(
+        jnp.concatenate([grad_in.reshape(-1, model), grad_out], 0), "seq", 1
+    )
+    mixer_came = swap(mixer_leaving, "seq", 1)
+    grad_kernel = filter_backward(s_spec, g_spec, tables).reshape(seq_length, width)
+    far_normed, grad_kernel, down_came, up_came = meet(far_normed, grad_kernel, down_came, up_came)
+
+    pieces = [p.reshape(rows, model) for p in (grad_normed[0], grad_normed[1], far_normed)]
     grad_x_rows, sums1 = input_backward(pieces, x_rows, grad_hidden, row(ln1_gain))
-    grad_x = to_home(grad_x_rows)
-
-    grad_in = input_weight_grad(normed_high, normed_low, grad_proj)
-    grad_in = lax.psum(grad_in, "seq")
-    grad_in = jnp.transpose(grad_in, (1, 0, 2))
-
-    grad_kernel = filter_backward(s_spec, g_spec, tables).reshape(seq_length, width)
+    grad_x_rows, grad_kernel, out_blocks, mixer_came, down_came, up_came, sums1 = meet(
+        grad_x_rows, grad_kernel, out_blocks, mixer_came, down_came, up_came, sums1
+    )
+
+    grad_x_blocks = transpose_blocks(grad_x_rows.reshape(blocks, quarter, model))
+    leaving, staying = split_rows(mixer_staying + mixer_came, "seq", 2)
+    came = swap(leaving, "seq", 2)
+    grad_up, grad_down = up_staying + up_came, join_rows(grad_down, down_came, "seq", 4)
+    down_came, up_came = swap(grad_down, "seq", 2), swap(grad_up, "seq", 4)
+    out_far, out_near = swap(out_blocks, "chan", 2), swap(out_blocks, "chan", 1)
     grad_fw1, grad_fb1, grad_fw2, grad_fb2, grad_fw3, grad_decay = filter_pull(grad_kernel)
-
+    grad_x_blocks, came, up_came, down_came, grad_fw3, out_far, out_near = meet(
+        grad_x_blocks, came, up_came, down_came, grad_fw3, out_far, out_near
+    )
+
+    grad_x_far = swap(grad_x_blocks, "chan", 2)
+    out_side = swap(out_far, "chan", 1)
+    leaving, staying = split_rows(staying + came, "seq", 4)
+    came = swap(leaving, "seq", 4)
+    grad_up, grad_down = join_rows(grad_up, up_came, "seq", 4), join_rows(grad_down, down_came, "seq", 2)
+    down_came, up_came = swap(grad_down, "seq", 1), swap(grad_up, "seq", 2)
     up_bias_grads = jnp.take(
-        jnp.concatenate(grads_up_bias, 0), jnp.arange(count, dtype=jnp.int32) ^ chan_index, axis=0
+        jnp.concatenate(bias_grads, 0), jnp.arange(count, dtype=jnp.int32) ^ chan_index, axis=0
     )
     shared = [sums1[0], sums1[1], *[sums2[i] for i in range(4)], up_bias_grads, grad_fw1, grad_fb1, grad_fw2, grad_fb2]
     split = [mixer_sums, grad_fw3, grad_decay]
-    shared_flat = total_over(pack(shared), "chan")
-    flat = total_over(jnp.concatenate([shared_flat, pack(split)]), "seq")
+    shared_flat, split_flat = pack(shared), pack(split)
+    came, up_came, out_side, shared_flat, grad_x_blocks = meet(came, up_came, out_side, shared_flat, grad_x_blocks)
+
+    mixer_grads = staying + came
+    came = swap(mixer_grads, "seq", 4)
+    grad_up = join_rows(grad_up, up_came, "seq", 2)
+    up_came = swap(grad_up, "seq", 1)
+    side_flat = swap(shared_flat, "chan", 1)
+    output = put_together(own, [out_blocks, out_near, out_far, out_side])
+    came, grad_x_far, output, side_flat, grad_x_blocks = meet(came, grad_x_far, output, side_flat, grad_x_blocks)
+
+    mixer_grads = join_rows(mixer_grads, came, "seq", 4)
+    came = swap(mixer_grads, "seq", 2)
+    grad_x_near, grad_x_side = swap(grad_x_blocks, "chan", 1), swap(grad_x_far, "chan", 1)
+    shared_flat = shared_flat + side_flat
+    side_flat = swap(shared_flat, "chan", 2)
+    came, grad_x_near, grad_x_side, side_flat, up_came, down_came = meet(
+        came, grad_x_near, grad_x_side, side_flat, up_came, down_came
+    )
+
+    flat = jnp.concatenate([shared_flat + side_flat, split_flat])
+    mixer_grads = join_rows(mixer_grads, came, "seq", 2)
+    side_flat, came = swap(flat, "seq", 2), swap(mixer_grads, "seq", 1)
+    grad_x = put_together(own, [grad_x_blocks, grad_x_near, grad_x_far, grad_x_side])
+    grad_down = join_rows(grad_down, down_came, "seq", 1)
+    side_flat, grad_x, grad_down = meet(side_flat, grad_x, grad_down)
+    flat = flat + side_flat
+    flat = flat + swap(flat, "seq", 4)
+    flat = flat + swap(flat, "seq", 1)
+    mixer_grads = join_rows(mixer_grads, came, "seq", 1)
+    grad_up = join_rows(grad_up, up_came, "seq", 1)
+    grad_in = jnp.transpose(mixer_grads[: 3 * width].reshape(3, width, model), (2, 0, 1))
+    grad_out = mixer_grads[3 * width :]
+
     cut = shared_flat.shape[0]
     grad_ln1_gain, grad_ln1_bias, grad_ln2_gain, grad_ln2_bias, grad_b_out, grad_b_fc2, up_bias_grads, *filt = unpack(
         flat[:cut], shared

time: 865 us -> 609 us (0.70)
  waiting for transfers between devices: 460 us -> 195 us
  starting transfers between devices: 33.6 us -> 82.3 us
  blocking collectives: 44.1 us -> 0 us
  other arithmetic: 19.4 us -> 40.7 us
  between operations: 15 us -> 2.27 us
  local copies, waits for them, and re-layouts: 39.5 us -> 49.5 us
    ppermute x44 -> x71, waiting for transfers between devices: 322 us -> 177 us  [swap(): return lax.ppermute(values, axis, [(i, i ^ bit) for i in range(size)])]
    psum x1 -> x0, waiting for transfers between devices: 94 us -> none  [sequence_device(): grad_in = lax.psum(grad_in, 'seq')]
    all_to_all x1 -> x0, blocking collectives: 44.1 us -> none  [transpose_blocks(): lax.all_to_all(values, 'seq', split_axis=0, concat_axis=0, tiled=True)]
    ppermute x44 -> x71, starting transfers between devices: 20.7 us -> 63.3 us  [swap(): return lax.ppermute(values, axis, [(i, i ^ bit) for i in range(size)])]
    all_to_all x3 -> x4, waiting for transfers between devices: 44.4 us -> 17.1 us  [transpose_blocks(): lax.all_to_all(values, 'seq', split_axis=0, concat_axis=0, tiled=True)]
    concatenate x2 -> x12, other arithmetic: 0.03 us -> 11.1 us  [the longest x9 9.75 us: join_rows(): jnp.concatenate([jnp.where(first, values, other), jnp.where(first, other,...]
    all_to_all x3 -> x4, starting transfers between devices: 12.8 us -> 19 us  [transpose_blocks(): lax.all_to_all(values, 'seq', split_axis=0, concat_axis=0, tiled=True)]
    add x12 -> x24, other arithmetic: 16.7 us -> 22.8 us  [the longest x2 4.79 us: sequence_device(): *sums, far_up, far_down = meet(*sums, up_2 + up_3, down_2 + down_3)]
  transfers between devices with their start and end apart: 48 -> 75, of which waited for: 17 -> 25; matrix products, arithmetic and copies ran while one was open for 8% -> 15% of each run, Pallas kernels for 24% -> 33%
where the time goes in v2:
time: 609 us; the launch traced here: 601 us
  Pallas kernels  213 us (35%)
  waiting for transfers between devices  195 us (32%)
  starting transfers between devices  82.3 us (14%)
  local copies, waits for them, and re-layouts  49.5 us (8%)
  other arithmetic  40.7 us (7%)
  matrix products  19.1 us (3%)
    pallas_call x14, Pallas kernels, run_kernel(): pl.pallas_call(body, name=name, grid=grid, in_specs=in_specs, out_specs=o...  213 us
    ppermute x71, waiting for transfers between devices, swap(): return lax.ppermute(values, axis, [(i, i ^ bit) for i in range(size)])  177 us
    ppermute x71, starting transfers between devices, swap(): return lax.ppermute(values, axis, [(i, i ^ bit) for i in range(size)])  63.3 us
    all_to_all x4, starting transfers between devices, transpose_blocks(): lax.all_to_all(values, 'seq', split_axis=0, concat_axis=0, tiled=True)  19 us
    all_to_all x4, waiting for transfers between devices, transpose_blocks(): lax.all_to_all(values, 'seq', split_axis=0, concat_axis=0, tiled=True)  17.1 us
    unnamed x187, local copies, waits for them, and re-layouts  14.7 us
  transfers between devices with their start and end apart: 75, of which 25 were waited for; matrix products, arithmetic and copies ran while one was open for 15% of the time, Pallas kernels for 33%

profile of v2, /device:TPU:0, one launch (start us, length us, event | category | flops | bytes accessed | tf_op | source)
XLA Modules:
  0.0 601.5 jit_solution(11476720966164315554)
XLA Ops:
  28.3 7.7 %filter_spectrum.1.refs_13_.refs_9_ = f32[8,512,192]{2,1,0:T(8,128)} custom-call(f32[8,256,192]{2,1,0:T(8,128)} %bitcast.48, bf16[512,256]{1,0:T(8,128)(2,1)} %constant.202.clone.high_ref.refs_14_, bf16[512,256]{1,0:T(8,128)(2,1)} %constant.203.clone.low_ref.refs_15_), custom_call_target="tpu_custom_call" | custom-call | flops 9200000000 | bytes 28800000 | tf_op jit(solution)/shard_map/filter_spectrum/pallas_call | solution.py:373
  37.9 15.9 %all-to-all-done.refs_2_ = f32[8,64,768]{2,1,0:T(8,128)S(1)} async-done(((f32[8,64,768]{2,1,0:T(8,128)}), f32[8,64,768]{2,1,0:T(8,128)S(1)}, u32[]{:S(2)}, u32[]{:S(2)}) %all-to-all-start) | async-done | bytes 1572896 | tf_op jit(solution)/shard_map/all_to_all | solution.py:1000
  61.1 28.1 %collective-permute-done.5.refs_4_ = f32[8,64,768]{2,1,0:T(8,128)} collective-permute-done((f32[8,64,768]{2,1,0:T(8,128)S(1)}, f32[8,64,768]{2,1,0:T(8,128)}, u32[]{:S(2)}, u32[]{:S(2)}) %collective-permute-start.5) | collective-permute-done | bytes 1572896 | tf_op jit(solution)/shard_map/ppermute | solution.py:971
  98.2 32.1 %mixer_forward.1 = (bf16[4,512,768]{2,1,0:T(8,128)(2,1)}, bf16[4,512,768]{2,1,0:T(8,128)(2,1)}, f32[4,3,512,192]{3,2,1,0:T(8,128)}, f32[4,512,192]{2,1,0:T(8,128...) custom-call(s32[1]{0:T(128)} %bitcast.refs_0_.own_ref, ...), custom_call_target="tpu_custom_call" | custom-call | flops 41400000512 | bytes 129600000 | tf_op jit(solution)/shard_map/mixer_forward/pallas_call | solution.py:373
  138.9 12.9 %collective-permute-done.11 = f32[8,64,192]{2,1,0:T(8,128)S(1)} collective-permute-done((f32[8,64,192]{2,1,0:T(8,128)}, f32[8,64,192]{2,1,0:T(8,128)S(1)}, u32[]{:S(2)}, u32[]{:S(2)}) %collective-permute-start.11) | collective-permute-done | bytes 393248 | tf_op jit(solution)/shard_map/ppermute | solution.py:971
  151.7 9.3 %collective-permute-done.12 = f32[8,64,192]{2,1,0:T(8,128)S(1)} collective-permute-done((f32[8,64,192]{2,1,0:T(8,128)}, f32[8,64,192]{2,1,0:T(8,128)S(1)}, u32[]{:S(2)}, u32[]{:S(2)}) %collective-permute-start.12) | collective-permute-done | bytes 393248 | tf_op jit(solution)/shard_map/ppermute | solution.py:971
  165.9 9.0 %hidden_forward.1 = (f32[512,768]{1,0:T(8,128)}, bf16[512,768]{1,0:T(8,128)(2,1)}, bf16[512,768]{1,0:T(8,128)(2,1)}, bf16[768,512]{1,0:T(8,128)(2,1)}, bf16[768,...) custom-call(f32[512,192]{1,0:T(8,128)} %bitcast.65, f32[512,192]{1,0:T(8,128)} %bitcast.56, ...), custom_call_target="tpu_custom_call" | custom-call | flops 10350000128 | bytes 32400000 | tf_op jit(solution)/shard_map/hidden_forward/pallas_call | solution.py:373
  177.3 17.1 %feed_forward.4 = (f32[512,768]{1,0:T(8,128)}, f32[512,768]{1,0:T(8,128)}, f32[768,768]{1,0:T(8,128)}, f32[768,768]{1,0:T(8,128)}, f32[1,768]{1,0:T(1,128)}) custom-call(s32[1]{0:T(128)} %bitcast.10.side_ref, bf16[512,768]{1,0:T(8,128)(2,1)} %get-tuple-element.218.refs_0_, bf16[512,768]{1,0:T(8,128)(2,1)} %get-tuple-element.219.refs_1_, ...), custom_call_target="tpu_custom_call" | custom-call | flops 20700000256 | bytes 64800000 | tf_op jit(solution)/shard_map/feed_forward/pallas_call | solution.py:373
  196.7 18.3 %feed_forward.5 = (f32[512,768]{1,0:T(8,128)}, f32[512,768]{1,0:T(8,128)}, f32[768,768]{1,0:T(8,128)}, f32[768,768]{1,0:T(8,128)}, f32[1,768]{1,0:T(1,128)}) custom-call(s32[1]{0:T(128)} %bitcast.10.side_ref, bf16[512,768]{1,0:T(8,128)(2,1)} %get-tuple-element.218.refs_0_, bf16[512,768]{1,0:T(8,128)(2,1)} %get-tuple-element.219.refs_1_, ...), custom_call_target="tpu_custom_call" | custom-call | flops 20700000256 | bytes 64800000 | tf_op jit(solution)/shard_map/feed_forward/pallas_call | solution.py:373
  225.2 18.0 %feed_forward.6 = (f32[512,768]{1,0:T(8,128)}, f32[512,768]{1,0:T(8,128)}, f32[768,768]{1,0:T(8,128)}, f32[768,768]{1,0:T(8,128)}, f32[1,768]{1,0:T(1,128)}) custom-call(s32[1]{0:T(128)} %bitcast.10.side_ref, bf16[512,768]{1,0:T(8,128)(2,1)} %get-tuple-element.218.refs_0_, bf16[512,768]{1,0:T(8,128)(2,1)} %get-tuple-element.219.refs_1_, ...), custom_call_target="tpu_custom_call" | custom-call | flops 20700000256 | bytes 64800000 | tf_op jit(solution)/shard_map/feed_forward/pallas_call | solution.py:373
  248.5 18.5 %feed_forward.7 = (f32[512,768]{1,0:T(8,128)}, f32[512,768]{1,0:T(8,128)}, f32[768,768]{1,0:T(8,128)}, f32[768,768]{1,0:T(8,128)}, f32[1,768]{1,0:T(1,128)}) custom-call(s32[1]{0:T(128)} %bitcast.10.side_ref, bf16[512,768]{1,0:T(8,128)(2,1)} %get-tuple-element.218.refs_0_, bf16[512,768]{1,0:T(8,128)(2,1)} %get-tuple-element.219.refs_1_, ...), custom_call_target="tpu_custom_call" | custom-call | flops 20700000256 | bytes 64800000 | tf_op jit(solution)/shard_map/feed_forward/pallas_call | solution.py:373
  272.7 14.9 %hidden_backward.1 = (f32[512,768]{1,0:T(8,128)}, f32[512,768]{1,0:T(8,128)}, f32[8,768]{1,0:T(8,128)}, f32[512,192]{1,0:T(8,128)}, f32[512,192]{1,0:T(8,128)}, ...) custom-call(f32[512,768]{1,0:T(8,128)} %get-tuple-element.217.refs_0_, ...), custom_call_target="tpu_custom_call" | custom-call | flops 17250000896 | bytes 54000000 | tf_op jit(solution)/shard_map/hidden_backward/pallas_call | solution.py:373
  306.2 10.5 %collective-permute-done.34.refs_5_ = f32[8,64,192]{2,1,0:T(8,128)} collective-permute-done((f32[8,64,192]{2,1,0:T(8,128)}, f32[8,64,192]{2,1,0:T(8,128)}, u32[]{:S(2)}, u32[]{:S(2)}) %collective-permute-start.34) | collective-permute-done | bytes 393248 | tf_op jit(solution)/shard_map/ppermute | solution.py:971
  322.5 33.6 %mixer_backward.1 = (f32[8,512,192]{2,1,0:T(8,128)}, f32[4,3,512,192]{3,2,1,0:T(8,128)}, f32[16,192]{1,0:T(8,128)}, f32[8,64,768]{2,1,0:T(8,128)}, f32[8,64,768]...) custom-call(s32[1]{0:T(128)} %bitcast.refs_0_.own_ref, s32[1]{0:T(128)} %dynamic_slice.96.refs_1_, ...), custom_call_target="tpu_custom_call" | custom-call | flops 40249999360 | bytes 126000000 | tf_op jit(solution)/shard_map/mixer_backward/pallas_call | solution.py:373
  367.7 10.0 %input_weight_grad.1 = f32[3,192,768]{2,1,0:T(8,128)} custom-call(bf16[4,512,768]{2,1,0:T(8,128)(2,1)} %get-tuple-element.281.nh_ref, bf16[4,512,768]{2,1,0:T(8,128)(2,1)} %get-tuple-element.282.nl_ref, f32[4,3,512,192]{3,2,1,0:T(8,128)} %get-tuple-element.298.gp_ref), custom_call_target="tpu_custom_call" | custom-call | flops 13799999488 | bytes 43200000 | tf_op jit(solution)/shard_map/input_weight_grad/pallas_call | solution.py:373
  377.6 7.6 %collective-permute-done.42 = f32[96,768]{1,0:T(8,128)S(1)} collective-permute-done((f32[96,768]{1,0:T(8,128)S(1)}, f32[96,768]{1,0:T(8,128)S(1)}, u32[]{:S(2)}, u32[]{:S(2)}) %collective-permute-start.42) | collective-permute-done | bytes 294944 | tf_op jit(solution)/shard_map/ppermute | solution.py:971
  393.6 12.6 %filter_backward.1 = f32[8,256,192]{2,1,0:T(8,128)} custom-call(f32[8,512,192]{2,1,0:T(8,128)} %get-tuple-element.309.s_ref, f32[8,512,192]{2,1,0:T(8,128)} %get-tuple-element.310.g_ref, bf16[256,512]{1,0:T(8,128)(2,1)} %constant.204.clone.refs_16_.ih_ref, bf16[256,512]{1,0:T(8,128)(2,1)} %constant.205.clone.refs_17_.il_ref), custom_call_target="tpu_custom_call" | custom-call | flops 14949999616 | bytes 46800000 | tf_op jit(solution)/shard_map/filter_backward/pallas_call | solution.py:373
  451.0 26.6 %collective-permute-done.51 = f32[96,768]{1,0:T(8,128)S(1)} collective-permute-done((f32[96,768]{1,0:T(8,128)S(1)}, f32[96,768]{1,0:T(8,128)S(1)}, u32[]{:S(2)}, u32[]{:S(2)}) %collective-permute-start.51) | collective-permute-done | bytes 294944 | tf_op jit(solution)/shard_map/ppermute | solution.py:971
  477.5 10.2 %collective-permute-done.50 = f32[192,768]{1,0:T(8,128)S(1)} collective-permute-done((f32[192,768]{1,0:T(8,128)S(1)}, f32[192,768]{1,0:T(8,128)S(1)}, u32[]{:S(2)}, u32[]{:S(2)}) %collective-permute-start.50) | collective-permute-done | bytes 589856 | tf_op jit(solution)/shard_map/ppermute | solution.py:971
  500.7 11.3 %collective-permute-done.55 = f32[96,768]{1,0:T(8,128)S(1)} collective-permute-done((f32[96,768]{1,0:T(8,128)S(1)}, f32[96,768]{1,0:T(8,128)S(1)}, u32[]{:S(2)}, u32[]{:S(2)}) %collective-permute-start.55) | collective-permute-done | bytes 294944 | tf_op jit(solution)/shard_map/ppermute | solution.py:971
  515.5 7.8 %put_together.2 = f32[8,256,768]{2,1,0:T(8,128)} custom-call(s32[1]{0:T(128)} %bitcast.refs_0_.own_ref, f32[8,64,768]{2,1,0:T(8,128)} %all-to-all-done.2.refs_0_, f32[8,64,768]{2,1,0:T(8,128)} %collective-permute-done.54.refs_1_, f32[8,64,768]{2,1,0:T(8,128)} %collective-permute-done.53.refs_2_, f32[8,64,768]{2,1,0:T(8,128)} %collective-permute-done.57.refs_3_), custom_call_target="tpu_custom_call" | custom-call | flops 9200000000 | bytes 28800000 | tf_op jit(solution)/shard_map/put_together/pallas_call | solution.py:373
  543.0 7.1 %collective-permute-done.61 = f32[192,768]{1,0:T(8,128)} collective-permute-done((f32[192,768]{1,0:T(8,128)}, f32[192,768]{1,0:T(8,128)}, u32[]{:S(2)}, u32[]{:S(2)}) %collective-permute-start.61) | collective-permute-done | bytes 589856 | tf_op jit(solution)/shard_map/ppermute | solution.py:971
  550.2 9.8 %collective-permute-done.65 = f32[384,768]{1,0:T(8,128)} collective-permute-done((f32[384,768]{1,0:T(8,128)}, f32[384,768]{1,0:T(8,128)}, u32[]{:S(2)}, u32[]{:S(2)}) %collective-permute-start.65) | collective-permute-done | bytes 1179680 | tf_op jit(solution)/shard_map/ppermute | solution.py:971
  566.2 7.9 %put_together.3 = f32[8,256,768]{2,1,0:T(8,128)} custom-call(s32[1]{0:T(128)} %bitcast.refs_0_.own_ref, f32[8,64,768]{2,1,0:T(8,128)} %all-to-all-done.3.refs_0_, f32[8,64,768]{2,1,0:T(8,128)} %collective-permute-done.62.refs_1_, f32[8,64,768]{2,1,0:T(8,128)} %collective-permute-done.59.refs_2_, f32[8,64,768]{2,1,0:T(8,128)} %collective-permute-done.63.refs_3_), custom_call_target="tpu_custom_call" | custom-call | flops 9200000000 | bytes 28800000 | tf_op jit(solution)/shard_map/put_together/pallas_call | solution.py:373
  (450 shorter events, 242.5 us)
Async XLA Ops:
  0.7 37.2 %collective-permute-start.1 = (f32[768]{0:T(1024)}, f32[768]{0:T(1024)S(1)}, u32[]{:S(2)}, u32[]{:S(2)}) collective-permute-start(f32[768]{0:T(1024)} %param.48), channel_id=1, source_target_pairs={{0,1},{1,0},{2,3},{3,2},{4,5},{5,4},{6,7},{7,6},{8,9},{9,8},{10,11... | collective-permute-start | bytes 9224 | tf_op jit(solution)/shard_map/ppermute | solution.py:971
  1.2 36.7 %collective-permute-start.2 = (f32[768]{0:T(1024)}, f32[768]{0:T(1024)S(1)}, u32[]{:S(2)}, u32[]{:S(2)}) collective-permute-start(f32[768]{0:T(1024)} %param.48), channel_id=1, source_target_pairs={{0,2},{1,3},{2,0},{3,1},{4,6},{5,7},{6,4},{7,5},{8,10},{9,11},{10,... | collective-permute-start | bytes 9224 | tf_op jit(solution)/shard_map/ppermute | solution.py:971
  10.6 43.2 %all-to-all-start = ((f32[8,64,768]{2,1,0:T(8,128)}), f32[8,64,768]{2,1,0:T(8,128)S(1)}, u32[]{:S(2)}, u32[]{:S(2)}) async-start(f32[8,64,768]{2,1,0:T(8,128)} %constant_dynamic-slice_fusion.15), calls=%async_computation | async-start | bytes 3145728 | tf_op jit(solution)/shard_map/all_to_all | solution.py:1000
  57.0 41.1 %all-to-all-start.1 = ((f32[8,64,768]{2,1,0:T(8,128)}), f32[8,64,768]{2,1,0:T(8,128)S(1)}, u32[]{:S(2)}, u32[]{:S(2)}) async-start(f32[8,64,768]{2,1,0:T(8,128)} %constant_dynamic-slice_fusion.13), calls=%async_computation.1 | async-start | bytes 3145728 | tf_op jit(solution)/shard_map/all_to_all | solution.py:1000
  61.0 37.2 %collective-permute-start.4 = (f32[8,64,768]{2,1,0:T(8,128)S(1)}, f32[8,64,768]{2,1,0:T(8,128)}, u32[]{:S(2)}, u32[]{:S(2)}) collective-permute-start(f32[8,64,768]{2,1,0:T(8,128)S(1)} %all-to-all-done.refs_2_), channel_id=1, source_target_pairs={{0,1},{1,0},{2,3},{3,2},{4,5},{5,4},{6,7},{7,6},{8,9},{9,8},{10,11... | collective-permute-start | bytes 4718600 | tf_op jit(solution)/shard_map/ppermute | solution.py:971
  93.3 41.3 %collective-permute-start.7 = (f32[768,384]{1,0:T(8,128)}, f32[768,384]{1,0:T(8,128)}, u32[]{:S(2)}, u32[]{:S(2)}) collective-permute-start(f32[768,384]{1,0:T(8,128)} %constant_dynamic-slice_fusion.12), channel_id=1, source_target_pairs={{0,2},{1,3},{2,0},{3,1},{4,6},{5,7},{6,4},{7,5},{8,10},{9,11},{10,... | collective-permute-start | bytes 3538952 | tf_op jit(solution)/shard_map/ppermute | solution.py:971
  93.8 40.8 %collective-permute-start.9 = (f32[384,768]{1,0:T(8,128)}, f32[384,768]{1,0:T(8,128)}, u32[]{:S(2)}, u32[]{:S(2)}) collective-permute-start(f32[384,768]{1,0:T(8,128)} %collective-permute-done.refs_7_), channel_id=1, source_target_pairs={{0,4},{4,0},{8,12},{12,8},{16,20},{20,16},{24,28},{28,24},{1,5},{5... | collective-permute-start | bytes 3538952 | tf_op jit(solution)/shard_map/ppermute | solution.py:971
  95.4 39.2 %collective-permute-start.8 = (f32[192,768]{1,0:T(8,128)}, f32[192,768]{1,0:T(8,128)}, u32[]{:S(2)}, u32[]{:S(2)}) collective-permute-start(f32[192,768]{1,0:T(8,128)} %refs_8_.3), channel_id=1, source_target_pairs={{0,2},{1,3},{2,0},{3,1},{4,6},{5,7},{6,4},{7,5},{8,10},{9,11},{10,... | collective-permute-start | bytes 1769480 | tf_op jit(solution)/shard_map/ppermute | solution.py:971
  248.0 39.7 %collective-permute-start.30 = (f32[256,768]{1,0:T(8,128)S(1)}, f32[256,768]{1,0:T(8,128)}, u32[]{:S(2)}, u32[]{:S(2)}) collective-permute-start(f32[256,768]{1,0:T(8,128)S(1)} %get-tuple-element.373), channel_id=1, source_target_pairs={{0,2},{1,3},{2,0},{3,1},{4,6},{5,7},{6,4},{7,5},{8,10},{9,11},{10,... | collective-permute-start | bytes 2359304 | tf_op jit(solution)/shard_map/ppermute | solution.py:971
  271.5 45.2 %collective-permute-start.35 = (f32[384,768]{1,0:T(8,128)}, f32[384,768]{1,0:T(8,128)}, u32[]{:S(2)}, u32[]{:S(2)}) collective-permute-start(f32[384,768]{1,0:T(8,128)} %dynamic-slice_add_fusion.1), channel_id=1, source_target_pairs={{0,4},{4,0},{8,12},{12,8},{16,20},{20,16},{24,28},{28,24},{1,5},{5... | collective-permute-start | bytes 3538952 | tf_op jit(solution)/shard_map/ppermute | solution.py:971
  288.5 67.6 %collective-permute-start.39 = (f32[96,768]{1,0:T(8,128)}, f32[96,768]{1,0:T(8,128)S(1)}, u32[]{:S(2)}, u32[]{:S(2)}) collective-permute-start(f32[96,768]{1,0:T(8,128)} %constant_dynamic-slice_fusion.5), channel_id=1, source_target_pairs={{0,16},{4,20},{8,24},{12,28},{16,0},{20,4},{24,8},{28,12},{1,17},{... | collective-permute-start | bytes 884744 | tf_op jit(solution)/shard_map/ppermute | solution.py:971
  293.0 64.9 %all-to-all-start.2 = ((f32[8,64,768]{2,1,0:T(8,128)}), f32[8,64,768]{2,1,0:T(8,128)}, u32[]{:S(2)}, u32[]{:S(2)}) async-start(f32[8,64,768]{2,1,0:T(8,128)} %bitcast.15), calls=%async_computation.2 | async-start | bytes 3145728 | tf_op jit(solution)/shard_map/all_to_all | solution.py:1000
  318.7 37.5 %collective-permute-start.37 = (f32[192,768]{1,0:T(8,128)S(1)}, f32[192,768]{1,0:T(8,128)S(1)}, u32[]{:S(2)}, u32[]{:S(2)}) collective-permute-start(f32[192,768]{1,0:T(8,128)S(1)} %constant_dynamic-slice_fusion.7), channel_id=1, source_target_pairs={{0,8},{4,12},{8,0},{12,4},{16,24},{20,28},{24,16},{28,20},{1,9},{5... | collective-permute-start | bytes 1769480 | tf_op jit(solution)/shard_map/ppermute | solution.py:971
  321.0 37.0 %collective-permute-start.36 = (f32[2,192,768]{2,1,0:T(8,128)S(1)}, f32[2,192,768]{2,1,0:T(8,128)}, u32[]{:S(2)}, u32[]{:S(2)}) collective-permute-start(f32[2,192,768]{2,1,0:T(8,128)S(1)} %copy-done.82), channel_id=1, source_target_pairs={{0,2},{1,3},{2,0},{3,1},{4,6},{5,7},{6,4},{7,5},{8,10},{9,11},{10,... | collective-permute-start | bytes 3538952 | tf_op jit(solution)/shard_map/ppermute | solution.py:971
  361.0 56.5 %collective-permute-start.45 = (f32[8,64,768]{2,1,0:T(8,128)}, f32[8,64,768]{2,1,0:T(8,128)}, u32[]{:S(2)}, u32[]{:S(2)}) collective-permute-start(f32[8,64,768]{2,1,0:T(8,128)} %get-tuple-element.307), channel_id=1, source_target_pairs={{0,1},{1,0},{2,3},{3,2},{4,5},{5,4},{6,7},{7,6},{8,9},{9,8},{10,11... | collective-permute-start | bytes 4718600 | tf_op jit(solution)/shard_map/ppermute | solution.py:971
  366.2 51.4 %collective-permute-start.46 = (f32[8,64,768]{2,1,0:T(8,128)S(1)}, f32[8,64,768]{2,1,0:T(8,128)S(1)}, u32[]{:S(2)}, u32[]{:S(2)}) collective-permute-start(f32[8,64,768]{2,1,0:T(8,128)S(1)} %add.236), channel_id=1, source_target_pairs={{0,2},{1,3},{2,0},{3,1},{4,6},{5,7},{6,4},{7,5},{8,10},{9,11},{10,... | collective-permute-start | bytes 4718600 | tf_op jit(solution)/shard_map/ppermute | solution.py:971
  424.2 64.3 %all-to-all-start.3 = ((f32[8,64,768]{2,1,0:T(8,128)}), f32[8,64,768]{2,1,0:T(8,128)}, u32[]{:S(2)}, u32[]{:S(2)}) async-start(f32[8,64,768]{2,1,0:T(8,128)} %bitcast.54), calls=%async_computation.3 | async-start | bytes 3145728 | tf_op jit(solution)/shard_map/all_to_all | solution.py:1000
  429.7 58.8 %collective-permute-start.53 = (f32[8,64,768]{2,1,0:T(8,128)}, f32[8,64,768]{2,1,0:T(8,128)}, u32[]{:S(2)}, u32[]{:S(2)}) collective-permute-start(f32[8,64,768]{2,1,0:T(8,128)} %all-to-all-done.2.refs_0_), channel_id=1, source_target_pairs={{0,2},{1,3},{2,0},{3,1},{4,6},{5,7},{6,4},{7,5},{8,10},{9,11},{10,... | collective-permute-start | bytes 4718600 | tf_op jit(solution)/shard_map/ppermute | solution.py:971
  431.2 57.3 %collective-permute-start.54 = (f32[8,64,768]{2,1,0:T(8,128)}, f32[8,64,768]{2,1,0:T(8,128)}, u32[]{:S(2)}, u32[]{:S(2)}) collective-permute-start(f32[8,64,768]{2,1,0:T(8,128)} %all-to-all-done.2.refs_0_), channel_id=1, source_target_pairs={{0,1},{1,0},{2,3},{3,2},{4,5},{5,4},{6,7},{7,6},{8,9},{9,8},{10,11... | collective-permute-start | bytes 4718600 | tf_op jit(solution)/shard_map/ppermute | solution.py:971
  432.3 45.2 %collective-permute-start.52 = (f32[192,768]{1,0:T(8,128)}, f32[192,768]{1,0:T(8,128)}, u32[]{:S(2)}, u32[]{:S(2)}) collective-permute-start(f32[192,768]{1,0:T(8,128)} %pad_maximum_fusion.6), channel_id=1, source_target_pairs={{0,8},{4,12},{8,0},{12,4},{16,24},{20,28},{24,16},{28,20},{1,9},{5... | collective-permute-start | bytes 1769480 | tf_op jit(solution)/shard_map/ppermute | solution.py:971
  437.3 40.2 %collective-permute-start.51 = (f32[96,768]{1,0:T(8,128)S(1)}, f32[96,768]{1,0:T(8,128)S(1)}, u32[]{:S(2)}, u32[]{:S(2)}) collective-permute-start(f32[96,768]{1,0:T(8,128)S(1)} %dynamic-slice_add_fusion.7), channel_id=1, source_target_pairs={{0,16},{4,20},{8,24},{12,28},{16,0},{20,4},{24,8},{28,12},{1,17},{... | collective-permute-start | bytes 884744 | tf_op jit(solution)/shard_map/ppermute | solution.py:971
  441.4 46.3 %collective-permute-start.50 = (f32[192,768]{1,0:T(8,128)S(1)}, f32[192,768]{1,0:T(8,128)S(1)}, u32[]{:S(2)}, u32[]{:S(2)}) collective-permute-start(f32[192,768]{1,0:T(8,128)S(1)} %constant_dynamic-slice_fusion.1), channel_id=1, source_target_pairs={{0,8},{4,12},{8,0},{12,4},{16,24},{20,28},{24,16},{28,20},{1,9},{5... | collective-permute-start | bytes 1769480 | tf_op jit(solution)/shard_map/ppermute | solution.py:971
  492.7 37.2 %collective-permute-start.59 = (f32[8,64,768]{2,1,0:T(8,128)}, f32[8,64,768]{2,1,0:T(8,128)}, u32[]{:S(2)}, u32[]{:S(2)}) collective-permute-start(f32[8,64,768]{2,1,0:T(8,128)} %all-to-all-done.3.refs_0_), channel_id=1, source_target_pairs={{0,2},{1,3},{2,0},{3,1},{4,6},{5,7},{6,4},{7,5},{8,10},{9,11},{10,... | collective-permute-start | bytes 4718600 | tf_op jit(solution)/shard_map/ppermute | solution.py:971
  499.2 39.5 %collective-permute-start.66 = (f32[384,768]{1,0:T(8,128)}, f32[384,768]{1,0:T(8,128)}, u32[]{:S(2)}, u32[]{:S(2)}) collective-permute-start(f32[384,768]{1,0:T(8,128)} %pad_maximum_fusion.4), channel_id=1, source_target_pairs={{0,4},{4,0},{8,12},{12,8},{16,20},{20,16},{24,28},{28,24},{1,5},{5... | collective-permute-start | bytes 3538952 | tf_op jit(solution)/shard_map/ppermute | solution.py:971
  (144 other events, 2034.9 us)

commit v3 on v2

--- a/solution.py
+++ b/solution.py
@@ -353,6 +353,16 @@
     return scale * (lifted - mean_one - unit * mean_two)
 
 
+def fold(rows):
+    half = rows.shape[0] // 2
+    return jnp.concatenate([rows[:half], rows[half:]], 1)
+
+
+def unfold(folded):
+    width = folded.shape[1] // 2
+    return jnp.concatenate([folded[:, :width], folded[:, width:]], 0)
+
+
 def column_sum(values):
     return jnp.sum(values, 0, keepdims=True)
 
@@ -506,13 +516,14 @@
         for u in range(pair):
             for k in range(count):
                 start = pl.multiple_of(u * block + (me ^ k) * quarter, quarter)
-                m_refs[k][u] = mixed_ref[pl.ds(start, quarter), :]
+                m_refs[k][u] = fold(mixed_ref[pl.ds(start, quarter), :])
 
     by_block = lambda *shape: pl.BlockSpec((1,) + shape, lambda b: (b,) + (0,) * len(shape))
     args = [own, length, *x_parts, gain, offset, weight, bias, conv_w, conv_b, skip, spectrum, *tables]
     by_pair = lambda n: pl.BlockSpec((pair, quarter, n), lambda b: (b, 0, 0))
     in_specs = [scalar_spec(), scalar_spec()] + [by_pair(model)] * count
     in_specs += [whole(a) for a in args[2 + count :]]
+    folded = pl.BlockSpec((pair, quarter // 2, 2 * width), lambda b: (b, 0, 0))
     s_shape = struct((blocks, 2 * block, width))
     outs = run_kernel(
         body,
@@ -521,10 +532,10 @@
         in_specs,
         [by_block(span, model)] * 2
         + [by_block(3, span, width), by_block(span, width), whole(s_shape)]
-        + [by_pair(width)] * count,
+        + [folded] * count,
         [struct((blocks // pair, span, model), BF16)] * 2
         + [struct((blocks // pair, 3, span, width)), struct((blocks // pair, span, width)), s_shape]
-        + [struct((blocks, quarter, width))] * count,
+        + [struct((blocks, quarter // 2, 2 * width))] * count,
         [
             pltpu.VMEM((3, model, width), BF16),
             pltpu.VMEM((3, model, width), BF16),
@@ -539,10 +550,12 @@
 
 
 def hidden_forward(m_parts, weights, x_own, cotangent, bias, gain, offset):
-    rows, width = m_parts[0].shape
-    model = x_own.shape[1]
+    blocks, half, width = m_parts[0].shape
+    rows, model = x_own.shape
+    width = width // 2
     count = len(m_parts)
-    step = min(128, rows)
+    group = math.gcd(blocks, max(128 // half, 1))
+    step = 2 * half * group
 
     def body(*refs):
         m_refs, w_refs = refs[:count], refs[count : 2 * count]
@@ -557,7 +570,8 @@
 
         hidden = x_ref[...] + bias_ref[...]
         for k in range(count):
-            hidden = hidden + dot_parts(parts_of(m_refs[k][...]), (wh_ref[k], wl_ref[k]), NN)
+            mixed = jnp.concatenate([unfold(m_refs[k][u]) for u in range(group)], 0)
+            hidden = hidden + dot_parts(parts_of(mixed), (wh_ref[k], wl_ref[k]), NN)
         h_ref[...] = hidden
         normed = normalise(hidden)[0] * gain_ref[...] + offset_ref[...]
         nh_ref[...], nl_ref[...] = parts_of(normed)
@@ -571,7 +585,7 @@
         body,
         "hidden_forward",
         (rows // step,),
-        [row_spec(width)] * count
+        [pl.BlockSpec((group, half, 2 * width), lambda r: (r, 0, 0))] * count
         + [whole(w) for w in weights]
         + [row_spec(model)] * 2
         + [whole(bias), whole(gain), whole(offset)],
@@ -659,9 +673,11 @@
 
 def hidden_backward(hidden, feed, grad_normed, cotangent, m_parts, weights, gain, bias):
     rows, model = hidden.shape
-    width = m_parts[0].shape[1]
+    blocks, half, width = m_parts[0].shape
+    width = width // 2
     count = len(m_parts)
-    step = min(128, rows)
+    group = math.gcd(blocks, max(128 // half, 1))
+    step = 2 * half * group
 
     def body(*refs):
         h_ref, f_ref, g_ref, c_ref = refs[:4]
@@ -689,9 +705,13 @@
         sum_ref[3:4] += column_sum(above)
         parts = parts_of(grad_hidden)
         for k in range(count):
-            gm_refs[k][...] = dot_parts(parts, (wh_ref[k], wl_ref[k]), NT)
-            gw_refs[k // 2][k % 2] += dot_parts(parts_of(m_refs[k][...]), parts, TN)
-
+            grad_mixed = dot_parts(parts, (wh_ref[k], wl_ref[k]), NT)
+            for u in range(group):
+                gm_refs[k][u] = fold(grad_mixed[u * 2 * half : (u + 1) * 2 * half])
+            mixed = jnp.concatenate([unfold(m_refs[k][u]) for u in range(group)], 0)
+            gw_refs[k // 2][k % 2] += dot_parts(parts_of(mixed), parts, TN)
+
+    folded = pl.BlockSpec((group, half, 2 * width), lambda r: (r, 0, 0))
     row_spec = lambda n: pl.BlockSpec((step, n), lambda r: (r, 0))
     args = [hidden, feed, grad_normed, cotangent, *m_parts, *weights, gain, bias]
     sums, pair = struct((8, model)), struct((2, width, model))
@@ -699,12 +719,12 @@
         body,
         "hidden_backward",
         (rows // step,),
-        [row_spec(model)] * 4 + [row_spec(width)] * count + [whole(w) for w in weights] + [whole(gain), whole(bias)],
+        [row_spec(model)] * 4 + [folded] * count + [whole(w) for w in weights] + [whole(gain), whole(bias)],
         [row_spec(model)] * 2
         + [whole(sums)]
-        + [row_spec(width)] * count
+        + [folded] * count
         + [whole(pair)] * 2,
-        [struct((rows, model))] * 2 + [sums] + [struct((rows, width))] * count + [pair] * 2,
+        [struct((rows, model))] * 2 + [sums] + [struct((blocks, half, 2 * width))] * count + [pair] * 2,
         [pltpu.VMEM((count, width, model), BF16)] * 2,
         args,
         15,
@@ -714,6 +734,7 @@
 
 def mixer_backward(own, length, gm_parts, proj, conv, s_spec, k_spec, conv_w, conv_b, skip, weight, tables):
     blocks, quarter, width = gm_parts[0].shape
+    quarter, width = 2 * quarter, width // 2
     count = len(gm_parts)
     block = quarter * count
     model = weight.shape[1]
@@ -744,7 +765,7 @@
         for u in range(pair):
             for k in range(count):
                 start = pl.multiple_of(u * block + (me ^ k) * quarter, quarter)
-                rows_ref[pl.ds(start, quarter), :] = gm_refs[k][u]
+                rows_ref[pl.ds(start, quarter), :] = unfold(gm_refs[k][u])
         inside = (slot > 0).astype(F32)
         short = []
         for k in range(3):
@@ -818,7 +839,7 @@
         "mixer_backward",
         (blocks // pair,),
         [scalar_spec(), scalar_spec()]
-        + [by_pair(width)] * count
+        + [pl.BlockSpec((pair, quarter // 2, 2 * width), lambda s: (last - s, 0, 0))] * count
         + [by_block(3, span, width), rim, by_block(span, width)]
         + [whole(a) for a in fixed],
         [whole(spectra), by_block(3, span, width), whole(sums)] + [by_pair(model)] * count,
@@ -912,7 +933,7 @@
 def input_backward(grad_pieces, x_own, grad_hidden, gain):
     rows, model = x_own.shape
     count = len(grad_pieces)
-    step = min(128, rows)
+    step = min(256, rows)
 
     def body(*refs):
         piece_refs = refs[:count]
@@ -946,17 +967,19 @@
 def put_together(own, pieces):
     groups, quarter, model = pieces[0].shape
     count = len(pieces)
+    pair = 2 - groups % 2
 
     def body(own_ref, *refs):
-        for k in range(count):
-            start = pl.multiple_of((own_ref[0] ^ k) * quarter, quarter)
-            refs[count][0, pl.ds(start, quarter), :] = refs[k][0]
-
-    by_group = lambda n: pl.BlockSpec((1, n, model), lambda s: (s, 0, 0))
+        for u in range(pair):
+            for k in range(count):
+                start = pl.multiple_of((own_ref[0] ^ k) * quarter, quarter)
+                refs[count][u, pl.ds(start, quarter), :] = refs[k][u]
+
+    by_group = lambda n: pl.BlockSpec((pair, n, model), lambda s: (s, 0, 0))
     return run_kernel(
         body,
         "put_together",
-        (groups,),
+        (groups // pair,),
         [scalar_spec()] + [by_group(quarter)] * count,
         [by_group(quarter * count)],
         [struct((groups, quarter * count, model))],
@@ -1110,14 +1133,15 @@
     out_parts = [output_weight, swap(output_weight, "chan", 1), out_far, out_3]
     up_parts = [[up_weight], [swap(up_weight, "chan", 1)], [up_far, up_other]]
     up_parts.append([swap(u, "chan", 1) for u in up_parts[2]])
-    down_parts = [[down_weight], [swap(down_weight, "chan", 1)], [down_far, down_other]]
-    down_parts.append([swap(d, "chan", 1) for d in down_parts[2]])
-    mixed = [m.reshape(rows, width) for m in mixed]
+    down_side = swap(down_far, "chan", 1)
 
     hidden, *rest = hidden_forward(
         mixed, out_parts, x_rows, cot_own, row(output_bias), row(ln2_gain), row(ln2_bias)
     )
+    rest, down_other, down_side = meet(rest, down_other, down_side)
     normed2, turned, cot_parts = rest[0:2], rest[2:4], rest[4:6]
+    down_parts = [[down_weight], [swap(down_weight, "chan", 1)], [down_far, down_other]]
+    down_parts.append([down_side, swap(down_other, "chan", 1)])
 
     def units(k, sums):
         return feed_forward(
@@ -1128,24 +1152,24 @@
     sums, (up_3, down_3, bias_grads[3]) = units(3, None)
     up_3, down_3 = swap(up_3, "chan", 1), swap(down_3, "chan", 1)
     sums, (up_2, down_2, bias_grads[2]) = units(2, sums)
-    *sums, far_up, far_down = meet(*sums, up_2 + up_3, down_2 + down_3)
+    *sums, up_2, up_3, down_2, down_3 = meet(*sums, up_2, up_3, down_2, down_3)
 
     third = model // 3
-    half = far_down.shape[0] // 2
-    far_ups = [swap(far_up[:third], "chan", 2)]
-    leaving, staying = split_rows(far_down, "seq", 1)
-    came = [swap(leaving[: half // 2], "seq", 1)]
+    far_up = lambda i: up_2[i * third : (i + 1) * third] + up_3[i * third : (i + 1) * third]
+    leaving_2, staying_2 = split_rows(down_2, "seq", 1)
+    leaving_3, staying_3 = split_rows(down_3, "seq", 1)
+    half = leaving_2.shape[0] // 2
+    far_ups = [swap(far_up(0), "chan", 2)]
+    came = [swap(leaving_2[:half] + leaving_3[:half], "seq", 1)]
     sums, (up_1, down_1, bias_grads[1]) = units(1, sums)
     *sums, far_ups[0], came[0], up_1, down_1 = meet(*sums, far_ups[0], came[0], up_1, down_1)
     up_1, down_1 = swap(up_1, "chan", 1), swap(down_1, "chan", 1)
-    far_ups.append(swap(far_up[third : 2 * third], "chan", 2))
-    came.append(swap(leaving[half // 2 :], "seq", 1))
+    far_ups.append(swap(far_up(1), "chan", 2))
+    came.append(swap(leaving_2[half:] + leaving_3[half:], "seq", 1))
     sums, (up_0, down_0, bias_grads[0]) = units(0, sums)
-    *sums, far_ups[1], far_down, up_1, down_1 = meet(
-        *sums, far_ups[1], staying + jnp.concatenate(came, 0), up_1, down_1
-    )
-    far_ups.append(swap(far_up[2 * third :], "chan", 2))
-    leaving, far_staying = split_rows(far_down, "seq", 2)
+    *sums, far_ups[1], came[1], up_1, down_1 = meet(*sums, far_ups[1], came[1], up_1, down_1)
+    far_ups.append(swap(far_up(2), "chan", 2))
+    leaving, far_staying = split_rows(staying_2 + staying_3 + jnp.concatenate(came, 0), "seq", 2)
     far_came = swap(leaving, "seq", 2)
     leaving_0, staying_0 = split_rows(down_0, "seq", 1)
     leaving_1, staying_1 = split_rows(down_1, "seq", 1)
@@ -1157,15 +1181,16 @@
         grad_hidden, far_ups[2], far_came, grad_mixed, out_rows
     )
 
-    grad_mixed = [g.reshape(blocks, quarter, width) for g in grad_mixed]
     grad_mixed = [g if k == 0 else swap(g, "chan", k) for k, g in enumerate(grad_mixed)]
     leaving, far_staying = split_rows(far_staying + far_came, "seq", 4)
     far_came = swap(leaving, "seq", 4)
     out_blocks = transpose_blocks(out_rows.reshape(blocks, quarter, model))
     grad_up = up_0 + up_1 + jnp.concatenate(far_ups, 0)
-    grad_mixed, grad_up, out_far, near_came = meet(grad_mixed, grad_up, out_far, near_came)
-
     up_leaving, up_staying = split_rows(grad_up, "seq", 1)
+    grad_mixed, up_leaving, up_staying, out_far, near_came = meet(
+        grad_mixed, up_leaving, up_staying, out_far, near_came
+    )
+
     up_came = swap(up_leaving, "seq", 1)
     leaving, near_staying = split_rows(staying_0 + staying_1 + near_came, "seq", 2)
     near_came = swap(leaving, "seq", 2)

time: 609 us -> 589 us (0.967)
  Pallas kernels: 213 us -> 206 us
    pallas_call x14, Pallas kernels: 213 us -> 206 us  [run_kernel(): pl.pallas_call(body, name=name, grid=grid, in_specs=in_specs, out_specs=o...]
    unnamed x187 -> x189, local copies, waits for them, and re-layouts: 14.7 us -> 11.9 us
  transfers between devices with their start and end apart: 75 -> 75, of which waited for: 25 -> 28; matrix products, arithmetic and copies ran while one was open for 15% -> 15% of each run, Pallas kernels for 33% -> 32%
where the time goes in v3:
time: 589 us; the launch traced here: 582 us
  Pallas kernels  206 us (35%)
  waiting for transfers between devices  189 us (32%)
  starting transfers between devices  81.4 us (14%)
  local copies, waits for them, and re-layouts  44.9 us (8%)
  other arithmetic  39.8 us (7%)
  matrix products  19.1 us (3%)
    pallas_call x14, Pallas kernels, run_kernel(): pl.pallas_call(body, name=name, grid=grid, in_specs=in_specs, out_specs=o...  206 us
    ppermute x71, waiting for transfers between devices, swap(): return lax.ppermute(values, axis, [(i, i ^ bit) for i in range(size)])  172 us
    ppermute x71, starting transfers between devices, swap(): return lax.ppermute(values, axis, [(i, i ^ bit) for i in range(size)])  61.6 us
    all_to_all x4, starting transfers between devices, transpose_blocks(): lax.all_to_all(values, 'seq', split_axis=0, concat_axis=0, tiled=True)  19.8 us
    all_to_all x4, waiting for transfers between devices, transpose_blocks(): lax.all_to_all(values, 'seq', split_axis=0, concat_axis=0, tiled=True)  17.3 us
    unnamed x189, local copies, waits for them, and re-layouts  11.9 us
  transfers between devices with their start and end apart: 75, of which 28 were waited for; matrix products, arithmetic and copies ran while one was open for 15% of the time, Pallas kernels for 32%

profile of v3, /device:TPU:0, one launch (start us, length us, event | category | flops | bytes accessed | tf_op | source)
XLA Modules:
  0.0 582.1 jit_solution(5082150444089933451)
XLA Ops:
  28.3 7.7 %filter_spectrum.1.refs_13_.refs_9_ = f32[8,512,192]{2,1,0:T(8,128)} custom-call(f32[8,256,192]{2,1,0:T(8,128)} %bitcast.40, bf16[512,256]{1,0:T(8,128)(2,1)} %constant.206.clone.high_ref.refs_14_, bf16[512,256]{1,0:T(8,128)(2,1)} %constant.207.clone.low_ref.refs_15_), custom_call_target="tpu_custom_call" | custom-call | flops 9200000000 | bytes 28800000 | tf_op jit(solution)/shard_map/filter_spectrum/pallas_call | solution.py:383
  37.9 15.9 %all-to-all-done.refs_2_ = f32[8,64,768]{2,1,0:T(8,128)S(1)} async-done(((f32[8,64,768]{2,1,0:T(8,128)}), f32[8,64,768]{2,1,0:T(8,128)S(1)}, u32[]{:S(2)}, u32[]{:S(2)}) %all-to-all-start) | async-done | bytes 1572896 | tf_op jit(solution)/shard_map/all_to_all | solution.py:1023
  61.2 28.0 %collective-permute-done.5.refs_4_ = f32[8,64,768]{2,1,0:T(8,128)} collective-permute-done((f32[8,64,768]{2,1,0:T(8,128)S(1)}, f32[8,64,768]{2,1,0:T(8,128)}, u32[]{:S(2)}, u32[]{:S(2)}) %collective-permute-start.5) | collective-permute-done | bytes 1572896 | tf_op jit(solution)/shard_map/ppermute | solution.py:994
  98.3 33.1 %mixer_forward.1 = (bf16[4,512,768]{2,1,0:T(8,128)(2,1)}, bf16[4,512,768]{2,1,0:T(8,128)(2,1)}, f32[4,3,512,192]{3,2,1,0:T(8,128)}, f32[4,512,192]{2,1,0:T(8,128...) custom-call(s32[1]{0:T(128)} %bitcast.refs_0_.own_ref, ...), custom_call_target="tpu_custom_call" | custom-call | flops 41400000512 | bytes 129600000 | tf_op jit(solution)/shard_map/mixer_forward/pallas_call | solution.py:383
  138.6 8.2 %collective-permute-done.11.refs_2_.refs_6_ = f32[8,32,384]{2,1,0:T(8,128)S(1)} collective-permute-done((f32[8,32,384]{2,1,0:T(8,128)}, f32[8,32,384]{2,1,0:T(8,128)S(1)}, u32[]{:S(2)}, u32[]{:S(2)}) %collective-permute-start.11) | collective-permute-done | bytes 393248 | tf_op jit(solution)/shard_map/ppermute | solution.py:994
  155.9 8.6 %hidden_forward.1 = (f32[512,768]{1,0:T(8,128)}, bf16[512,768]{1,0:T(8,128)(2,1)}, bf16[512,768]{1,0:T(8,128)(2,1)}, bf16[768,512]{1,0:T(8,128)(2,1)}, bf16[768,...) custom-call(f32[8,32,384]{2,1,0:T(8,128)} %get-tuple-element.222.refs_0_.refs_4_, ...), custom_call_target="tpu_custom_call" | custom-call | flops 10350000128 | bytes 32400000 | tf_op jit(solution)/shard_map/hidden_forward/pallas_call | solution.py:383
  169.4 17.6 %feed_forward.4 = (f32[512,768]{1,0:T(8,128)}, f32[512,768]{1,0:T(8,128)}, f32[768,768]{1,0:T(8,128)}, f32[768,768]{1,0:T(8,128)}, f32[1,768]{1,0:T(1,128)}) custom-call(s32[1]{0:T(128)} %bitcast.6.side_ref, bf16[512,768]{1,0:T(8,128)(2,1)} %get-tuple-element.236.refs_0_, bf16[512,768]{1,0:T(8,128)(2,1)} %get-tuple-element.237.refs_1_, ...), custom_call_target="tpu_custom_call" | custom-call | flops 20700000256 | bytes 64800000 | tf_op jit(solution)/shard_map/feed_forward/pallas_call | solution.py:383
  189.3 18.1 %feed_forward.5 = (f32[512,768]{1,0:T(8,128)}, f32[512,768]{1,0:T(8,128)}, f32[768,768]{1,0:T(8,128)}, f32[768,768]{1,0:T(8,128)}, f32[1,768]{1,0:T(1,128)}) custom-call(s32[1]{0:T(128)} %bitcast.6.side_ref, bf16[512,768]{1,0:T(8,128)(2,1)} %get-tuple-element.236.refs_0_, bf16[512,768]{1,0:T(8,128)(2,1)} %get-tuple-element.237.refs_1_, ...), custom_call_target="tpu_custom_call" | custom-call | flops 20700000256 | bytes 64800000 | tf_op jit(solution)/shard_map/feed_forward/pallas_call | solution.py:383
  213.5 18.2 %feed_forward.6 = (f32[512,768]{1,0:T(8,128)}, f32[512,768]{1,0:T(8,128)}, f32[768,768]{1,0:T(8,128)}, f32[768,768]{1,0:T(8,128)}, f32[1,768]{1,0:T(1,128)}) custom-call(s32[1]{0:T(128)} %bitcast.6.side_ref, bf16[512,768]{1,0:T(8,128)(2,1)} %get-tuple-element.236.refs_0_, bf16[512,768]{1,0:T(8,128)(2,1)} %get-tuple-element.237.refs_1_, ...), custom_call_target="tpu_custom_call" | custom-call | flops 20700000256 | bytes 64800000 | tf_op jit(solution)/shard_map/feed_forward/pallas_call | solution.py:383
  237.3 18.1 %feed_forward.7 = (f32[512,768]{1,0:T(8,128)}, f32[512,768]{1,0:T(8,128)}, f32[768,768]{1,0:T(8,128)}, f32[768,768]{1,0:T(8,128)}, f32[1,768]{1,0:T(1,128)}) custom-call(s32[1]{0:T(128)} %bitcast.6.side_ref, bf16[512,768]{1,0:T(8,128)(2,1)} %get-tuple-element.236.refs_0_, bf16[512,768]{1,0:T(8,128)(2,1)} %get-tuple-element.237.refs_1_, ...), custom_call_target="tpu_custom_call" | custom-call | flops 20700000256 | bytes 64800000 | tf_op jit(solution)/shard_map/feed_forward/pallas_call | solution.py:383
  262.2 11.6 %hidden_backward.1 = (f32[512,768]{1,0:T(8,128)}, f32[512,768]{1,0:T(8,128)}, f32[8,768]{1,0:T(8,128)}, f32[8,32,384]{2,1,0:T(8,128)}, f32[8,32,384]{2,1,0:T(8,1...) custom-call(f32[512,768]{1,0:T(8,128)} %get-tuple-element.228.refs_0_, ...), custom_call_target="tpu_custom_call" | custom-call | flops 17250000896 | bytes 54000000 | tf_op jit(solution)/shard_map/hidden_backward/pallas_call | solution.py:383
  289.5 7.7 %collective-permute-done.34.refs_5_ = f32[8,32,384]{2,1,0:T(8,128)} collective-permute-done((f32[8,32,384]{2,1,0:T(8,128)}, f32[8,32,384]{2,1,0:T(8,128)}, u32[]{:S(2)}, u32[]{:S(2)}) %collective-permute-start.34) | collective-permute-done | bytes 393248 | tf_op jit(solution)/shard_map/ppermute | solution.py:994
  301.7 33.7 %mixer_backward.1 = (f32[8,512,192]{2,1,0:T(8,128)}, f32[4,3,512,192]{3,2,1,0:T(8,128)}, f32[16,192]{1,0:T(8,128)}, f32[8,64,768]{2,1,0:T(8,128)}, f32[8,64,768]...) custom-call(s32[1]{0:T(128)} %bitcast.refs_0_.own_ref, s32[1]{0:T(128)} %dynamic_slice.102.refs_1_, ...), custom_call_target="tpu_custom_call" | custom-call | flops 40249999360 | bytes 126000000 | tf_op jit(solution)/shard_map/mixer_backward/pallas_call | solution.py:383
  349.9 10.0 %input_weight_grad.1 = f32[3,192,768]{2,1,0:T(8,128)} custom-call(bf16[4,512,768]{2,1,0:T(8,128)(2,1)} %get-tuple-element.302.nh_ref, bf16[4,512,768]{2,1,0:T(8,128)(2,1)} %get-tuple-element.303.nl_ref, f32[4,3,512,192]{3,2,1,0:T(8,128)} %get-tuple-element.320.gp_ref), custom_call_target="tpu_custom_call" | custom-call | flops 13799999488 | bytes 43200000 | tf_op jit(solution)/shard_map/input_weight_grad/pallas_call | solution.py:383
  359.9 7.5 %collective-permute-done.42 = f32[96,768]{1,0:T(8,128)S(1)} collective-permute-done((f32[96,768]{1,0:T(8,128)S(1)}, f32[96,768]{1,0:T(8,128)S(1)}, u32[]{:S(2)}, u32[]{:S(2)}) %collective-permute-start.42) | collective-permute-done | bytes 294944 | tf_op jit(solution)/shard_map/ppermute | solution.py:994
  374.1 12.7 %filter_backward.1 = f32[8,256,192]{2,1,0:T(8,128)} custom-call(f32[8,512,192]{2,1,0:T(8,128)} %get-tuple-element.331.s_ref, f32[8,512,192]{2,1,0:T(8,128)} %get-tuple-element.332.g_ref, bf16[256,512]{1,0:T(8,128)(2,1)} %constant.208.clone.refs_16_.ih_ref, bf16[256,512]{1,0:T(8,128)(2,1)} %constant.209.clone.refs_17_.il_ref), custom_call_target="tpu_custom_call" | custom-call | flops 14949999616 | bytes 46800000 | tf_op jit(solution)/shard_map/filter_backward/pallas_call | solution.py:383
  386.7 7.4 %collective-permute-done.48 = f32[96,768]{1,0:T(8,128)S(1)} collective-permute-done((f32[96,768]{1,0:T(8,128)S(1)}, f32[96,768]{1,0:T(8,128)S(1)}, u32[]{:S(2)}, u32[]{:S(2)}) %collective-permute-start.48) | collective-permute-done | bytes 294944 | tf_op jit(solution)/shard_map/ppermute | solution.py:994
  431.7 26.0 %collective-permute-done.51 = f32[96,768]{1,0:T(8,128)S(1)} collective-permute-done((f32[96,768]{1,0:T(8,128)S(1)}, f32[96,768]{1,0:T(8,128)S(1)}, u32[]{:S(2)}, u32[]{:S(2)}) %collective-permute-start.51) | collective-permute-done | bytes 294944 | tf_op jit(solution)/shard_map/ppermute | solution.py:994
  458.2 10.1 %collective-permute-done.50 = f32[192,768]{1,0:T(8,128)S(1)} collective-permute-done((f32[192,768]{1,0:T(8,128)S(1)}, f32[192,768]{1,0:T(8,128)S(1)}, u32[]{:S(2)}, u32[]{:S(2)}) %collective-permute-start.50) | collective-permute-done | bytes 589856 | tf_op jit(solution)/shard_map/ppermute | solution.py:994
  480.9 11.5 %collective-permute-done.55 = f32[96,768]{1,0:T(8,128)S(1)} collective-permute-done((f32[96,768]{1,0:T(8,128)S(1)}, f32[96,768]{1,0:T(8,128)S(1)}, u32[]{:S(2)}, u32[]{:S(2)}) %collective-permute-start.55) | collective-permute-done | bytes 294944 | tf_op jit(solution)/shard_map/ppermute | solution.py:994
  501.7 8.8 %collective-permute-done.59.refs_2_ = f32[8,64,768]{2,1,0:T(8,128)} collective-permute-done((f32[8,64,768]{2,1,0:T(8,128)}, f32[8,64,768]{2,1,0:T(8,128)}, u32[]{:S(2)}, u32[]{:S(2)}) %collective-permute-start.59) | collective-permute-done | bytes 1572896 | tf_op jit(solution)/shard_map/ppermute | solution.py:994
  523.7 7.1 %collective-permute-done.61 = f32[192,768]{1,0:T(8,128)} collective-permute-done((f32[192,768]{1,0:T(8,128)}, f32[192,768]{1,0:T(8,128)}, u32[]{:S(2)}, u32[]{:S(2)}) %collective-permute-start.61) | collective-permute-done | bytes 589856 | tf_op jit(solution)/shard_map/ppermute | solution.py:994
  530.8 9.9 %collective-permute-done.65 = f32[384,768]{1,0:T(8,128)} collective-permute-done((f32[384,768]{1,0:T(8,128)}, f32[384,768]{1,0:T(8,128)}, u32[]{:S(2)}, u32[]{:S(2)}) %collective-permute-start.65) | collective-permute-done | bytes 1179680 | tf_op jit(solution)/shard_map/ppermute | solution.py:994
  564.0 9.0 %collective-permute-done.69 = f32[30720]{0:T(1024)S(1)} collective-permute-done((f32[30720]{0:T(1024)S(1)}, f32[30720]{0:T(1024)S(1)}, u32[]{:S(2)}, u32[]{:S(2)}) %collective-permute-start.69) | collective-permute-done | bytes 122912 | tf_op jit(solution)/shard_map/ppermute | solution.py:994
  (450 shorter events, 233.7 us)
Async XLA Ops:
  0.7 37.2 %collective-permute-start.1 = (f32[768]{0:T(1024)}, f32[768]{0:T(1024)S(1)}, u32[]{:S(2)}, u32[]{:S(2)}) collective-permute-start(f32[768]{0:T(1024)} %param.48), channel_id=1, source_target_pairs={{0,1},{1,0},{2,3},{3,2},{4,5},{5,4},{6,7},{7,6},{8,9},{9,8},{10,11... | collective-permute-start | bytes 9224 | tf_op jit(solution)/shard_map/ppermute | solution.py:994
  1.2 36.7 %collective-permute-start.2 = (f32[768]{0:T(1024)}, f32[768]{0:T(1024)S(1)}, u32[]{:S(2)}, u32[]{:S(2)}) collective-permute-start(f32[768]{0:T(1024)} %param.48), channel_id=1, source_target_pairs={{0,2},{1,3},{2,0},{3,1},{4,6},{5,7},{6,4},{7,5},{8,10},{9,11},{10,... | collective-permute-start | bytes 9224 | tf_op jit(solution)/shard_map/ppermute | solution.py:994
  10.6 43.2 %all-to-all-start = ((f32[8,64,768]{2,1,0:T(8,128)}), f32[8,64,768]{2,1,0:T(8,128)S(1)}, u32[]{:S(2)}, u32[]{:S(2)}) async-start(f32[8,64,768]{2,1,0:T(8,128)} %constant_dynamic-slice_fusion.14), calls=%async_computation | async-start | bytes 3145728 | tf_op jit(solution)/shard_map/all_to_all | solution.py:1023
  57.0 41.3 %all-to-all-start.1 = ((f32[8,64,768]{2,1,0:T(8,128)}), f32[8,64,768]{2,1,0:T(8,128)S(1)}, u32[]{:S(2)}, u32[]{:S(2)}) async-start(f32[8,64,768]{2,1,0:T(8,128)} %constant_dynamic-slice_fusion.12), calls=%async_computation.1 | async-start | bytes 3145728 | tf_op jit(solution)/shard_map/all_to_all | solution.py:1023
  61.1 37.2 %collective-permute-start.4 = (f32[8,64,768]{2,1,0:T(8,128)S(1)}, f32[8,64,768]{2,1,0:T(8,128)}, u32[]{:S(2)}, u32[]{:S(2)}) collective-permute-start(f32[8,64,768]{2,1,0:T(8,128)S(1)} %all-to-all-done.refs_2_), channel_id=1, source_target_pairs={{0,1},{1,0},{2,3},{3,2},{4,5},{5,4},{6,7},{7,6},{8,9},{9,8},{10,11... | collective-permute-start | bytes 4718600 | tf_op jit(solution)/shard_map/ppermute | solution.py:994
  93.3 41.3 %collective-permute-start.7 = (f32[768,384]{1,0:T(8,128)}, f32[768,384]{1,0:T(8,128)}, u32[]{:S(2)}, u32[]{:S(2)}) collective-permute-start(f32[768,384]{1,0:T(8,128)} %constant_dynamic-slice_fusion.11), channel_id=1, source_target_pairs={{0,2},{1,3},{2,0},{3,1},{4,6},{5,7},{6,4},{7,5},{8,10},{9,11},{10,... | collective-permute-start | bytes 3538952 | tf_op jit(solution)/shard_map/ppermute | solution.py:994
  93.8 40.8 %collective-permute-start.9 = (f32[384,768]{1,0:T(8,128)}, f32[384,768]{1,0:T(8,128)}, u32[]{:S(2)}, u32[]{:S(2)}) collective-permute-start(f32[384,768]{1,0:T(8,128)} %collective-permute-done.refs_7_), channel_id=1, source_target_pairs={{0,4},{4,0},{8,12},{12,8},{16,20},{20,16},{24,28},{28,24},{1,5},{5... | collective-permute-start | bytes 3538952 | tf_op jit(solution)/shard_map/ppermute | solution.py:994
  95.4 39.2 %collective-permute-start.8 = (f32[192,768]{1,0:T(8,128)}, f32[192,768]{1,0:T(8,128)}, u32[]{:S(2)}, u32[]{:S(2)}) collective-permute-start(f32[192,768]{1,0:T(8,128)} %refs_8_.3), channel_id=1, source_target_pairs={{0,2},{1,3},{2,0},{3,1},{4,6},{5,7},{6,4},{7,5},{8,10},{9,11},{10,... | collective-permute-start | bytes 1769480 | tf_op jit(solution)/shard_map/ppermute | solution.py:994
  236.3 37.5 %collective-permute-start.30 = (f32[256,768]{1,0:T(8,128)S(1)}, f32[256,768]{1,0:T(8,128)S(1)}, u32[]{:S(2)}, u32[]{:S(2)}) collective-permute-start(f32[256,768]{1,0:T(8,128)S(1)} %get-tuple-element.389), channel_id=1, source_target_pairs={{0,2},{1,3},{2,0},{3,1},{4,6},{5,7},{6,4},{7,5},{8,10},{9,11},{10,... | collective-permute-start | bytes 2359304 | tf_op jit(solution)/shard_map/ppermute | solution.py:994
  274.7 60.6 %collective-permute-start.39 = (f32[96,768]{1,0:T(8,128)}, f32[96,768]{1,0:T(8,128)S(1)}, u32[]{:S(2)}, u32[]{:S(2)}) collective-permute-start(f32[96,768]{1,0:T(8,128)} %constant_dynamic-slice_fusion.5), channel_id=1, source_target_pairs={{0,16},{4,20},{8,24},{12,28},{16,0},{20,4},{24,8},{28,12},{1,17},{... | collective-permute-start | bytes 884744 | tf_op jit(solution)/shard_map/ppermute | solution.py:994
  279.2 57.1 %all-to-all-start.2 = ((f32[8,64,768]{2,1,0:T(8,128)}), f32[8,64,768]{2,1,0:T(8,128)}, u32[]{:S(2)}, u32[]{:S(2)}) async-start(f32[8,64,768]{2,1,0:T(8,128)} %bitcast.46), calls=%async_computation.2 | async-start | bytes 3145728 | tf_op jit(solution)/shard_map/all_to_all | solution.py:1023
  298.9 36.5 %collective-permute-start.37 = (f32[192,768]{1,0:T(8,128)S(1)}, f32[192,768]{1,0:T(8,128)S(1)}, u32[]{:S(2)}, u32[]{:S(2)}) collective-permute-start(f32[192,768]{1,0:T(8,128)S(1)} %constant_dynamic-slice_fusion.6), channel_id=1, source_target_pairs={{0,8},{4,12},{8,0},{12,4},{16,24},{20,28},{24,16},{28,20},{1,9},{5... | collective-permute-start | bytes 1769480 | tf_op jit(solution)/shard_map/ppermute | solution.py:994
  299.3 36.8 %collective-permute-start.36 = (f32[2,192,768]{2,1,0:T(8,128)S(1)}, f32[2,192,768]{2,1,0:T(8,128)}, u32[]{:S(2)}, u32[]{:S(2)}) collective-permute-start(f32[2,192,768]{2,1,0:T(8,128)S(1)} %copy-done.82), channel_id=1, source_target_pairs={{0,2},{1,3},{2,0},{3,1},{4,6},{5,7},{6,4},{7,5},{8,10},{9,11},{10,... | collective-permute-start | bytes 3538952 | tf_op jit(solution)/shard_map/ppermute | solution.py:994
  340.0 59.2 %collective-permute-start.45 = (f32[8,64,768]{2,1,0:T(8,128)}, f32[8,64,768]{2,1,0:T(8,128)}, u32[]{:S(2)}, u32[]{:S(2)}) collective-permute-start(f32[8,64,768]{2,1,0:T(8,128)} %get-tuple-element.329), channel_id=1, source_target_pairs={{0,1},{1,0},{2,3},{3,2},{4,5},{5,4},{6,7},{7,6},{8,9},{9,8},{10,11... | collective-permute-start | bytes 4718600 | tf_op jit(solution)/shard_map/ppermute | solution.py:994
  349.0 50.2 %collective-permute-start.46 = (f32[8,64,768]{2,1,0:T(8,128)S(1)}, f32[8,64,768]{2,1,0:T(8,128)S(1)}, u32[]{:S(2)}, u32[]{:S(2)}) collective-permute-start(f32[8,64,768]{2,1,0:T(8,128)S(1)} %add.255), channel_id=1, source_target_pairs={{0,2},{1,3},{2,0},{3,1},{4,6},{5,7},{6,4},{7,5},{8,10},{9,11},{10,... | collective-permute-start | bytes 4718600 | tf_op jit(solution)/shard_map/ppermute | solution.py:994
  405.2 64.0 %all-to-all-start.3 = ((f32[8,64,768]{2,1,0:T(8,128)}), f32[8,64,768]{2,1,0:T(8,128)}, u32[]{:S(2)}, u32[]{:S(2)}) async-start(f32[8,64,768]{2,1,0:T(8,128)} %bitcast.47), calls=%async_computation.3 | async-start | bytes 3145728 | tf_op jit(solution)/shard_map/all_to_all | solution.py:1023
  410.9 58.2 %collective-permute-start.53 = (f32[8,64,768]{2,1,0:T(8,128)}, f32[8,64,768]{2,1,0:T(8,128)}, u32[]{:S(2)}, u32[]{:S(2)}) collective-permute-start(f32[8,64,768]{2,1,0:T(8,128)} %all-to-all-done.2.refs_0_), channel_id=1, source_target_pairs={{0,2},{1,3},{2,0},{3,1},{4,6},{5,7},{6,4},{7,5},{8,10},{9,11},{10,... | collective-permute-start | bytes 4718600 | tf_op jit(solution)/shard_map/ppermute | solution.py:994
  411.9 57.2 %collective-permute-start.54 = (f32[8,64,768]{2,1,0:T(8,128)}, f32[8,64,768]{2,1,0:T(8,128)}, u32[]{:S(2)}, u32[]{:S(2)}) collective-permute-start(f32[8,64,768]{2,1,0:T(8,128)} %all-to-all-done.2.refs_0_), channel_id=1, source_target_pairs={{0,1},{1,0},{2,3},{3,2},{4,5},{5,4},{6,7},{7,6},{8,9},{9,8},{10,11... | collective-permute-start | bytes 4718600 | tf_op jit(solution)/shard_map/ppermute | solution.py:994
  413.0 45.2 %collective-permute-start.52 = (f32[192,768]{1,0:T(8,128)}, f32[192,768]{1,0:T(8,128)}, u32[]{:S(2)}, u32[]{:S(2)}) collective-permute-start(f32[192,768]{1,0:T(8,128)} %pad_maximum_fusion.6), channel_id=1, source_target_pairs={{0,8},{4,12},{8,0},{12,4},{16,24},{20,28},{24,16},{28,20},{1,9},{5... | collective-permute-start | bytes 1769480 | tf_op jit(solution)/shard_map/ppermute | solution.py:994
  418.0 39.7 %collective-permute-start.51 = (f32[96,768]{1,0:T(8,128)S(1)}, f32[96,768]{1,0:T(8,128)S(1)}, u32[]{:S(2)}, u32[]{:S(2)}) collective-permute-start(f32[96,768]{1,0:T(8,128)S(1)} %dynamic-slice_add_fusion.8), channel_id=1, source_target_pairs={{0,16},{4,20},{8,24},{12,28},{16,0},{20,4},{24,8},{28,12},{1,17},{... | collective-permute-start | bytes 884744 | tf_op jit(solution)/shard_map/ppermute | solution.py:994
  422.1 46.2 %collective-permute-start.50 = (f32[192,768]{1,0:T(8,128)S(1)}, f32[192,768]{1,0:T(8,128)S(1)}, u32[]{:S(2)}, u32[]{:S(2)}) collective-permute-start(f32[192,768]{1,0:T(8,128)S(1)} %constant_dynamic-slice_fusion.1), channel_id=1, source_target_pairs={{0,8},{4,12},{8,0},{12,4},{16,24},{20,28},{24,16},{28,20},{1,9},{5... | collective-permute-start | bytes 1769480 | tf_op jit(solution)/shard_map/ppermute | solution.py:994
  473.3 37.2 %collective-permute-start.59 = (f32[8,64,768]{2,1,0:T(8,128)}, f32[8,64,768]{2,1,0:T(8,128)}, u32[]{:S(2)}, u32[]{:S(2)}) collective-permute-start(f32[8,64,768]{2,1,0:T(8,128)} %all-to-all-done.3.refs_0_), channel_id=1, source_target_pairs={{0,2},{1,3},{2,0},{3,1},{4,6},{5,7},{6,4},{7,5},{8,10},{9,11},{10,... | collective-permute-start | bytes 4718600 | tf_op jit(solution)/shard_map/ppermute | solution.py:994
  479.4 40.0 %collective-permute-start.66 = (f32[384,768]{1,0:T(8,128)}, f32[384,768]{1,0:T(8,128)}, u32[]{:S(2)}, u32[]{:S(2)}) collective-permute-start(f32[384,768]{1,0:T(8,128)} %pad_maximum_fusion.4), channel_id=1, source_target_pairs={{0,4},{4,0},{8,12},{12,8},{16,20},{20,16},{24,28},{28,24},{1,5},{5... | collective-permute-start | bytes 3538952 | tf_op jit(solution)/shard_map/ppermute | solution.py:994
  543.0 36.6 %collective-permute-start.70 = (f32[384,768]{1,0:T(8,128)}, f32[384,768]{1,0:T(8,128)S(1)}, u32[]{:S(2)}, u32[]{:S(2)}) collective-permute-start(f32[384,768]{1,0:T(8,128)} %pad_maximum_fusion.5), channel_id=1, source_target_pairs={{0,4},{4,0},{8,12},{12,8},{16,20},{20,16},{24,28},{28,24},{1,5},{5... | collective-permute-start | bytes 3538952 | tf_op jit(solution)/shard_map/ppermute | solution.py:994
  (145 other events, 1948.3 us)

commit v4 on v3

--- a/solution.py
+++ b/solution.py
@@ -671,6 +671,76 @@
     return outs[:2], outs[2:]
 
 
+def feed_forward_pair(normed, turned, cotangent, ups, biases, downs, sums):
+    rows, model = normed[0].shape
+    units = biases[0].shape[1]
+    step = min(256, units)
+    tiles = units // step
+
+    def body(*refs):
+        nh_ref, nl_ref, th_ref, tl_ref, ch_ref, cl_ref, bias_ref = refs[:7]
+        up_refs, down_refs, (feed_in, grad_in) = refs[7:9], refs[9:11], refs[11:13]
+        feed_ref, grad_ref, gbias_ref = refs[13:16]
+        gup_refs, gdown_refs = refs[16:18], refs[18:20]
+        uh_ref, ul_ref, dh_ref, dl_ref = refs[20:]
+        t = pl.program_id(0)
+
+        @pl.when(t == 0)
+        def _():
+            feed_ref[...] = feed_in[...]
+            grad_ref[...] = grad_in[...]
+
+        for j in range(2):
+
+            @pl.when(t // tiles == j)
+            def _(j=j):
+                uh_ref[...], ul_ref[...] = parts_of(up_refs[j][...])
+                dh_ref[...], dl_ref[...] = parts_of(down_refs[j][...])
+
+        own_normed = (nh_ref[...], nl_ref[...])
+        own_cotangent = (ch_ref[...], cl_ref[...])
+        up_parts, down_parts = (uh_ref[...], ul_ref[...]), (dh_ref[...], dl_ref[...])
+        before = dot_parts(own_normed, up_parts, NN) + bias_ref[...]
+        grad_active = dot_parts(own_cotangent, down_parts, NT)
+        below = 0.5 + 0.5 * lax.erf(before * math.sqrt(0.5))
+        slope = below + before * (jnp.exp(-0.5 * before * before) * (1.0 / math.sqrt(2.0 * math.pi)))
+        active = before * below
+        grad_before = grad_active * slope
+        gbias_ref[...] = column_sum(grad_before)
+        active_parts = parts_of(active)
+        grad_parts = parts_of(grad_before)
+        feed_ref[...] += dot_parts(active_parts, down_parts, NN)
+        grad_ref[...] += dot_parts(grad_parts, up_parts, NT)
+        grad_up = dot_parts((th_ref[...], tl_ref[...]), grad_parts, NN)
+        grad_down = dot_parts(active_parts, own_cotangent, TN)
+        for j in range(2):
+
+            @pl.when(t // tiles == j)
+            def _(j=j):
+                gup_refs[j][...] = grad_up
+                gdown_refs[j][...] = grad_down
+
+    total = struct((rows, model))
+    bias = jnp.concatenate(biases, 1)
+    args = [*normed, *turned, *cotangent, bias, *ups, *downs, *sums]
+    place = lambda t, j: jnp.minimum(t, tiles - 1) if j == 0 else jnp.maximum(t - tiles, 0)
+    columns = [pl.BlockSpec((model, step), lambda t, j=j: (0, place(t, j))) for j in range(2)]
+    some_rows = [pl.BlockSpec((step, model), lambda t, j=j: (place(t, j), 0)) for j in range(2)]
+    one_row = pl.BlockSpec((1, step), lambda t: (0, t))
+    outs = run_kernel(
+        body,
+        "feed_forward_pair",
+        (2 * tiles,),
+        [whole(a) for a in args[:6]] + [one_row] + columns + some_rows + [whole(total)] * 2,
+        [whole(total)] * 2 + [one_row] + columns + some_rows,
+        [total, total, struct(bias.shape)] + [struct((model, units))] * 2 + [struct((units, model))] * 2,
+        [pltpu.VMEM((model, step), BF16)] * 2 + [pltpu.VMEM((step, model), BF16)] * 2,
+        args,
+        31,
+    )
+    return outs[:2], outs[2], outs[3:5], outs[5:7]
+
+
 def hidden_backward(hidden, feed, grad_normed, cotangent, m_parts, weights, gain, bias):
     rows, model = hidden.shape
     blocks, half, width = m_parts[0].shape
@@ -1158,27 +1228,28 @@
     far_up = lambda i: up_2[i * third : (i + 1) * third] + up_3[i * third : (i + 1) * third]
     leaving_2, staying_2 = split_rows(down_2, "seq", 1)
     leaving_3, staying_3 = split_rows(down_3, "seq", 1)
-    half = leaving_2.shape[0] // 2
-    far_ups = [swap(far_up(0), "chan", 2)]
-    came = [swap(leaving_2[:half] + leaving_3[:half], "seq", 1)]
-    sums, (up_1, down_1, bias_grads[1]) = units(1, sums)
-    *sums, far_ups[0], came[0], up_1, down_1 = meet(*sums, far_ups[0], came[0], up_1, down_1)
-    up_1, down_1 = swap(up_1, "chan", 1), swap(down_1, "chan", 1)
-    far_ups.append(swap(far_up(1), "chan", 2))
-    came.append(swap(leaving_2[half:] + leaving_3[half:], "seq", 1))
-    sums, (up_0, down_0, bias_grads[0]) = units(0, sums)
-    *sums, far_ups[1], came[1], up_1, down_1 = meet(*sums, far_ups[1], came[1], up_1, down_1)
-    far_ups.append(swap(far_up(2), "chan", 2))
-    leaving, far_staying = split_rows(staying_2 + staying_3 + jnp.concatenate(came, 0), "seq", 2)
+    far_ups = [swap(up_2[: 2 * third] + up_3[: 2 * third], "chan", 2)]
+    came = swap(leaving_2 + leaving_3, "seq", 1)
+    sums, near_bias, (up_1, up_0), (down_1, down_0) = feed_forward_pair(
+        normed2, turned, cot_parts, [up_parts[1][0], up_parts[0][0]], [row(up_bias_parts[1]), row(up_bias_parts[0])],
+        [down_parts[1][0], down_parts[0][0]], sums,
+    )
+    bias_grads[1], bias_grads[0] = jnp.split(near_bias, 2, 1)
+    *sums, far_ups[0], came, up_1, down_1 = meet(*sums, far_ups[0], came, up_1, down_1)
+    down_1, up_1 = swap(down_1, "chan", 1), swap(up_1, "chan", 1)
+    far_ups.append(swap(up_2[2 * third :] + up_3[2 * third :], "chan", 2))
+    leaving, far_staying = split_rows(staying_2 + staying_3 + came, "seq", 2)
     far_came = swap(leaving, "seq", 2)
     leaving_0, staying_0 = split_rows(down_0, "seq", 1)
     leaving_1, staying_1 = split_rows(down_1, "seq", 1)
-    near_came = swap(leaving_0 + leaving_1, "seq", 1)
+    near_leaving = leaving_0 + leaving_1
+    near_leaving, *sums = meet(near_leaving, *sums)
+    near_came = swap(near_leaving, "seq", 1)
     (out_rows, grad_hidden, sums2), grad_mixed, (out_near, out_far) = hidden_backward(
         hidden, sums[0], sums[1], cot_own, mixed, out_parts, row(ln2_gain), row(down_bias)
     )
-    grad_hidden, far_ups[2], far_came, grad_mixed, out_rows = meet(
-        grad_hidden, far_ups[2], far_came, grad_mixed, out_rows
+    grad_hidden, far_ups[1], far_came, grad_mixed, out_rows, up_1 = meet(
+        grad_hidden, far_ups[1], far_came, grad_mixed, out_rows, up_1
     )
 
     grad_mixed = [g if k == 0 else swap(g, "chan", k) for k, g in enumerate(grad_mixed)]
@@ -1239,57 +1310,56 @@
     came = swap(leaving, "seq", 2)
     grad_up, grad_down = up_staying + up_came, join_rows(grad_down, down_came, "seq", 4)
     down_came, up_came = swap(grad_down, "seq", 2), swap(grad_up, "seq", 4)
-    out_far, out_near = swap(out_blocks, "chan", 2), swap(out_blocks, "chan", 1)
+    out_far = swap(out_blocks, "chan", 2)
     grad_fw1, grad_fb1, grad_fw2, grad_fb2, grad_fw3, grad_decay = filter_pull(grad_kernel)
-    grad_x_blocks, came, up_came, down_came, grad_fw3, out_far, out_near = meet(
-        grad_x_blocks, came, up_came, down_came, grad_fw3, out_far, out_near
-    )
-
-    grad_x_far = swap(grad_x_blocks, "chan", 2)
-    out_side = swap(out_far, "chan", 1)
-    leaving, staying = split_rows(staying + came, "seq", 4)
-    came = swap(leaving, "seq", 4)
-    grad_up, grad_down = join_rows(grad_up, up_came, "seq", 4), join_rows(grad_down, down_came, "seq", 2)
-    down_came, up_came = swap(grad_down, "seq", 1), swap(grad_up, "seq", 2)
     up_bias_grads = jnp.take(
         jnp.concatenate(bias_grads, 0), jnp.arange(count, dtype=jnp.int32) ^ chan_index, axis=0
     )
     shared = [sums1[0], sums1[1], *[sums2[i] for i in range(4)], up_bias_grads, grad_fw1, grad_fb1, grad_fw2, grad_fb2]
     split = [mixer_sums, grad_fw3, grad_decay]
     shared_flat, split_flat = pack(shared), pack(split)
-    came, up_came, out_side, shared_flat, grad_x_blocks = meet(came, up_came, out_side, shared_flat, grad_x_blocks)
+    shared_flat = shared_flat + swap(shared_flat, "chan", 1)
+    side_flat = swap(shared_flat, "chan", 2)
+    grad_x_blocks, came, up_came, down_came, side_flat, out_far, out_blocks = meet(
+        grad_x_blocks, came, up_came, down_came, side_flat, out_far, out_blocks
+    )
+
+    grad_x_far = swap(grad_x_blocks, "chan", 2)
+    grad_up, grad_down = join_rows(grad_up, up_came, "seq", 4), join_rows(grad_down, down_came, "seq", 2)
+    down_came, up_came = swap(grad_down, "seq", 1), swap(grad_up, "seq", 2)
+    leaving, staying = split_rows(staying + came, "seq", 4)
+    came = swap(leaving, "seq", 4)
+    came, up_came, grad_x_blocks, out_far, out_blocks = meet(came, up_came, grad_x_blocks, out_far, out_blocks)
 
     mixer_grads = staying + came
     came = swap(mixer_grads, "seq", 4)
     grad_up = join_rows(grad_up, up_came, "seq", 2)
     up_came = swap(grad_up, "seq", 1)
-    side_flat = swap(shared_flat, "chan", 1)
-    output = put_together(own, [out_blocks, out_near, out_far, out_side])
-    came, grad_x_far, output, side_flat, grad_x_blocks = meet(came, grad_x_far, output, side_flat, grad_x_blocks)
+    flat = jnp.concatenate([shared_flat + side_flat, split_flat])
+    side_flat = swap(flat, "seq", 2)
+    came, grad_x_far, side_flat, grad_x_blocks, out_far, out_blocks, down_came = meet(
+        came, grad_x_far, side_flat, grad_x_blocks, out_far, out_blocks, down_came
+    )
 
     mixer_grads = join_rows(mixer_grads, came, "seq", 4)
     came = swap(mixer_grads, "seq", 2)
     grad_x_near, grad_x_side = swap(grad_x_blocks, "chan", 1), swap(grad_x_far, "chan", 1)
-    shared_flat = shared_flat + side_flat
-    side_flat = swap(shared_flat, "chan", 2)
-    came, grad_x_near, grad_x_side, side_flat, up_came, down_came = meet(
-        came, grad_x_near, grad_x_side, side_flat, up_came, down_came
-    )
-
-    flat = jnp.concatenate([shared_flat + side_flat, split_flat])
+    flat = flat + side_flat
+    side_flat = swap(flat, "seq", 4)
+    grad_down = join_rows(grad_down, down_came, "seq", 1)
+    came, side_flat, grad_x_near, grad_x_side, out_far, out_blocks = meet(
+        came, side_flat, grad_x_near, grad_x_side, out_far, out_blocks
+    )
+    flat = flat + side_flat
+    side_flat = swap(flat, "seq", 1)
     mixer_grads = join_rows(mixer_grads, came, "seq", 2)
-    side_flat, came = swap(flat, "seq", 2), swap(mixer_grads, "seq", 1)
+    came = swap(mixer_grads, "seq", 1)
+    out_near, out_side = swap(out_blocks, "chan", 1), swap(out_far, "chan", 1)
     grad_x = put_together(own, [grad_x_blocks, grad_x_near, grad_x_far, grad_x_side])
-    grad_down = join_rows(grad_down, down_came, "seq", 1)
-    side_flat, grad_x, grad_down = meet(side_flat, grad_x, grad_down)
+    up_came, side_flat, out_near, out_side, grad_x = meet(up_came, side_flat, out_near, out_side, grad_x)
     flat = flat + side_flat
-    flat = flat + swap(flat, "seq", 4)
-    flat = flat + swap(flat, "seq", 1)
-    mixer_grads = join_rows(mixer_grads, came, "seq", 1)
     grad_up = join_rows(grad_up, up_came, "seq", 1)
-    grad_in = jnp.transpose(mixer_grads[: 3 * width].reshape(3, width, model), (2, 0, 1))
-    grad_out = mixer_grads[3 * width :]
-
+    output = put_together(own, [out_blocks, out_near, out_far, out_side])
     cut = shared_flat.shape[0]
     grad_ln1_gain, grad_ln1_bias, grad_ln2_gain, grad_ln2_bias, grad_b_out, grad_b_fc2, up_bias_grads, *filt = unpack(
         flat[:cut], shared
@@ -1300,6 +1370,16 @@
     grad_conv_b = mixer_sums[1:4]
     grad_conv_w = mixer_sums[4:13].reshape(3, 3, width)
     grad_b_in = mixer_sums[13:16]
+    small = (
+        [grad_ln1_gain, grad_ln1_bias, grad_ln2_gain, grad_ln2_bias, grad_b_out, grad_b_fc2, grad_b_fc1]
+        + [*filt, grad_fw3, grad_decay, grad_skip, grad_conv_b, grad_conv_w, grad_b_in]
+    )
+    output, grad_up, came, small = meet(output, grad_up, came, small)
+    grad_ln1_gain, grad_ln1_bias, grad_ln2_gain, grad_ln2_bias, grad_b_out, grad_b_fc2, grad_b_fc1 = small[:7]
+    *filt, grad_fw3, grad_decay, grad_skip, grad_conv_b, grad_conv_w, grad_b_in = small[7:]
+    mixer_grads = join_rows(mixer_grads, came, "seq", 1)
+    grad_in = jnp.transpose(mixer_grads[: 3 * width].reshape(3, width, model), (2, 0, 1))
+    grad_out = mixer_grads[3 * width :]
     return (
         output,
         grad_x,

time: 589 us -> 580 us (0.985)
  waiting for transfers between devices: 189 us -> 176 us
  other arithmetic: 39.8 us -> 50 us
    all_to_all x4, waiting for transfers between devices: 17.3 us -> 8.61 us  [transpose_blocks(): lax.all_to_all(values, 'seq', split_axis=0, concat_axis=0, tiled=True)]
    ppermute x71 -> x69, waiting for transfers between devices: 172 us -> 168 us  [swap(): return lax.ppermute(values, axis, [(i, i ^ bit) for i in range(size)])]
    ppermute x71 -> x69, starting transfers between devices: 61.6 us -> 60.3 us  [swap(): return lax.ppermute(values, axis, [(i, i ^ bit) for i in range(size)])]
    unnamed x189 -> x157, local copies, waits for them, and re-layouts: 11.9 us -> 10.9 us
    pallas_call x14 -> x13, Pallas kernels: 206 us -> 206 us  [run_kernel(): pl.pallas_call(body, name=name, grid=grid, in_specs=in_specs, out_specs=o...]
  transfers between devices with their start and end apart: 75 -> 73, of which waited for: 28 -> 29; matrix products, arithmetic and copies ran while one was open for 15% -> 17% of each run, Pallas kernels for 32% -> 33%
where the time goes in v4:
time: 580 us; the launch traced here: 573 us
  Pallas kernels  206 us (36%)
  waiting for transfers between devices  176 us (30%)
  starting transfers between devices  79.1 us (14%)
  other arithmetic  50 us (9%)
  local copies, waits for them, and re-layouts  42 us (7%)
  matrix products  17.4 us (3%)
    pallas_call x13, Pallas kernels, run_kernel(): pl.pallas_call(body, name=name, grid=grid, in_specs=in_specs, out_specs=o...  206 us
    ppermute x69, waiting for transfers between devices, swap(): return lax.ppermute(values, axis, [(i, i ^ bit) for i in range(size)])  168 us
    ppermute x69, starting transfers between devices, swap(): return lax.ppermute(values, axis, [(i, i ^ bit) for i in range(size)])  60.3 us
    all_to_all x4, starting transfers between devices, transpose_blocks(): lax.all_to_all(values, 'seq', split_axis=0, concat_axis=0, tiled=True)  18.9 us
  transfers between devices with their start and end apart: 73, of which 29 were waited for; matrix products, arithmetic and copies ran while one was open for 17% of the time, Pallas kernels for 33%

profile of v4, /device:TPU:0, one launch (start us, length us, event | category | flops | bytes accessed | tf_op | source)
XLA Modules:
  0.0 572.7 jit_solution(4033026565905998226)
XLA Ops:
  6.5 6.0 %all-to-all-start = ((f32[8,64,768]{2,1,0:T(8,128)}), f32[8,64,768]{2,1,0:T(8,128)S(1)}, u32[]{:S(2)}, u32[]{:S(2)}) async-start(f32[8,64,768]{2,1,0:T(8,128)} %constant_dynamic-slice_fusion.14), calls=%async_computation | async-start | bytes 3145728 | tf_op jit(solution)/shard_map/all_to_all | solution.py:1093
  28.2 7.7 %filter_spectrum.1.refs_13_.refs_9_ = f32[8,512,192]{2,1,0:T(8,128)} custom-call(f32[8,256,192]{2,1,0:T(8,128)} %bitcast.40, bf16[512,256]{1,0:T(8,128)(2,1)} %constant.206.clone.high_ref.refs_14_, bf16[512,256]{1,0:T(8,128)(2,1)} %constant.207.clone.low_ref.refs_15_), custom_call_target="tpu_custom_call" | custom-call | flops 9200000000 | bytes 28800000 | tf_op jit(solution)/shard_map/filter_spectrum/pallas_call | solution.py:383
  43.2 6.8 %all-to-all-done.refs_2_ = f32[8,64,768]{2,1,0:T(8,128)S(1)} async-done(((f32[8,64,768]{2,1,0:T(8,128)}), f32[8,64,768]{2,1,0:T(8,128)S(1)}, u32[]{:S(2)}, u32[]{:S(2)}) %all-to-all-start) | async-done | bytes 1572896 | tf_op jit(solution)/shard_map/all_to_all | solution.py:1093
  58.3 27.4 %collective-permute-done.5.refs_4_ = f32[8,64,768]{2,1,0:T(8,128)} collective-permute-done((f32[8,64,768]{2,1,0:T(8,128)S(1)}, f32[8,64,768]{2,1,0:T(8,128)}, u32[]{:S(2)}, u32[]{:S(2)}) %collective-permute-start.5) | collective-permute-done | bytes 1572896 | tf_op jit(solution)/shard_map/ppermute | solution.py:1064
  95.1 33.1 %mixer_forward.1 = (bf16[4,512,768]{2,1,0:T(8,128)(2,1)}, bf16[4,512,768]{2,1,0:T(8,128)(2,1)}, f32[4,3,512,192]{3,2,1,0:T(8,128)}, f32[4,512,192]{2,1,0:T(8,128...) custom-call(s32[1]{0:T(128)} %bitcast.refs_0_.own_ref, ...), custom_call_target="tpu_custom_call" | custom-call | flops 41400000512 | bytes 129600000 | tf_op jit(solution)/shard_map/mixer_forward/pallas_call | solution.py:383
  135.0 8.4 %collective-permute-done.11.refs_2_.refs_6_ = f32[8,32,384]{2,1,0:T(8,128)S(1)} collective-permute-done((f32[8,32,384]{2,1,0:T(8,128)}, f32[8,32,384]{2,1,0:T(8,128)S(1)}, u32[]{:S(2)}, u32[]{:S(2)}) %collective-permute-start.11) | collective-permute-done | bytes 393248 | tf_op jit(solution)/shard_map/ppermute | solution.py:1064
  152.4 8.6 %hidden_forward.1 = (f32[512,768]{1,0:T(8,128)}, bf16[512,768]{1,0:T(8,128)(2,1)}, bf16[512,768]{1,0:T(8,128)(2,1)}, bf16[768,512]{1,0:T(8,128)(2,1)}, bf16[768,...) custom-call(f32[8,32,384]{2,1,0:T(8,128)} %get-tuple-element.241.refs_0_.refs_4_, ...), custom_call_target="tpu_custom_call" | custom-call | flops 10350000128 | bytes 32400000 | tf_op jit(solution)/shard_map/hidden_forward/pallas_call | solution.py:383
  166.0 17.3 %feed_forward.2 = (f32[512,768]{1,0:T(8,128)}, f32[512,768]{1,0:T(8,128)}, f32[768,768]{1,0:T(8,128)}, f32[768,768]{1,0:T(8,128)}, f32[1,768]{1,0:T(1,128)}) custom-call(s32[1]{0:T(128)} %bitcast.6.side_ref, bf16[512,768]{1,0:T(8,128)(2,1)} %get-tuple-element.255.refs_0_, bf16[512,768]{1,0:T(8,128)(2,1)} %get-tuple-element.256.refs_1_, ...), custom_call_target="tpu_custom_call" | custom-call | flops 20700000256 | bytes 64800000 | tf_op jit(solution)/shard_map/feed_forward/pallas_call | solution.py:383
  185.6 18.1 %feed_forward.3 = (f32[512,768]{1,0:T(8,128)}, f32[512,768]{1,0:T(8,128)}, f32[768,768]{1,0:T(8,128)}, f32[768,768]{1,0:T(8,128)}, f32[1,768]{1,0:T(1,128)}) custom-call(s32[1]{0:T(128)} %bitcast.6.side_ref, bf16[512,768]{1,0:T(8,128)(2,1)} %get-tuple-element.255.refs_0_, bf16[512,768]{1,0:T(8,128)(2,1)} %get-tuple-element.256.refs_1_, ...), custom_call_target="tpu_custom_call" | custom-call | flops 20700000256 | bytes 64800000 | tf_op jit(solution)/shard_map/feed_forward/pallas_call | solution.py:383
  210.0 36.3 %feed_forward_pair.1 = (f32[512,768]{1,0:T(8,128)}, f32[512,768]{1,0:T(8,128)}, f32[1,1536]{1,0:T(1,128)}, f32[768,768]{1,0:T(8,128)}, f32[768,768]{1,0:T(8,128)...) custom-call(bf16[512,768]{1,0:T(8,128)(2,1)} %get-tuple-element.255.refs_0_, bf16[512,768]{1,0:T(8,128)(2,1)} %get-tuple-element.256.refs_1_, ...), custom_call_target="tpu_custom_call" | custom-call | flops 35649998848 | bytes 111600000 | tf_op jit(solution)/shard_map/feed_forward_pair/pallas_call | solution.py:383
  256.4 11.6 %hidden_backward.1 = (f32[512,768]{1,0:T(8,128)}, f32[512,768]{1,0:T(8,128)}, f32[8,768]{1,0:T(8,128)}, f32[8,32,384]{2,1,0:T(8,128)}, f32[8,32,384]{2,1,0:T(8,1...) custom-call(f32[512,768]{1,0:T(8,128)} %get-tuple-element.247.refs_0_, ...), custom_call_target="tpu_custom_call" | custom-call | flops 17250000896 | bytes 54000000 | tf_op jit(solution)/shard_map/hidden_backward/pallas_call | solution.py:383
  284.3 6.1 %collective-permute-done.32.refs_5_ = f32[8,32,384]{2,1,0:T(8,128)} collective-permute-done((f32[8,32,384]{2,1,0:T(8,128)}, f32[8,32,384]{2,1,0:T(8,128)}, u32[]{:S(2)}, u32[]{:S(2)}) %collective-permute-start.32) | collective-permute-done | bytes 393248 | tf_op jit(solution)/shard_map/ppermute | solution.py:1064
  300.0 33.6 %mixer_backward.1 = (f32[8,512,192]{2,1,0:T(8,128)}, f32[4,3,512,192]{3,2,1,0:T(8,128)}, f32[16,192]{1,0:T(8,128)}, f32[8,64,768]{2,1,0:T(8,128)}, f32[8,64,768]...) custom-call(s32[1]{0:T(128)} %bitcast.refs_0_.own_ref, s32[1]{0:T(128)} %dynamic_slice.102.refs_1_, ...), custom_call_target="tpu_custom_call" | custom-call | flops 40249999360 | bytes 126000000 | tf_op jit(solution)/shard_map/mixer_backward/pallas_call | solution.py:383
  350.4 10.0 %input_weight_grad.1 = f32[3,192,768]{2,1,0:T(8,128)} custom-call(bf16[4,512,768]{2,1,0:T(8,128)(2,1)} %get-tuple-element.317.nh_ref, bf16[4,512,768]{2,1,0:T(8,128)(2,1)} %get-tuple-element.318.nl_ref, f32[4,3,512,192]{3,2,1,0:T(8,128)} %get-tuple-element.335.gp_ref), custom_call_target="tpu_custom_call" | custom-call | flops 13799999488 | bytes 43200000 | tf_op jit(solution)/shard_map/input_weight_grad/pallas_call | solution.py:383
  363.0 6.4 %collective-permute-done.42 = f32[192,768]{1,0:T(8,128)S(1)} collective-permute-done((f32[192,768]{1,0:T(8,128)S(1)}, f32[192,768]{1,0:T(8,128)S(1)}, u32[]{:S(2)}, u32[]{:S(2)}) %collective-permute-start.42) | collective-permute-done | bytes 589856 | tf_op jit(solution)/shard_map/ppermute | solution.py:1064
  372.9 12.7 %filter_backward.1 = f32[8,256,192]{2,1,0:T(8,128)} custom-call(f32[8,512,192]{2,1,0:T(8,128)} %get-tuple-element.346.s_ref, f32[8,512,192]{2,1,0:T(8,128)} %get-tuple-element.347.g_ref, bf16[256,512]{1,0:T(8,128)(2,1)} %constant.208.clone.refs_16_.ih_ref, bf16[256,512]{1,0:T(8,128)(2,1)} %constant.209.clone.refs_17_.il_ref), custom_call_target="tpu_custom_call" | custom-call | flops 14949999616 | bytes 46800000 | tf_op jit(solution)/shard_map/filter_backward/pallas_call | solution.py:383
  430.3 23.3 %collective-permute-done.52 = f32[14336]{0:T(1024)S(1)} collective-permute-done((f32[14336]{0:T(1024)S(1)}, f32[14336]{0:T(1024)S(1)}, u32[]{:S(2)}, u32[]{:S(2)}) %collective-permute-start.52) | collective-permute-done | bytes 57376 | tf_op jit(solution)/shard_map/ppermute | solution.py:1064
  456.8 10.0 %collective-permute-done.50 = f32[192,768]{1,0:T(8,128)} collective-permute-done((f32[192,768]{1,0:T(8,128)S(1)}, f32[192,768]{1,0:T(8,128)}, u32[]{:S(2)}, u32[]{:S(2)}) %collective-permute-start.50) | collective-permute-done | bytes 589856 | tf_op jit(solution)/shard_map/ppermute | solution.py:1064
  483.9 8.5 %collective-permute-done.55 = f32[192,768]{1,0:T(8,128)} collective-permute-done((f32[192,768]{1,0:T(8,128)}, f32[192,768]{1,0:T(8,128)}, u32[]{:S(2)}, u32[]{:S(2)}) %collective-permute-start.55) | collective-permute-done | bytes 589856 | tf_op jit(solution)/shard_map/ppermute | solution.py:1064
  500.8 6.3 %collective-permute-done.56 = f32[96,768]{1,0:T(8,128)S(1)} collective-permute-done((f32[96,768]{1,0:T(8,128)S(1)}, f32[96,768]{1,0:T(8,128)S(1)}, u32[]{:S(2)}, u32[]{:S(2)}) %collective-permute-start.56) | collective-permute-done | bytes 294944 | tf_op jit(solution)/shard_map/ppermute | solution.py:1064
  515.1 12.0 %collective-permute-done.61 = f32[30720]{0:T(1024)S(1)} collective-permute-done((f32[30720]{0:T(1024)S(1)}, f32[30720]{0:T(1024)S(1)}, u32[]{:S(2)}, u32[]{:S(2)}) %collective-permute-start.61) | collective-permute-done | bytes 122912 | tf_op jit(solution)/shard_map/ppermute | solution.py:1064
  537.1 5.8 %put_together.2 = f32[8,256,768]{2,1,0:T(8,128)} custom-call(s32[1]{0:T(128)} %bitcast.refs_0_.own_ref, f32[8,64,768]{2,1,0:T(8,128)} %all-to-all-done.3.refs_0_, f32[8,64,768]{2,1,0:T(8,128)} %copy-done.63, f32[8,64,768]{2,1,0:T(8,128)} %collective-permute-done.57.refs_2_, f32[8,64,768]{2,1,0:T(8,128)} %copy-done.64), custom_call_target="tpu_custom_call" | custom-call | flops 9200000000 | bytes 28800000 | tf_op jit(solution)/shard_map/put_together/pallas_call | solution.py:383
  556.9 5.8 %put_together.3 = f32[8,256,768]{2,1,0:T(8,128)} custom-call(s32[1]{0:T(128)} %bitcast.refs_0_.own_ref, f32[8,64,768]{2,1,0:T(8,128)} %all-to-all-done.2.refs_0_, f32[8,64,768]{2,1,0:T(8,128)} %collective-permute-done.66.refs_1_, f32[8,64,768]{2,1,0:T(8,128)} %collective-permute-done.53.refs_2_, f32[8,64,768]{2,1,0:T(8,128)} %collective-permute-done.67.refs_3_), custom_call_target="tpu_custom_call" | custom-call | flops 9200000000 | bytes 28800000 | tf_op jit(solution)/shard_map/put_together/pallas_call | solution.py:383
  562.7 6.2 %collective-permute-done.68 = f32[384,768]{1,0:T(8,128)} collective-permute-done((f32[384,768]{1,0:T(8,128)}, f32[384,768]{1,0:T(8,128)}, u32[]{:S(2)}, u32[]{:S(2)}) %collective-permute-start.68) | collective-permute-done | bytes 1179680 | tf_op jit(solution)/shard_map/ppermute | solution.py:1064
  (416 shorter events, 242.6 us)
Async XLA Ops:
  0.7 37.2 %collective-permute-start.1 = (f32[768]{0:T(1024)}, f32[768]{0:T(1024)S(1)}, u32[]{:S(2)}, u32[]{:S(2)}) collective-permute-start(f32[768]{0:T(1024)} %param.48), channel_id=1, source_target_pairs={{0,1},{1,0},{2,3},{3,2},{4,5},{5,4},{6,7},{7,6},{8,9},{9,8},{10,11... | collective-permute-start | bytes 9224 | tf_op jit(solution)/shard_map/ppermute | solution.py:1064
  1.2 36.7 %collective-permute-start.2 = (f32[768]{0:T(1024)}, f32[768]{0:T(1024)S(1)}, u32[]{:S(2)}, u32[]{:S(2)}) collective-permute-start(f32[768]{0:T(1024)} %param.48), channel_id=1, source_target_pairs={{0,2},{1,3},{2,0},{3,1},{4,6},{5,7},{6,4},{7,5},{8,10},{9,11},{10,... | collective-permute-start | bytes 9224 | tf_op jit(solution)/shard_map/ppermute | solution.py:1064
  6.5 43.5 %all-to-all-start = ((f32[8,64,768]{2,1,0:T(8,128)}), f32[8,64,768]{2,1,0:T(8,128)S(1)}, u32[]{:S(2)}, u32[]{:S(2)}) async-start(f32[8,64,768]{2,1,0:T(8,128)} %constant_dynamic-slice_fusion.14), calls=%async_computation | async-start | bytes 3145728 | tf_op jit(solution)/shard_map/all_to_all | solution.py:1093
  54.2 40.8 %all-to-all-start.1 = ((f32[8,64,768]{2,1,0:T(8,128)}), f32[8,64,768]{2,1,0:T(8,128)S(1)}, u32[]{:S(2)}, u32[]{:S(2)}) async-start(f32[8,64,768]{2,1,0:T(8,128)} %constant_dynamic-slice_fusion.12), calls=%async_computation.1 | async-start | bytes 3145728 | tf_op jit(solution)/shard_map/all_to_all | solution.py:1093
  58.2 36.9 %collective-permute-start.4 = (f32[8,64,768]{2,1,0:T(8,128)S(1)}, f32[8,64,768]{2,1,0:T(8,128)}, u32[]{:S(2)}, u32[]{:S(2)}) collective-permute-start(f32[8,64,768]{2,1,0:T(8,128)S(1)} %all-to-all-done.refs_2_), channel_id=1, source_target_pairs={{0,1},{1,0},{2,3},{3,2},{4,5},{5,4},{6,7},{7,6},{8,9},{9,8},{10,11... | collective-permute-start | bytes 4718600 | tf_op jit(solution)/shard_map/ppermute | solution.py:1064
  89.8 41.3 %collective-permute-start.7 = (f32[768,384]{1,0:T(8,128)}, f32[768,384]{1,0:T(8,128)}, u32[]{:S(2)}, u32[]{:S(2)}) collective-permute-start(f32[768,384]{1,0:T(8,128)} %constant_dynamic-slice_fusion.11), channel_id=1, source_target_pairs={{0,2},{1,3},{2,0},{3,1},{4,6},{5,7},{6,4},{7,5},{8,10},{9,11},{10,... | collective-permute-start | bytes 3538952 | tf_op jit(solution)/shard_map/ppermute | solution.py:1064
  91.3 39.8 %collective-permute-start.8 = (f32[192,768]{1,0:T(8,128)}, f32[192,768]{1,0:T(8,128)}, u32[]{:S(2)}, u32[]{:S(2)}) collective-permute-start(f32[192,768]{1,0:T(8,128)} %refs_8_.3), channel_id=1, source_target_pairs={{0,2},{1,3},{2,0},{3,1},{4,6},{5,7},{6,4},{7,5},{8,10},{9,11},{10,... | collective-permute-start | bytes 1769480 | tf_op jit(solution)/shard_map/ppermute | solution.py:1064
  91.8 39.3 %collective-permute-start.9 = (f32[384,768]{1,0:T(8,128)}, f32[384,768]{1,0:T(8,128)}, u32[]{:S(2)}, u32[]{:S(2)}) collective-permute-start(f32[384,768]{1,0:T(8,128)} %collective-permute-done.refs_7_), channel_id=1, source_target_pairs={{0,4},{4,0},{8,12},{12,8},{16,20},{20,16},{24,28},{28,24},{1,5},{5... | collective-permute-start | bytes 3538952 | tf_op jit(solution)/shard_map/ppermute | solution.py:1064
  206.7 39.7 %collective-permute-start.24 = (f32[512,768]{1,0:T(8,128)S(1)}, f32[512,768]{1,0:T(8,128)}, u32[]{:S(2)}, u32[]{:S(2)}) collective-permute-start(f32[512,768]{1,0:T(8,128)S(1)} %slice_add_fusion), channel_id=1, source_target_pairs={{0,2},{1,3},{2,0},{3,1},{4,6},{5,7},{6,4},{7,5},{8,10},{9,11},{10,... | collective-permute-start | bytes 4718600 | tf_op jit(solution)/shard_map/ppermute | solution.py:1064
  208.5 37.9 %collective-permute-start.25 = (f32[384,768]{1,0:T(8,128)S(1)}, f32[384,768]{1,0:T(8,128)S(1)}, u32[]{:S(2)}, u32[]{:S(2)}) collective-permute-start(f32[384,768]{1,0:T(8,128)S(1)} %dynamic-slice_add_fusion.1), channel_id=1, source_target_pairs={{0,4},{4,0},{8,12},{12,8},{16,20},{20,16},{24,28},{28,24},{1,5},{5... | collective-permute-start | bytes 3538952 | tf_op jit(solution)/shard_map/ppermute | solution.py:1064
  255.7 35.8 %collective-permute-start.33 = (f32[384,768]{1,0:T(8,128)}, f32[384,768]{1,0:T(8,128)S(1)}, u32[]{:S(2)}, u32[]{:S(2)}) collective-permute-start(f32[384,768]{1,0:T(8,128)} %dynamic-slice_add_fusion), channel_id=1, source_target_pairs={{0,4},{4,0},{8,12},{12,8},{16,20},{20,16},{24,28},{28,24},{1,5},{5... | collective-permute-start | bytes 3538952 | tf_op jit(solution)/shard_map/ppermute | solution.py:1064
  272.3 62.1 %all-to-all-start.2 = ((f32[8,64,768]{2,1,0:T(8,128)}), f32[8,64,768]{2,1,0:T(8,128)}, u32[]{:S(2)}, u32[]{:S(2)}) async-start(f32[8,64,768]{2,1,0:T(8,128)} %bitcast.46), calls=%async_computation.2 | async-start | bytes 3145728 | tf_op jit(solution)/shard_map/all_to_all | solution.py:1093
  278.3 55.4 %collective-permute-start.37 = (f32[96,768]{1,0:T(8,128)S(1)}, f32[96,768]{1,0:T(8,128)S(1)}, u32[]{:S(2)}, u32[]{:S(2)}) collective-permute-start(f32[96,768]{1,0:T(8,128)S(1)} %constant_dynamic-slice_fusion.5), channel_id=1, source_target_pairs={{0,16},{4,20},{8,24},{12,28},{16,0},{20,4},{24,8},{28,12},{1,17},{... | collective-permute-start | bytes 884744 | tf_op jit(solution)/shard_map/ppermute | solution.py:1064
  292.4 42.0 %collective-permute-start.34 = (f32[2,192,768]{2,1,0:T(8,128)S(1)}, f32[2,192,768]{2,1,0:T(8,128)}, u32[]{:S(2)}, u32[]{:S(2)}) collective-permute-start(f32[2,192,768]{2,1,0:T(8,128)S(1)} %copy-done.66), channel_id=1, source_target_pairs={{0,2},{1,3},{2,0},{3,1},{4,6},{5,7},{6,4},{7,5},{8,10},{9,11},{10,... | collective-permute-start | bytes 3538952 | tf_op jit(solution)/shard_map/ppermute | solution.py:1064
  296.1 37.5 %collective-permute-start.35 = (f32[192,768]{1,0:T(8,128)S(1)}, f32[192,768]{1,0:T(8,128)S(1)}, u32[]{:S(2)}, u32[]{:S(2)}) collective-permute-start(f32[192,768]{1,0:T(8,128)S(1)} %constant_dynamic-slice_fusion.6), channel_id=1, source_target_pairs={{0,8},{4,12},{8,0},{12,4},{16,24},{20,28},{24,16},{28,20},{1,9},{5... | collective-permute-start | bytes 1769480 | tf_op jit(solution)/shard_map/ppermute | solution.py:1064
  297.6 36.9 %collective-permute-start.36 = (f32[384,768]{1,0:T(8,128)S(1)}, f32[384,768]{1,0:T(8,128)}, u32[]{:S(2)}, u32[]{:S(2)}) collective-permute-start(f32[384,768]{1,0:T(8,128)S(1)} %get-tuple-element.326), channel_id=1, source_target_pairs={{0,4},{4,0},{8,12},{12,8},{16,20},{20,16},{24,28},{28,24},{1,5},{5... | collective-permute-start | bytes 3538952 | tf_op jit(solution)/shard_map/ppermute | solution.py:1064
  335.5 61.6 %collective-permute-start.43 = (f32[8,64,768]{2,1,0:T(8,128)}, f32[8,64,768]{2,1,0:T(8,128)}, u32[]{:S(2)}, u32[]{:S(2)}) collective-permute-start(f32[8,64,768]{2,1,0:T(8,128)} %get-tuple-element.344), channel_id=1, source_target_pairs={{0,1},{1,0},{2,3},{3,2},{4,5},{5,4},{6,7},{7,6},{8,9},{9,8},{10,11... | collective-permute-start | bytes 4718600 | tf_op jit(solution)/shard_map/ppermute | solution.py:1064
  345.3 51.8 %collective-permute-start.44 = (f32[8,64,768]{2,1,0:T(8,128)}, f32[8,64,768]{2,1,0:T(8,128)S(1)}, u32[]{:S(2)}, u32[]{:S(2)}) collective-permute-start(f32[8,64,768]{2,1,0:T(8,128)} %add.247), channel_id=1, source_target_pairs={{0,2},{1,3},{2,0},{3,1},{4,6},{5,7},{6,4},{7,5},{8,10},{9,11},{10,... | collective-permute-start | bytes 4718600 | tf_op jit(solution)/shard_map/ppermute | solution.py:1064
  403.2 63.5 %all-to-all-start.3 = ((f32[8,64,768]{2,1,0:T(8,128)}), f32[8,64,768]{2,1,0:T(8,128)}, u32[]{:S(2)}, u32[]{:S(2)}) async-start(f32[8,64,768]{2,1,0:T(8,128)} %bitcast.47), calls=%async_computation.3 | async-start | bytes 3145728 | tf_op jit(solution)/shard_map/all_to_all | solution.py:1093
  410.1 46.7 %collective-permute-start.48 = (f32[192,768]{1,0:T(8,128)}, f32[192,768]{1,0:T(8,128)}, u32[]{:S(2)}, u32[]{:S(2)}) collective-permute-start(f32[192,768]{1,0:T(8,128)} %constant_dynamic-slice_fusion.1), channel_id=1, source_target_pairs={{0,8},{4,12},{8,0},{12,4},{16,24},{20,28},{24,16},{28,20},{1,9},{5... | collective-permute-start | bytes 1769480 | tf_op jit(solution)/shard_map/ppermute | solution.py:1064
  412.8 44.0 %collective-permute-start.49 = (f32[96,768]{1,0:T(8,128)}, f32[96,768]{1,0:T(8,128)}, u32[]{:S(2)}, u32[]{:S(2)}) collective-permute-start(f32[96,768]{1,0:T(8,128)} %dynamic-slice_add_fusion.7), channel_id=1, source_target_pairs={{0,16},{4,20},{8,24},{12,28},{16,0},{20,4},{24,8},{28,12},{1,17},{... | collective-permute-start | bytes 884744 | tf_op jit(solution)/shard_map/ppermute | solution.py:1064
  417.1 49.6 %collective-permute-start.53 = (f32[8,64,768]{2,1,0:T(8,128)}, f32[8,64,768]{2,1,0:T(8,128)}, u32[]{:S(2)}, u32[]{:S(2)}) collective-permute-start(f32[8,64,768]{2,1,0:T(8,128)} %all-to-all-done.2.refs_0_), channel_id=1, source_target_pairs={{0,2},{1,3},{2,0},{3,1},{4,6},{5,7},{6,4},{7,5},{8,10},{9,11},{10,... | collective-permute-start | bytes 4718600 | tf_op jit(solution)/shard_map/ppermute | solution.py:1064
  426.4 40.3 %collective-permute-start.50 = (f32[192,768]{1,0:T(8,128)S(1)}, f32[192,768]{1,0:T(8,128)}, u32[]{:S(2)}, u32[]{:S(2)}) collective-permute-start(f32[192,768]{1,0:T(8,128)S(1)} %pad_maximum_fusion.6), channel_id=1, source_target_pairs={{0,8},{4,12},{8,0},{12,4},{16,24},{20,28},{24,16},{28,20},{1,9},{5... | collective-permute-start | bytes 1769480 | tf_op jit(solution)/shard_map/ppermute | solution.py:1064
  473.3 36.1 %collective-permute-start.57 = (f32[8,64,768]{2,1,0:T(8,128)}, f32[8,64,768]{2,1,0:T(8,128)}, u32[]{:S(2)}, u32[]{:S(2)}) collective-permute-start(f32[8,64,768]{2,1,0:T(8,128)} %all-to-all-done.3.refs_0_), channel_id=1, source_target_pairs={{0,2},{1,3},{2,0},{3,1},{4,6},{5,7},{6,4},{7,5},{8,10},{9,11},{10,... | collective-permute-start | bytes 4718600 | tf_op jit(solution)/shard_map/ppermute | solution.py:1064
  (127 other events, 1646.6 us)

commit v5 on v4

--- a/solution.py
+++ b/solution.py
@@ -1297,19 +1297,23 @@
     )
     mixer_came = swap(mixer_leaving, "seq", 1)
     grad_kernel = filter_backward(s_spec, g_spec, tables).reshape(seq_length, width)
-    far_normed, grad_kernel, down_came, up_came = meet(far_normed, grad_kernel, down_came, up_came)
+    grad_kernel, down_came = meet(grad_kernel, down_came)
+    grad_down = join_rows(grad_down, down_came, "seq", 4)
+    far_normed, up_came, grad_down = meet(far_normed, up_came, grad_down)
+    down_came = swap(grad_down, "seq", 2)
 
     pieces = [p.reshape(rows, model) for p in (grad_normed[0], grad_normed[1], far_normed)]
     grad_x_rows, sums1 = input_backward(pieces, x_rows, grad_hidden, row(ln1_gain))
-    grad_x_rows, grad_kernel, out_blocks, mixer_came, down_came, up_came, sums1 = meet(
-        grad_x_rows, grad_kernel, out_blocks, mixer_came, down_came, up_came, sums1
+    grad_x_rows, grad_kernel, out_blocks, mixer_came, up_came, sums1 = meet(
+        grad_x_rows, grad_kernel, out_blocks, mixer_came, up_came, sums1
     )
 
     grad_x_blocks = transpose_blocks(grad_x_rows.reshape(blocks, quarter, model))
     leaving, staying = split_rows(mixer_staying + mixer_came, "seq", 2)
     came = swap(leaving, "seq", 2)
-    grad_up, grad_down = up_staying + up_came, join_rows(grad_down, down_came, "seq", 4)
-    down_came, up_came = swap(grad_down, "seq", 2), swap(grad_up, "seq", 4)
+    grad_up = up_staying + up_came
+    grad_down = join_rows(grad_down, down_came, "seq", 2)
+    up_came, down_came = swap(grad_up, "seq", 4), swap(grad_down, "seq", 1)
     out_far = swap(out_blocks, "chan", 2)
     grad_fw1, grad_fb1, grad_fw2, grad_fb2, grad_fw3, grad_decay = filter_pull(grad_kernel)
     up_bias_grads = jnp.take(
@@ -1320,45 +1324,44 @@
     shared_flat, split_flat = pack(shared), pack(split)
     shared_flat = shared_flat + swap(shared_flat, "chan", 1)
     side_flat = swap(shared_flat, "chan", 2)
-    grad_x_blocks, came, up_came, down_came, side_flat, out_far, out_blocks = meet(
-        grad_x_blocks, came, up_came, down_came, side_flat, out_far, out_blocks
+    grad_x_blocks, came, up_came, down_came, out_far, out_blocks = meet(
+        grad_x_blocks, came, up_came, down_came, out_far, out_blocks
     )
 
     grad_x_far = swap(grad_x_blocks, "chan", 2)
-    grad_up, grad_down = join_rows(grad_up, up_came, "seq", 4), join_rows(grad_down, down_came, "seq", 2)
-    down_came, up_came = swap(grad_down, "seq", 1), swap(grad_up, "seq", 2)
+    grad_up, grad_down = join_rows(grad_up, up_came, "seq", 4), join_rows(grad_down, down_came, "seq", 1)
+    up_came, up_low = swap(grad_up, "seq", 2), swap(grad_up, "seq", 1)
     leaving, staying = split_rows(staying + came, "seq", 4)
     came = swap(leaving, "seq", 4)
-    came, up_came, grad_x_blocks, out_far, out_blocks = meet(came, up_came, grad_x_blocks, out_far, out_blocks)
+    came, up_came, up_low, grad_x_blocks, out_far, out_blocks, side_flat = meet(
+        came, up_came, up_low, grad_x_blocks, out_far, out_blocks, side_flat
+    )
 
     mixer_grads = staying + came
     came = swap(mixer_grads, "seq", 4)
-    grad_up = join_rows(grad_up, up_came, "seq", 2)
-    up_came = swap(grad_up, "seq", 1)
+    up_high = swap(up_came, "seq", 1)
     flat = jnp.concatenate([shared_flat + side_flat, split_flat])
     side_flat = swap(flat, "seq", 2)
-    came, grad_x_far, side_flat, grad_x_blocks, out_far, out_blocks, down_came = meet(
-        came, grad_x_far, side_flat, grad_x_blocks, out_far, out_blocks, down_came
+    came, grad_x_far, side_flat, grad_x_blocks, out_far, out_blocks, grad_down, up_high = meet(
+        came, grad_x_far, side_flat, grad_x_blocks, out_far, out_blocks, grad_down, up_high
     )
 
     mixer_grads = join_rows(mixer_grads, came, "seq", 4)
-    came = swap(mixer_grads, "seq", 2)
+    came, low = swap(mixer_grads, "seq", 2), swap(mixer_grads, "seq", 1)
     grad_x_near, grad_x_side = swap(grad_x_blocks, "chan", 1), swap(grad_x_far, "chan", 1)
     flat = flat + side_flat
     side_flat = swap(flat, "seq", 4)
-    grad_down = join_rows(grad_down, down_came, "seq", 1)
-    came, side_flat, grad_x_near, grad_x_side, out_far, out_blocks = meet(
-        came, side_flat, grad_x_near, grad_x_side, out_far, out_blocks
+    came, low, side_flat, grad_x_near, grad_x_side, out_far, out_blocks = meet(
+        came, low, side_flat, grad_x_near, grad_x_side, out_far, out_blocks
     )
     flat = flat + side_flat
     side_flat = swap(flat, "seq", 1)
-    mixer_grads = join_rows(mixer_grads, came, "seq", 2)
-    came = swap(mixer_grads, "seq", 1)
+    mixer_grads, came = join_rows(mixer_grads, came, "seq", 2), swap(came, "seq", 1)
     out_near, out_side = swap(out_blocks, "chan", 1), swap(out_far, "chan", 1)
     grad_x = put_together(own, [grad_x_blocks, grad_x_near, grad_x_far, grad_x_side])
-    up_came, side_flat, out_near, out_side, grad_x = meet(up_came, side_flat, out_near, out_side, grad_x)
+    side_flat, out_near, out_side, grad_x = meet(side_flat, out_near, out_side, grad_x)
     flat = flat + side_flat
-    grad_up = join_rows(grad_up, up_came, "seq", 1)
+    grad_up = join_rows(join_rows(grad_up, up_came, "seq", 2), join_rows(up_low, up_high, "seq", 2), "seq", 1)
     output = put_together(own, [out_blocks, out_near, out_far, out_side])
     cut = shared_flat.shape[0]
     grad_ln1_gain, grad_ln1_bias, grad_ln2_gain, grad_ln2_bias, grad_b_out, grad_b_fc2, up_bias_grads, *filt = unpack(
@@ -1377,7 +1380,7 @@
     output, grad_up, came, small = meet(output, grad_up, came, small)
     grad_ln1_gain, grad_ln1_bias, grad_ln2_gain, grad_ln2_bias, grad_b_out, grad_b_fc2, grad_b_fc1 = small[:7]
     *filt, grad_fw3, grad_decay, grad_skip, grad_conv_b, grad_conv_w, grad_b_in = small[7:]
-    mixer_grads = join_rows(mixer_grads, came, "seq", 1)
+    mixer_grads = join_rows(mixer_grads, join_rows(low, came, "seq", 2), "seq", 1)
     grad_in = jnp.transpose(mixer_grads[: 3 * width].reshape(3, width, model), (2, 0, 1))
     grad_out = mixer_grads[3 * width :]
     return (

time: 580 us -> 552 us (0.952)
  waiting for transfers between devices: 176 us -> 159 us
  other arithmetic: 50 us -> 41.1 us
    ppermute x69 -> x71, waiting for transfers between devices: 168 us -> 150 us  [swap(): return lax.ppermute(values, axis, [(i, i ^ bit) for i in range(size)])]
    ppermute x69 -> x71, starting transfers between devices: 60.3 us -> 60.3 us  [swap(): return lax.ppermute(values, axis, [(i, i ^ bit) for i in range(size)])]
  transfers between devices with their start and end apart: 73 -> 75, of which waited for: 29 -> 26; matrix products, arithmetic and copies ran while one was open for 17% -> 16% of each run, Pallas kernels for 33% -> 35%
where the time goes in v5:
time: 552 us; the launch traced here: 545 us
  Pallas kernels  206 us (37%)
  waiting for transfers between devices  159 us (29%)
  starting transfers between devices  79.2 us (14%)
  other arithmetic  41.1 us (7%)
  local copies, waits for them, and re-layouts  40.7 us (7%)
  matrix products  17.4 us (3%)
    pallas_call x13, Pallas kernels, run_kernel(): pl.pallas_call(body, name=name, grid=grid, in_specs=in_specs, out_specs=o...  206 us
    ppermute x71, waiting for transfers between devices, swap(): return lax.ppermute(values, axis, [(i, i ^ bit) for i in range(size)])  150 us
    ppermute x71, starting transfers between devices, swap(): return lax.ppermute(values, axis, [(i, i ^ bit) for i in range(size)])  60.3 us
    all_to_all x4, starting transfers between devices, transpose_blocks(): lax.all_to_all(values, 'seq', split_axis=0, concat_axis=0, tiled=True)  18.9 us
  transfers between devices with their start and end apart: 75, of which 26 were waited for; matrix products, arithmetic and copies ran while one was open for 16% of the time, Pallas kernels for 35%

profile of v5, /device:TPU:0, one launch (start us, length us, event | category | flops | bytes accessed | tf_op | source)
XLA Modules:
  0.0 544.9 jit_solution(14721283208798548671)
XLA Ops:
  6.5 6.0 %all-to-all-start = ((f32[8,64,768]{2,1,0:T(8,128)}), f32[8,64,768]{2,1,0:T(8,128)S(1)}, u32[]{:S(2)}, u32[]{:S(2)}) async-start(f32[8,64,768]{2,1,0:T(8,128)} %constant_dynamic-slice_fusion.14), calls=%async_computation | async-start | bytes 3145728 | tf_op jit(solution)/shard_map/all_to_all | solution.py:1093
  28.2 7.8 %filter_spectrum.1.refs_13_.refs_9_ = f32[8,512,192]{2,1,0:T(8,128)} custom-call(f32[8,256,192]{2,1,0:T(8,128)} %bitcast.40, bf16[512,256]{1,0:T(8,128)(2,1)} %constant.214.clone.high_ref.refs_14_, bf16[512,256]{1,0:T(8,128)(2,1)} %constant.215.clone.low_ref.refs_15_), custom_call_target="tpu_custom_call" | custom-call | flops 9200000000 | bytes 28800000 | tf_op jit(solution)/shard_map/filter_spectrum/pallas_call | solution.py:383
  43.2 6.8 %all-to-all-done.refs_2_ = f32[8,64,768]{2,1,0:T(8,128)S(1)} async-done(((f32[8,64,768]{2,1,0:T(8,128)}), f32[8,64,768]{2,1,0:T(8,128)S(1)}, u32[]{:S(2)}, u32[]{:S(2)}) %all-to-all-start) | async-done | bytes 1572896 | tf_op jit(solution)/shard_map/all_to_all | solution.py:1093
  58.3 27.4 %collective-permute-done.5.refs_4_ = f32[8,64,768]{2,1,0:T(8,128)} collective-permute-done((f32[8,64,768]{2,1,0:T(8,128)S(1)}, f32[8,64,768]{2,1,0:T(8,128)}, u32[]{:S(2)}, u32[]{:S(2)}) %collective-permute-start.5) | collective-permute-done | bytes 1572896 | tf_op jit(solution)/shard_map/ppermute | solution.py:1064
  95.1 33.1 %mixer_forward.1 = (bf16[4,512,768]{2,1,0:T(8,128)(2,1)}, bf16[4,512,768]{2,1,0:T(8,128)(2,1)}, f32[4,3,512,192]{3,2,1,0:T(8,128)}, f32[4,512,192]{2,1,0:T(8,128...) custom-call(s32[1]{0:T(128)} %bitcast.refs_0_.own_ref, ...), custom_call_target="tpu_custom_call" | custom-call | flops 41400000512 | bytes 129600000 | tf_op jit(solution)/shard_map/mixer_forward/pallas_call | solution.py:383
  135.0 8.4 %collective-permute-done.11.refs_2_.refs_6_ = f32[8,32,384]{2,1,0:T(8,128)S(1)} collective-permute-done((f32[8,32,384]{2,1,0:T(8,128)}, f32[8,32,384]{2,1,0:T(8,128)S(1)}, u32[]{:S(2)}, u32[]{:S(2)}) %collective-permute-start.11) | collective-permute-done | bytes 393248 | tf_op jit(solution)/shard_map/ppermute | solution.py:1064
  145.1 5.7 %collective-permute-done.12.refs_3_.refs_7_ = f32[8,32,384]{2,1,0:T(8,128)S(1)} collective-permute-done((f32[8,32,384]{2,1,0:T(8,128)}, f32[8,32,384]{2,1,0:T(8,128)S(1)}, u32[]{:S(2)}, u32[]{:S(2)}) %collective-permute-start.12) | collective-permute-done | bytes 393248 | tf_op jit(solution)/shard_map/ppermute | solution.py:1064
  152.4 8.6 %hidden_forward.1 = (f32[512,768]{1,0:T(8,128)}, bf16[512,768]{1,0:T(8,128)(2,1)}, bf16[512,768]{1,0:T(8,128)(2,1)}, bf16[768,512]{1,0:T(8,128)(2,1)}, bf16[768,...) custom-call(f32[8,32,384]{2,1,0:T(8,128)} %get-tuple-element.243.refs_0_.refs_4_, ...), custom_call_target="tpu_custom_call" | custom-call | flops 10350000128 | bytes 32400000 | tf_op jit(solution)/shard_map/hidden_forward/pallas_call | solution.py:383
  166.0 17.3 %feed_forward.2 = (f32[512,768]{1,0:T(8,128)}, f32[512,768]{1,0:T(8,128)}, f32[768,768]{1,0:T(8,128)}, f32[768,768]{1,0:T(8,128)}, f32[1,768]{1,0:T(1,128)}) custom-call(s32[1]{0:T(128)} %bitcast.6.side_ref, bf16[512,768]{1,0:T(8,128)(2,1)} %get-tuple-element.257.refs_0_, bf16[512,768]{1,0:T(8,128)(2,1)} %get-tuple-element.258.refs_1_, ...), custom_call_target="tpu_custom_call" | custom-call | flops 20700000256 | bytes 64800000 | tf_op jit(solution)/shard_map/feed_forward/pallas_call | solution.py:383
  185.6 18.1 %feed_forward.3 = (f32[512,768]{1,0:T(8,128)}, f32[512,768]{1,0:T(8,128)}, f32[768,768]{1,0:T(8,128)}, f32[768,768]{1,0:T(8,128)}, f32[1,768]{1,0:T(1,128)}) custom-call(s32[1]{0:T(128)} %bitcast.6.side_ref, bf16[512,768]{1,0:T(8,128)(2,1)} %get-tuple-element.257.refs_0_, bf16[512,768]{1,0:T(8,128)(2,1)} %get-tuple-element.258.refs_1_, ...), custom_call_target="tpu_custom_call" | custom-call | flops 20700000256 | bytes 64800000 | tf_op jit(solution)/shard_map/feed_forward/pallas_call | solution.py:383
  210.0 36.4 %feed_forward_pair.1 = (f32[512,768]{1,0:T(8,128)}, f32[512,768]{1,0:T(8,128)}, f32[1,1536]{1,0:T(1,128)}, f32[768,768]{1,0:T(8,128)}, f32[768,768]{1,0:T(8,128)...) custom-call(bf16[512,768]{1,0:T(8,128)(2,1)} %get-tuple-element.257.refs_0_, bf16[512,768]{1,0:T(8,128)(2,1)} %get-tuple-element.258.refs_1_, ...), custom_call_target="tpu_custom_call" | custom-call | flops 35649998848 | bytes 111600000 | tf_op jit(solution)/shard_map/feed_forward_pair/pallas_call | solution.py:383
  256.4 11.6 %hidden_backward.1 = (f32[512,768]{1,0:T(8,128)}, f32[512,768]{1,0:T(8,128)}, f32[8,768]{1,0:T(8,128)}, f32[8,32,384]{2,1,0:T(8,128)}, f32[8,32,384]{2,1,0:T(8,1...) custom-call(f32[512,768]{1,0:T(8,128)} %get-tuple-element.249.refs_0_, ...), custom_call_target="tpu_custom_call" | custom-call | flops 17250000896 | bytes 54000000 | tf_op jit(solution)/shard_map/hidden_backward/pallas_call | solution.py:383
  284.4 6.0 %collective-permute-done.32.refs_5_ = f32[8,32,384]{2,1,0:T(8,128)} collective-permute-done((f32[8,32,384]{2,1,0:T(8,128)}, f32[8,32,384]{2,1,0:T(8,128)}, u32[]{:S(2)}, u32[]{:S(2)}) %collective-permute-start.32) | collective-permute-done | bytes 393248 | tf_op jit(solution)/shard_map/ppermute | solution.py:1064
  300.0 33.6 %mixer_backward.1 = (f32[8,512,192]{2,1,0:T(8,128)}, f32[4,3,512,192]{3,2,1,0:T(8,128)}, f32[16,192]{1,0:T(8,128)}, f32[8,64,768]{2,1,0:T(8,128)}, f32[8,64,768]...) custom-call(s32[1]{0:T(128)} %bitcast.refs_0_.own_ref, s32[1]{0:T(128)} %dynamic_slice.102.refs_1_, ...), custom_call_target="tpu_custom_call" | custom-call | flops 40249999360 | bytes 126000000 | tf_op jit(solution)/shard_map/mixer_backward/pallas_call | solution.py:383
  350.4 10.0 %input_weight_grad.1 = f32[3,192,768]{2,1,0:T(8,128)} custom-call(bf16[4,512,768]{2,1,0:T(8,128)(2,1)} %get-tuple-element.319.nh_ref, bf16[4,512,768]{2,1,0:T(8,128)(2,1)} %get-tuple-element.320.nl_ref, f32[4,3,512,192]{3,2,1,0:T(8,128)} %get-tuple-element.337.gp_ref), custom_call_target="tpu_custom_call" | custom-call | flops 13799999488 | bytes 43200000 | tf_op jit(solution)/shard_map/input_weight_grad/pallas_call | solution.py:383
  363.0 6.4 %collective-permute-done.42 = f32[192,768]{1,0:T(8,128)S(1)} collective-permute-done((f32[192,768]{1,0:T(8,128)S(1)}, f32[192,768]{1,0:T(8,128)S(1)}, u32[]{:S(2)}, u32[]{:S(2)}) %collective-permute-start.42) | collective-permute-done | bytes 589856 | tf_op jit(solution)/shard_map/ppermute | solution.py:1064
  373.9 12.7 %filter_backward.1 = f32[8,256,192]{2,1,0:T(8,128)} custom-call(f32[8,512,192]{2,1,0:T(8,128)} %get-tuple-element.351.s_ref, f32[8,512,192]{2,1,0:T(8,128)} %get-tuple-element.352.g_ref, bf16[256,512]{1,0:T(8,128)(2,1)} %constant.216.clone.refs_16_.ih_ref, bf16[256,512]{1,0:T(8,128)(2,1)} %constant.217.clone.refs_17_.il_ref), custom_call_target="tpu_custom_call" | custom-call | flops 14949999616 | bytes 46800000 | tf_op jit(solution)/shard_map/filter_backward/pallas_call | solution.py:383
  386.6 10.7 %collective-permute-done.46 = f32[96,768]{1,0:T(8,128)S(1)} collective-permute-done((f32[96,768]{1,0:T(8,128)S(1)}, f32[96,768]{1,0:T(8,128)S(1)}, u32[]{:S(2)}, u32[]{:S(2)}) %collective-permute-start.46) | collective-permute-done | bytes 294944 | tf_op jit(solution)/shard_map/ppermute | solution.py:1064
  434.3 20.1 %collective-permute-done.49 = f32[96,768]{1,0:T(8,128)} collective-permute-done((f32[96,768]{1,0:T(8,128)}, f32[96,768]{1,0:T(8,128)}, u32[]{:S(2)}, u32[]{:S(2)}) %collective-permute-start.49) | collective-permute-done | bytes 294944 | tf_op jit(solution)/shard_map/ppermute | solution.py:1064
  466.3 15.4 %collective-permute-done.53 = f32[96,768]{1,0:T(8,128)S(1)} collective-permute-done((f32[96,768]{1,0:T(8,128)S(1)}, f32[96,768]{1,0:T(8,128)S(1)}, u32[]{:S(2)}, u32[]{:S(2)}) %collective-permute-start.53) | collective-permute-done | bytes 294944 | tf_op jit(solution)/shard_map/ppermute | solution.py:1064
  488.4 5.5 %collective-permute-done.60 = f32[30720]{0:T(1024)S(1)} collective-permute-done((f32[30720]{0:T(1024)S(1)}, f32[30720]{0:T(1024)S(1)}, u32[]{:S(2)}, u32[]{:S(2)}) %collective-permute-start.60) | collective-permute-done | bytes 122912 | tf_op jit(solution)/shard_map/ppermute | solution.py:1064
  504.0 13.1 %collective-permute-done.64 = f32[30720]{0:T(1024)S(1)} collective-permute-done((f32[30720]{0:T(1024)S(1)}, f32[30720]{0:T(1024)S(1)}, u32[]{:S(2)}, u32[]{:S(2)}) %collective-permute-start.64) | collective-permute-done | bytes 122912 | tf_op jit(solution)/shard_map/ppermute | solution.py:1064
  523.8 5.8 %put_together.2 = f32[8,256,768]{2,1,0:T(8,128)} custom-call(s32[1]{0:T(128)} %bitcast.refs_0_.own_ref, f32[8,64,768]{2,1,0:T(8,128)} %all-to-all-done.3.refs_0_, f32[8,64,768]{2,1,0:T(8,128)} %collective-permute-done.65.refs_1_, f32[8,64,768]{2,1,0:T(8,128)} %collective-permute-done.59.refs_2_, f32[8,64,768]{2,1,0:T(8,128)} %collective-permute-done.66.refs_3_), custom_call_target="tpu_custom_call" | custom-call | flops 9200000000 | bytes 28800000 | tf_op jit(solution)/shard_map/put_together/pallas_call | solution.py:383
  536.4 5.8 %put_together.3 = f32[8,256,768]{2,1,0:T(8,128)} custom-call(s32[1]{0:T(128)} %bitcast.refs_0_.own_ref, f32[8,64,768]{2,1,0:T(8,128)} %all-to-all-done.2.refs_0_, f32[8,64,768]{2,1,0:T(8,128)} %copy-done.63, f32[8,64,768]{2,1,0:T(8,128)} %collective-permute-done.52.refs_2_, f32[8,64,768]{2,1,0:T(8,128)} %collective-permute-done.69.refs_3_), custom_call_target="tpu_custom_call" | custom-call | flops 9200000000 | bytes 28800000 | tf_op jit(solution)/shard_map/put_together/pallas_call | solution.py:383
  (416 shorter events, 210.5 us)
Async XLA Ops:
  0.7 37.2 %collective-permute-start.1 = (f32[768]{0:T(1024)}, f32[768]{0:T(1024)S(1)}, u32[]{:S(2)}, u32[]{:S(2)}) collective-permute-start(f32[768]{0:T(1024)} %param.48), channel_id=1, source_target_pairs={{0,1},{1,0},{2,3},{3,2},{4,5},{5,4},{6,7},{7,6},{8,9},{9,8},{10,11... | collective-permute-start | bytes 9224 | tf_op jit(solution)/shard_map/ppermute | solution.py:1064
  1.2 36.7 %collective-permute-start.2 = (f32[768]{0:T(1024)}, f32[768]{0:T(1024)S(1)}, u32[]{:S(2)}, u32[]{:S(2)}) collective-permute-start(f32[768]{0:T(1024)} %param.48), channel_id=1, source_target_pairs={{0,2},{1,3},{2,0},{3,1},{4,6},{5,7},{6,4},{7,5},{8,10},{9,11},{10,... | collective-permute-start | bytes 9224 | tf_op jit(solution)/shard_map/ppermute | solution.py:1064
  6.5 43.5 %all-to-all-start = ((f32[8,64,768]{2,1,0:T(8,128)}), f32[8,64,768]{2,1,0:T(8,128)S(1)}, u32[]{:S(2)}, u32[]{:S(2)}) async-start(f32[8,64,768]{2,1,0:T(8,128)} %constant_dynamic-slice_fusion.14), calls=%async_computation | async-start | bytes 3145728 | tf_op jit(solution)/shard_map/all_to_all | solution.py:1093
  50.0 35.6 %collective-permute-start.5 = (f32[8,64,768]{2,1,0:T(8,128)S(1)}, f32[8,64,768]{2,1,0:T(8,128)}, u32[]{:S(2)}, u32[]{:S(2)}) collective-permute-start(f32[8,64,768]{2,1,0:T(8,128)S(1)} %all-to-all-done.refs_2_), channel_id=1, source_target_pairs={{0,2},{1,3},{2,0},{3,1},{4,6},{5,7},{6,4},{7,5},{8,10},{9,11},{10,... | collective-permute-start | bytes 4718600 | tf_op jit(solution)/shard_map/ppermute | solution.py:1064
  54.2 40.8 %all-to-all-start.1 = ((f32[8,64,768]{2,1,0:T(8,128)}), f32[8,64,768]{2,1,0:T(8,128)S(1)}, u32[]{:S(2)}, u32[]{:S(2)}) async-start(f32[8,64,768]{2,1,0:T(8,128)} %constant_dynamic-slice_fusion.12), calls=%async_computation.1 | async-start | bytes 3145728 | tf_op jit(solution)/shard_map/all_to_all | solution.py:1093
  58.2 36.9 %collective-permute-start.4 = (f32[8,64,768]{2,1,0:T(8,128)S(1)}, f32[8,64,768]{2,1,0:T(8,128)}, u32[]{:S(2)}, u32[]{:S(2)}) collective-permute-start(f32[8,64,768]{2,1,0:T(8,128)S(1)} %all-to-all-done.refs_2_), channel_id=1, source_target_pairs={{0,1},{1,0},{2,3},{3,2},{4,5},{5,4},{6,7},{7,6},{8,9},{9,8},{10,11... | collective-permute-start | bytes 4718600 | tf_op jit(solution)/shard_map/ppermute | solution.py:1064
  89.8 41.3 %collective-permute-start.7 = (f32[768,384]{1,0:T(8,128)}, f32[768,384]{1,0:T(8,128)}, u32[]{:S(2)}, u32[]{:S(2)}) collective-permute-start(f32[768,384]{1,0:T(8,128)} %constant_dynamic-slice_fusion.11), channel_id=1, source_target_pairs={{0,2},{1,3},{2,0},{3,1},{4,6},{5,7},{6,4},{7,5},{8,10},{9,11},{10,... | collective-permute-start | bytes 3538952 | tf_op jit(solution)/shard_map/ppermute | solution.py:1064
  91.3 39.8 %collective-permute-start.8 = (f32[192,768]{1,0:T(8,128)}, f32[192,768]{1,0:T(8,128)}, u32[]{:S(2)}, u32[]{:S(2)}) collective-permute-start(f32[192,768]{1,0:T(8,128)} %refs_8_.3), channel_id=1, source_target_pairs={{0,2},{1,3},{2,0},{3,1},{4,6},{5,7},{6,4},{7,5},{8,10},{9,11},{10,... | collective-permute-start | bytes 1769480 | tf_op jit(solution)/shard_map/ppermute | solution.py:1064
  91.8 39.3 %collective-permute-start.9 = (f32[384,768]{1,0:T(8,128)}, f32[384,768]{1,0:T(8,128)}, u32[]{:S(2)}, u32[]{:S(2)}) collective-permute-start(f32[384,768]{1,0:T(8,128)} %collective-permute-done.refs_7_), channel_id=1, source_target_pairs={{0,4},{4,0},{8,12},{12,8},{16,20},{20,16},{24,28},{28,24},{1,5},{5... | collective-permute-start | bytes 3538952 | tf_op jit(solution)/shard_map/ppermute | solution.py:1064
  206.7 39.7 %collective-permute-start.24 = (f32[512,768]{1,0:T(8,128)S(1)}, f32[512,768]{1,0:T(8,128)}, u32[]{:S(2)}, u32[]{:S(2)}) collective-permute-start(f32[512,768]{1,0:T(8,128)S(1)} %slice_add_fusion), channel_id=1, source_target_pairs={{0,2},{1,3},{2,0},{3,1},{4,6},{5,7},{6,4},{7,5},{8,10},{9,11},{10,... | collective-permute-start | bytes 4718600 | tf_op jit(solution)/shard_map/ppermute | solution.py:1064
  208.5 37.9 %collective-permute-start.25 = (f32[384,768]{1,0:T(8,128)S(1)}, f32[384,768]{1,0:T(8,128)S(1)}, u32[]{:S(2)}, u32[]{:S(2)}) collective-permute-start(f32[384,768]{1,0:T(8,128)S(1)} %dynamic-slice_add_fusion.1), channel_id=1, source_target_pairs={{0,4},{4,0},{8,12},{12,8},{16,20},{20,16},{24,28},{28,24},{1,5},{5... | collective-permute-start | bytes 3538952 | tf_op jit(solution)/shard_map/ppermute | solution.py:1064
  255.7 35.8 %collective-permute-start.33 = (f32[384,768]{1,0:T(8,128)}, f32[384,768]{1,0:T(8,128)S(1)}, u32[]{:S(2)}, u32[]{:S(2)}) collective-permute-start(f32[384,768]{1,0:T(8,128)} %dynamic-slice_add_fusion), channel_id=1, source_target_pairs={{0,4},{4,0},{8,12},{12,8},{16,20},{20,16},{24,28},{28,24},{1,5},{5... | collective-permute-start | bytes 3538952 | tf_op jit(solution)/shard_map/ppermute | solution.py:1064
  272.4 62.0 %all-to-all-start.2 = ((f32[8,64,768]{2,1,0:T(8,128)}), f32[8,64,768]{2,1,0:T(8,128)}, u32[]{:S(2)}, u32[]{:S(2)}) async-start(f32[8,64,768]{2,1,0:T(8,128)} %bitcast.47), calls=%async_computation.2 | async-start | bytes 3145728 | tf_op jit(solution)/shard_map/all_to_all | solution.py:1093
  278.4 55.3 %collective-permute-start.37 = (f32[96,768]{1,0:T(8,128)S(1)}, f32[96,768]{1,0:T(8,128)S(1)}, u32[]{:S(2)}, u32[]{:S(2)}) collective-permute-start(f32[96,768]{1,0:T(8,128)S(1)} %constant_dynamic-slice_fusion.5), channel_id=1, source_target_pairs={{0,16},{4,20},{8,24},{12,28},{16,0},{20,4},{24,8},{28,12},{1,17},{... | collective-permute-start | bytes 884744 | tf_op jit(solution)/shard_map/ppermute | solution.py:1064
  292.5 42.0 %collective-permute-start.34 = (f32[2,192,768]{2,1,0:T(8,128)S(1)}, f32[2,192,768]{2,1,0:T(8,128)}, u32[]{:S(2)}, u32[]{:S(2)}) collective-permute-start(f32[2,192,768]{2,1,0:T(8,128)S(1)} %copy-done.64), channel_id=1, source_target_pairs={{0,2},{1,3},{2,0},{3,1},{4,6},{5,7},{6,4},{7,5},{8,10},{9,11},{10,... | collective-permute-start | bytes 3538952 | tf_op jit(solution)/shard_map/ppermute | solution.py:1064
  296.1 37.5 %collective-permute-start.35 = (f32[192,768]{1,0:T(8,128)S(1)}, f32[192,768]{1,0:T(8,128)S(1)}, u32[]{:S(2)}, u32[]{:S(2)}) collective-permute-start(f32[192,768]{1,0:T(8,128)S(1)} %constant_dynamic-slice_fusion.6), channel_id=1, source_target_pairs={{0,8},{4,12},{8,0},{12,4},{16,24},{20,28},{24,16},{28,20},{1,9},{5... | collective-permute-start | bytes 1769480 | tf_op jit(solution)/shard_map/ppermute | solution.py:1064
  297.6 36.8 %collective-permute-start.36 = (f32[384,768]{1,0:T(8,128)S(1)}, f32[384,768]{1,0:T(8,128)}, u32[]{:S(2)}, u32[]{:S(2)}) collective-permute-start(f32[384,768]{1,0:T(8,128)S(1)} %get-tuple-element.328), channel_id=1, source_target_pairs={{0,4},{4,0},{8,12},{12,8},{16,20},{20,16},{24,28},{28,24},{1,5},{5... | collective-permute-start | bytes 3538952 | tf_op jit(solution)/shard_map/ppermute | solution.py:1064
  335.5 62.0 %collective-permute-start.43 = (f32[8,64,768]{2,1,0:T(8,128)}, f32[8,64,768]{2,1,0:T(8,128)}, u32[]{:S(2)}, u32[]{:S(2)}) collective-permute-start(f32[8,64,768]{2,1,0:T(8,128)} %get-tuple-element.346), channel_id=1, source_target_pairs={{0,1},{1,0},{2,3},{3,2},{4,5},{5,4},{6,7},{7,6},{8,9},{9,8},{10,11... | collective-permute-start | bytes 4718600 | tf_op jit(solution)/shard_map/ppermute | solution.py:1064
  345.3 52.1 %collective-permute-start.44 = (f32[8,64,768]{2,1,0:T(8,128)}, f32[8,64,768]{2,1,0:T(8,128)}, u32[]{:S(2)}, u32[]{:S(2)}) collective-permute-start(f32[8,64,768]{2,1,0:T(8,128)} %add.249), channel_id=1, source_target_pairs={{0,2},{1,3},{2,0},{3,1},{4,6},{5,7},{6,4},{7,5},{8,10},{9,11},{10,... | collective-permute-start | bytes 4718600 | tf_op jit(solution)/shard_map/ppermute | solution.py:1064
  402.4 56.9 %all-to-all-start.3 = ((f32[8,64,768]{2,1,0:T(8,128)}), f32[8,64,768]{2,1,0:T(8,128)}, u32[]{:S(2)}, u32[]{:S(2)}) async-start(f32[8,64,768]{2,1,0:T(8,128)} %bitcast.46), calls=%async_computation.3 | async-start | bytes 3145728 | tf_op jit(solution)/shard_map/all_to_all | solution.py:1093
  409.4 47.1 %collective-permute-start.48 = (f32[192,768]{1,0:T(8,128)}, f32[192,768]{1,0:T(8,128)}, u32[]{:S(2)}, u32[]{:S(2)}) collective-permute-start(f32[192,768]{1,0:T(8,128)} %constant_dynamic-slice_fusion.1), channel_id=1, source_target_pairs={{0,8},{4,12},{8,0},{12,4},{16,24},{20,28},{24,16},{28,20},{1,9},{5... | collective-permute-start | bytes 1769480 | tf_op jit(solution)/shard_map/ppermute | solution.py:1064
  412.1 42.4 %collective-permute-start.49 = (f32[96,768]{1,0:T(8,128)}, f32[96,768]{1,0:T(8,128)}, u32[]{:S(2)}, u32[]{:S(2)}) collective-permute-start(f32[96,768]{1,0:T(8,128)} %dynamic-slice_add_fusion.7), channel_id=1, source_target_pairs={{0,16},{4,20},{8,24},{12,28},{16,0},{20,4},{24,8},{28,12},{1,17},{... | collective-permute-start | bytes 884744 | tf_op jit(solution)/shard_map/ppermute | solution.py:1064
  414.4 44.9 %collective-permute-start.52 = (f32[8,64,768]{2,1,0:T(8,128)}, f32[8,64,768]{2,1,0:T(8,128)}, u32[]{:S(2)}, u32[]{:S(2)}) collective-permute-start(f32[8,64,768]{2,1,0:T(8,128)} %all-to-all-done.2.refs_0_), channel_id=1, source_target_pairs={{0,2},{1,3},{2,0},{3,1},{4,6},{5,7},{6,4},{7,5},{8,10},{9,11},{10,... | collective-permute-start | bytes 4718600 | tf_op jit(solution)/shard_map/ppermute | solution.py:1064
  460.4 40.2 %collective-permute-start.59 = (f32[8,64,768]{2,1,0:T(8,128)}, f32[8,64,768]{2,1,0:T(8,128)}, u32[]{:S(2)}, u32[]{:S(2)}) collective-permute-start(f32[8,64,768]{2,1,0:T(8,128)} %all-to-all-done.3.refs_0_), channel_id=1, source_target_pairs={{0,2},{1,3},{2,0},{3,1},{4,6},{5,7},{6,4},{7,5},{8,10},{9,11},{10,... | collective-permute-start | bytes 4718600 | tf_op jit(solution)/shard_map/ppermute | solution.py:1064
  (127 other events, 1706.4 us)

commit v6 on v5

--- a/solution.py
+++ b/solution.py
@@ -448,7 +448,7 @@
     block = quarter * count
     width = weight.shape[2]
     tile = min(32, block)
-    pair = 2 - blocks % 2
+    pair = math.gcd(blocks, 4)
     span = pair * block
 
     def body(*refs):
@@ -809,7 +809,7 @@
     block = quarter * count
     model = weight.shape[1]
     tile = min(32, block)
-    pair = 2 - blocks % 2
+    pair = math.gcd(blocks, 4)
     span = pair * block
 
     def body(*refs):

time: 552 us -> 554 us (level)
  no operation moved by 1% of the time
where the time goes in v6:
time: 554 us; the launch traced here: 548 us
  Pallas kernels  210 us (38%)
  waiting for transfers between devices  157 us (28%)
  starting transfers between devices  79.3 us (14%)
  other arithmetic  41.1 us (7%)
  local copies, waits for them, and re-layouts  40.7 us (7%)
  matrix products  17.4 us (3%)
    pallas_call x13, Pallas kernels, run_kernel(): pl.pallas_call(body, name=name, grid=grid, in_specs=in_specs, out_specs=o...  210 us
    ppermute x71, waiting for transfers between devices, swap(): return lax.ppermute(values, axis, [(i, i ^ bit) for i in range(size)])  148 us
    ppermute x71, starting transfers between devices, swap(): return lax.ppermute(values, axis, [(i, i ^ bit) for i in range(size)])  60.3 us
    all_to_all x4, starting transfers between devices, transpose_blocks(): lax.all_to_all(values, 'seq', split_axis=0, concat_axis=0, tiled=True)  18.9 us
  transfers between devices with their start and end apart: 75, of which 26 were waited for; matrix products, arithmetic and copies ran while one was open for 16% of the time, Pallas kernels for 35%

profile of v6, /device:TPU:0, one launch (start us, length us, event | category | flops | bytes accessed | tf_op | source)
XLA Modules:
  0.0 547.7 jit_solution(3734199049385979190)
XLA Ops:
  6.5 6.0 %all-to-all-start = ((f32[8,64,768]{2,1,0:T(8,128)}), f32[8,64,768]{2,1,0:T(8,128)S(1)}, u32[]{:S(2)}, u32[]{:S(2)}) async-start(f32[8,64,768]{2,1,0:T(8,128)} %constant_dynamic-slice_fusion.14), calls=%async_computation | async-start | bytes 3145728 | tf_op jit(solution)/shard_map/all_to_all | solution.py:1093
  28.2 7.8 %filter_spectrum.1.refs_13_.refs_9_ = f32[8,512,192]{2,1,0:T(8,128)} custom-call(f32[8,256,192]{2,1,0:T(8,128)} %bitcast.40, bf16[512,256]{1,0:T(8,128)(2,1)} %constant.214.clone.high_ref.refs_14_, bf16[512,256]{1,0:T(8,128)(2,1)} %constant.215.clone.low_ref.refs_15_), custom_call_target="tpu_custom_call" | custom-call | flops 9200000000 | bytes 28800000 | tf_op jit(solution)/shard_map/filter_spectrum/pallas_call | solution.py:383
  43.2 6.8 %all-to-all-done.refs_2_ = f32[8,64,768]{2,1,0:T(8,128)S(1)} async-done(((f32[8,64,768]{2,1,0:T(8,128)}), f32[8,64,768]{2,1,0:T(8,128)S(1)}, u32[]{:S(2)}, u32[]{:S(2)}) %all-to-all-start) | async-done | bytes 1572896 | tf_op jit(solution)/shard_map/all_to_all | solution.py:1093
  58.3 27.4 %collective-permute-done.5.refs_4_ = f32[8,64,768]{2,1,0:T(8,128)} collective-permute-done((f32[8,64,768]{2,1,0:T(8,128)S(1)}, f32[8,64,768]{2,1,0:T(8,128)}, u32[]{:S(2)}, u32[]{:S(2)}) %collective-permute-start.5) | collective-permute-done | bytes 1572896 | tf_op jit(solution)/shard_map/ppermute | solution.py:1064
  95.1 35.0 %mixer_forward.1 = (bf16[2,1024,768]{2,1,0:T(8,128)(2,1)}, bf16[2,1024,768]{2,1,0:T(8,128)(2,1)}, f32[2,3,1024,192]{3,2,1,0:T(8,128)}, f32[2,1024,192]{2,1,0:T(8...) custom-call(s32[1]{0:T(128)} %bitcast.refs_0_.own_ref, ...), custom_call_target="tpu_custom_call" | custom-call | flops 41400000512 | bytes 129600000 | tf_op jit(solution)/shard_map/mixer_forward/pallas_call | solution.py:383
  135.0 8.4 %collective-permute-done.11.refs_2_.refs_6_ = f32[8,32,384]{2,1,0:T(8,128)S(1)} collective-permute-done((f32[8,32,384]{2,1,0:T(8,128)}, f32[8,32,384]{2,1,0:T(8,128)S(1)}, u32[]{:S(2)}, u32[]{:S(2)}) %collective-permute-start.11) | collective-permute-done | bytes 393248 | tf_op jit(solution)/shard_map/ppermute | solution.py:1064
  145.1 5.7 %collective-permute-done.12.refs_3_.refs_7_ = f32[8,32,384]{2,1,0:T(8,128)S(1)} collective-permute-done((f32[8,32,384]{2,1,0:T(8,128)}, f32[8,32,384]{2,1,0:T(8,128)S(1)}, u32[]{:S(2)}, u32[]{:S(2)}) %collective-permute-start.12) | collective-permute-done | bytes 393248 | tf_op jit(solution)/shard_map/ppermute | solution.py:1064
  152.4 8.6 %hidden_forward.1 = (f32[512,768]{1,0:T(8,128)}, bf16[512,768]{1,0:T(8,128)(2,1)}, bf16[512,768]{1,0:T(8,128)(2,1)}, bf16[768,512]{1,0:T(8,128)(2,1)}, bf16[768,...) custom-call(f32[8,32,384]{2,1,0:T(8,128)} %get-tuple-element.243.refs_0_.refs_4_, ...), custom_call_target="tpu_custom_call" | custom-call | flops 10350000128 | bytes 32400000 | tf_op jit(solution)/shard_map/hidden_forward/pallas_call | solution.py:383
  166.0 17.3 %feed_forward.2 = (f32[512,768]{1,0:T(8,128)}, f32[512,768]{1,0:T(8,128)}, f32[768,768]{1,0:T(8,128)}, f32[768,768]{1,0:T(8,128)}, f32[1,768]{1,0:T(1,128)}) custom-call(s32[1]{0:T(128)} %bitcast.6.side_ref, bf16[512,768]{1,0:T(8,128)(2,1)} %get-tuple-element.257.refs_0_, bf16[512,768]{1,0:T(8,128)(2,1)} %get-tuple-element.258.refs_1_, ...), custom_call_target="tpu_custom_call" | custom-call | flops 20700000256 | bytes 64800000 | tf_op jit(solution)/shard_map/feed_forward/pallas_call | solution.py:383
  185.6 18.1 %feed_forward.3 = (f32[512,768]{1,0:T(8,128)}, f32[512,768]{1,0:T(8,128)}, f32[768,768]{1,0:T(8,128)}, f32[768,768]{1,0:T(8,128)}, f32[1,768]{1,0:T(1,128)}) custom-call(s32[1]{0:T(128)} %bitcast.6.side_ref, bf16[512,768]{1,0:T(8,128)(2,1)} %get-tuple-element.257.refs_0_, bf16[512,768]{1,0:T(8,128)(2,1)} %get-tuple-element.258.refs_1_, ...), custom_call_target="tpu_custom_call" | custom-call | flops 20700000256 | bytes 64800000 | tf_op jit(solution)/shard_map/feed_forward/pallas_call | solution.py:383
  210.0 36.4 %feed_forward_pair.1 = (f32[512,768]{1,0:T(8,128)}, f32[512,768]{1,0:T(8,128)}, f32[1,1536]{1,0:T(1,128)}, f32[768,768]{1,0:T(8,128)}, f32[768,768]{1,0:T(8,128)...) custom-call(bf16[512,768]{1,0:T(8,128)(2,1)} %get-tuple-element.257.refs_0_, bf16[512,768]{1,0:T(8,128)(2,1)} %get-tuple-element.258.refs_1_, ...), custom_call_target="tpu_custom_call" | custom-call | flops 35649998848 | bytes 111600000 | tf_op jit(solution)/shard_map/feed_forward_pair/pallas_call | solution.py:383
  256.4 11.6 %hidden_backward.1 = (f32[512,768]{1,0:T(8,128)}, f32[512,768]{1,0:T(8,128)}, f32[8,768]{1,0:T(8,128)}, f32[8,32,384]{2,1,0:T(8,128)}, f32[8,32,384]{2,1,0:T(8,1...) custom-call(f32[512,768]{1,0:T(8,128)} %get-tuple-element.249.refs_0_, ...), custom_call_target="tpu_custom_call" | custom-call | flops 17250000896 | bytes 54000000 | tf_op jit(solution)/shard_map/hidden_backward/pallas_call | solution.py:383
  284.2 6.3 %collective-permute-done.32.refs_5_ = f32[8,32,384]{2,1,0:T(8,128)} collective-permute-done((f32[8,32,384]{2,1,0:T(8,128)}, f32[8,32,384]{2,1,0:T(8,128)}, u32[]{:S(2)}, u32[]{:S(2)}) %collective-permute-start.32) | collective-permute-done | bytes 393248 | tf_op jit(solution)/shard_map/ppermute | solution.py:1064
  300.0 36.0 %mixer_backward.1 = (f32[8,512,192]{2,1,0:T(8,128)}, f32[2,3,1024,192]{3,2,1,0:T(8,128)}, f32[16,192]{1,0:T(8,128)}, f32[8,64,768]{2,1,0:T(8,128)}, f32[8,64,768...) custom-call(s32[1]{0:T(128)} %bitcast.refs_0_.own_ref, s32[1]{0:T(128)} %dynamic_slice.102.refs_1_, ...), custom_call_target="tpu_custom_call" | custom-call | flops 40249999360 | bytes 126000000 | tf_op jit(solution)/shard_map/mixer_backward/pallas_call | solution.py:383
  352.9 10.2 %input_weight_grad.1 = f32[3,192,768]{2,1,0:T(8,128)} custom-call(bf16[2,1024,768]{2,1,0:T(8,128)(2,1)} %get-tuple-element.319.nh_ref, bf16[2,1024,768]{2,1,0:T(8,128)(2,1)} %get-tuple-element.320.nl_ref, f32[2,3,1024,192]{3,2,1,0:T(8,128)} %get-tuple-element.337.gp_ref), custom_call_target="tpu_custom_call" | custom-call | flops 13799999488 | bytes 43200000 | tf_op jit(solution)/shard_map/input_weight_grad/pallas_call | solution.py:383
  365.4 6.4 %collective-permute-done.42 = f32[192,768]{1,0:T(8,128)S(1)} collective-permute-done((f32[192,768]{1,0:T(8,128)S(1)}, f32[192,768]{1,0:T(8,128)S(1)}, u32[]{:S(2)}, u32[]{:S(2)}) %collective-permute-start.42) | collective-permute-done | bytes 589856 | tf_op jit(solution)/shard_map/ppermute | solution.py:1064
  376.3 12.7 %filter_backward.1 = f32[8,256,192]{2,1,0:T(8,128)} custom-call(f32[8,512,192]{2,1,0:T(8,128)} %get-tuple-element.351.s_ref, f32[8,512,192]{2,1,0:T(8,128)} %get-tuple-element.352.g_ref, bf16[256,512]{1,0:T(8,128)(2,1)} %constant.216.clone.refs_16_.ih_ref, bf16[256,512]{1,0:T(8,128)(2,1)} %constant.217.clone.refs_17_.il_ref), custom_call_target="tpu_custom_call" | custom-call | flops 14949999616 | bytes 46800000 | tf_op jit(solution)/shard_map/filter_backward/pallas_call | solution.py:383
  389.0 10.7 %collective-permute-done.46 = f32[96,768]{1,0:T(8,128)S(1)} collective-permute-done((f32[96,768]{1,0:T(8,128)S(1)}, f32[96,768]{1,0:T(8,128)S(1)}, u32[]{:S(2)}, u32[]{:S(2)}) %collective-permute-start.46) | collective-permute-done | bytes 294944 | tf_op jit(solution)/shard_map/ppermute | solution.py:1064
  436.9 20.0 %collective-permute-done.49 = f32[96,768]{1,0:T(8,128)} collective-permute-done((f32[96,768]{1,0:T(8,128)}, f32[96,768]{1,0:T(8,128)}, u32[]{:S(2)}, u32[]{:S(2)}) %collective-permute-start.49) | collective-permute-done | bytes 294944 | tf_op jit(solution)/shard_map/ppermute | solution.py:1064
  468.7 15.5 %collective-permute-done.53 = f32[96,768]{1,0:T(8,128)S(1)} collective-permute-done((f32[96,768]{1,0:T(8,128)S(1)}, f32[96,768]{1,0:T(8,128)S(1)}, u32[]{:S(2)}, u32[]{:S(2)}) %collective-permute-start.53) | collective-permute-done | bytes 294944 | tf_op jit(solution)/shard_map/ppermute | solution.py:1064
  490.9 5.6 %collective-permute-done.60 = f32[30720]{0:T(1024)S(1)} collective-permute-done((f32[30720]{0:T(1024)S(1)}, f32[30720]{0:T(1024)S(1)}, u32[]{:S(2)}, u32[]{:S(2)}) %collective-permute-start.60) | collective-permute-done | bytes 122912 | tf_op jit(solution)/shard_map/ppermute | solution.py:1064
  506.5 13.1 %collective-permute-done.64 = f32[30720]{0:T(1024)S(1)} collective-permute-done((f32[30720]{0:T(1024)S(1)}, f32[30720]{0:T(1024)S(1)}, u32[]{:S(2)}, u32[]{:S(2)}) %collective-permute-start.64) | collective-permute-done | bytes 122912 | tf_op jit(solution)/shard_map/ppermute | solution.py:1064
  526.3 5.8 %put_together.2 = f32[8,256,768]{2,1,0:T(8,128)} custom-call(s32[1]{0:T(128)} %bitcast.refs_0_.own_ref, f32[8,64,768]{2,1,0:T(8,128)} %all-to-all-done.3.refs_0_, f32[8,64,768]{2,1,0:T(8,128)} %collective-permute-done.65.refs_1_, f32[8,64,768]{2,1,0:T(8,128)} %collective-permute-done.59.refs_2_, f32[8,64,768]{2,1,0:T(8,128)} %collective-permute-done.66.refs_3_), custom_call_target="tpu_custom_call" | custom-call | flops 9200000000 | bytes 28800000 | tf_op jit(solution)/shard_map/put_together/pallas_call | solution.py:383
  539.0 5.8 %put_together.3 = f32[8,256,768]{2,1,0:T(8,128)} custom-call(s32[1]{0:T(128)} %bitcast.refs_0_.own_ref, f32[8,64,768]{2,1,0:T(8,128)} %all-to-all-done.2.refs_0_, f32[8,64,768]{2,1,0:T(8,128)} %copy-done.63, f32[8,64,768]{2,1,0:T(8,128)} %collective-permute-done.52.refs_2_, f32[8,64,768]{2,1,0:T(8,128)} %collective-permute-done.69.refs_3_), custom_call_target="tpu_custom_call" | custom-call | flops 9200000000 | bytes 28800000 | tf_op jit(solution)/shard_map/put_together/pallas_call | solution.py:383
  (416 shorter events, 208.0 us)
Async XLA Ops:
  0.7 37.2 %collective-permute-start.1 = (f32[768]{0:T(1024)}, f32[768]{0:T(1024)S(1)}, u32[]{:S(2)}, u32[]{:S(2)}) collective-permute-start(f32[768]{0:T(1024)} %param.48), channel_id=1, source_target_pairs={{0,1},{1,0},{2,3},{3,2},{4,5},{5,4},{6,7},{7,6},{8,9},{9,8},{10,11... | collective-permute-start | bytes 9224 | tf_op jit(solution)/shard_map/ppermute | solution.py:1064
  1.2 36.7 %collective-permute-start.2 = (f32[768]{0:T(1024)}, f32[768]{0:T(1024)S(1)}, u32[]{:S(2)}, u32[]{:S(2)}) collective-permute-start(f32[768]{0:T(1024)} %param.48), channel_id=1, source_target_pairs={{0,2},{1,3},{2,0},{3,1},{4,6},{5,7},{6,4},{7,5},{8,10},{9,11},{10,... | collective-permute-start | bytes 9224 | tf_op jit(solution)/shard_map/ppermute | solution.py:1064
  6.5 43.5 %all-to-all-start = ((f32[8,64,768]{2,1,0:T(8,128)}), f32[8,64,768]{2,1,0:T(8,128)S(1)}, u32[]{:S(2)}, u32[]{:S(2)}) async-start(f32[8,64,768]{2,1,0:T(8,128)} %constant_dynamic-slice_fusion.14), calls=%async_computation | async-start | bytes 3145728 | tf_op jit(solution)/shard_map/all_to_all | solution.py:1093
  50.0 35.6 %collective-permute-start.5 = (f32[8,64,768]{2,1,0:T(8,128)S(1)}, f32[8,64,768]{2,1,0:T(8,128)}, u32[]{:S(2)}, u32[]{:S(2)}) collective-permute-start(f32[8,64,768]{2,1,0:T(8,128)S(1)} %all-to-all-done.refs_2_), channel_id=1, source_target_pairs={{0,2},{1,3},{2,0},{3,1},{4,6},{5,7},{6,4},{7,5},{8,10},{9,11},{10,... | collective-permute-start | bytes 4718600 | tf_op jit(solution)/shard_map/ppermute | solution.py:1064
  54.2 40.8 %all-to-all-start.1 = ((f32[8,64,768]{2,1,0:T(8,128)}), f32[8,64,768]{2,1,0:T(8,128)S(1)}, u32[]{:S(2)}, u32[]{:S(2)}) async-start(f32[8,64,768]{2,1,0:T(8,128)} %constant_dynamic-slice_fusion.12), calls=%async_computation.1 | async-start | bytes 3145728 | tf_op jit(solution)/shard_map/all_to_all | solution.py:1093
  58.2 36.9 %collective-permute-start.4 = (f32[8,64,768]{2,1,0:T(8,128)S(1)}, f32[8,64,768]{2,1,0:T(8,128)}, u32[]{:S(2)}, u32[]{:S(2)}) collective-permute-start(f32[8,64,768]{2,1,0:T(8,128)S(1)} %all-to-all-done.refs_2_), channel_id=1, source_target_pairs={{0,1},{1,0},{2,3},{3,2},{4,5},{5,4},{6,7},{7,6},{8,9},{9,8},{10,11... | collective-permute-start | bytes 4718600 | tf_op jit(solution)/shard_map/ppermute | solution.py:1064
  89.8 41.3 %collective-permute-start.7 = (f32[768,384]{1,0:T(8,128)}, f32[768,384]{1,0:T(8,128)}, u32[]{:S(2)}, u32[]{:S(2)}) collective-permute-start(f32[768,384]{1,0:T(8,128)} %constant_dynamic-slice_fusion.11), channel_id=1, source_target_pairs={{0,2},{1,3},{2,0},{3,1},{4,6},{5,7},{6,4},{7,5},{8,10},{9,11},{10,... | collective-permute-start | bytes 3538952 | tf_op jit(solution)/shard_map/ppermute | solution.py:1064
  91.3 39.8 %collective-permute-start.8 = (f32[192,768]{1,0:T(8,128)}, f32[192,768]{1,0:T(8,128)}, u32[]{:S(2)}, u32[]{:S(2)}) collective-permute-start(f32[192,768]{1,0:T(8,128)} %refs_8_.3), channel_id=1, source_target_pairs={{0,2},{1,3},{2,0},{3,1},{4,6},{5,7},{6,4},{7,5},{8,10},{9,11},{10,... | collective-permute-start | bytes 1769480 | tf_op jit(solution)/shard_map/ppermute | solution.py:1064
  91.8 39.3 %collective-permute-start.9 = (f32[384,768]{1,0:T(8,128)}, f32[384,768]{1,0:T(8,128)}, u32[]{:S(2)}, u32[]{:S(2)}) collective-permute-start(f32[384,768]{1,0:T(8,128)} %collective-permute-done.refs_7_), channel_id=1, source_target_pairs={{0,4},{4,0},{8,12},{12,8},{16,20},{20,16},{24,28},{28,24},{1,5},{5... | collective-permute-start | bytes 3538952 | tf_op jit(solution)/shard_map/ppermute | solution.py:1064
  206.7 39.7 %collective-permute-start.24 = (f32[512,768]{1,0:T(8,128)S(1)}, f32[512,768]{1,0:T(8,128)}, u32[]{:S(2)}, u32[]{:S(2)}) collective-permute-start(f32[512,768]{1,0:T(8,128)S(1)} %slice_add_fusion), channel_id=1, source_target_pairs={{0,2},{1,3},{2,0},{3,1},{4,6},{5,7},{6,4},{7,5},{8,10},{9,11},{10,... | collective-permute-start | bytes 4718600 | tf_op jit(solution)/shard_map/ppermute | solution.py:1064
  208.5 37.9 %collective-permute-start.25 = (f32[384,768]{1,0:T(8,128)S(1)}, f32[384,768]{1,0:T(8,128)S(1)}, u32[]{:S(2)}, u32[]{:S(2)}) collective-permute-start(f32[384,768]{1,0:T(8,128)S(1)} %dynamic-slice_add_fusion.1), channel_id=1, source_target_pairs={{0,4},{4,0},{8,12},{12,8},{16,20},{20,16},{24,28},{28,24},{1,5},{5... | collective-permute-start | bytes 3538952 | tf_op jit(solution)/shard_map/ppermute | solution.py:1064
  255.7 35.8 %collective-permute-start.33 = (f32[384,768]{1,0:T(8,128)}, f32[384,768]{1,0:T(8,128)S(1)}, u32[]{:S(2)}, u32[]{:S(2)}) collective-permute-start(f32[384,768]{1,0:T(8,128)} %dynamic-slice_add_fusion), channel_id=1, source_target_pairs={{0,4},{4,0},{8,12},{12,8},{16,20},{20,16},{24,28},{28,24},{1,5},{5... | collective-permute-start | bytes 3538952 | tf_op jit(solution)/shard_map/ppermute | solution.py:1064
  272.4 64.5 %all-to-all-start.2 = ((f32[8,64,768]{2,1,0:T(8,128)}), f32[8,64,768]{2,1,0:T(8,128)}, u32[]{:S(2)}, u32[]{:S(2)}) async-start(f32[8,64,768]{2,1,0:T(8,128)} %bitcast.47), calls=%async_computation.2 | async-start | bytes 3145728 | tf_op jit(solution)/shard_map/all_to_all | solution.py:1093
  278.1 57.9 %collective-permute-start.37 = (f32[96,768]{1,0:T(8,128)S(1)}, f32[96,768]{1,0:T(8,128)S(1)}, u32[]{:S(2)}, u32[]{:S(2)}) collective-permute-start(f32[96,768]{1,0:T(8,128)S(1)} %constant_dynamic-slice_fusion.5), channel_id=1, source_target_pairs={{0,16},{4,20},{8,24},{12,28},{16,0},{20,4},{24,8},{28,12},{1,17},{... | collective-permute-start | bytes 884744 | tf_op jit(solution)/shard_map/ppermute | solution.py:1064
  292.5 44.4 %collective-permute-start.34 = (f32[2,192,768]{2,1,0:T(8,128)S(1)}, f32[2,192,768]{2,1,0:T(8,128)}, u32[]{:S(2)}, u32[]{:S(2)}) collective-permute-start(f32[2,192,768]{2,1,0:T(8,128)S(1)} %copy-done.64), channel_id=1, source_target_pairs={{0,2},{1,3},{2,0},{3,1},{4,6},{5,7},{6,4},{7,5},{8,10},{9,11},{10,... | collective-permute-start | bytes 3538952 | tf_op jit(solution)/shard_map/ppermute | solution.py:1064
  296.2 39.8 %collective-permute-start.35 = (f32[192,768]{1,0:T(8,128)S(1)}, f32[192,768]{1,0:T(8,128)S(1)}, u32[]{:S(2)}, u32[]{:S(2)}) collective-permute-start(f32[192,768]{1,0:T(8,128)S(1)} %constant_dynamic-slice_fusion.6), channel_id=1, source_target_pairs={{0,8},{4,12},{8,0},{12,4},{16,24},{20,28},{24,16},{28,20},{1,9},{5... | collective-permute-start | bytes 1769480 | tf_op jit(solution)/shard_map/ppermute | solution.py:1064
  297.6 39.3 %collective-permute-start.36 = (f32[384,768]{1,0:T(8,128)S(1)}, f32[384,768]{1,0:T(8,128)}, u32[]{:S(2)}, u32[]{:S(2)}) collective-permute-start(f32[384,768]{1,0:T(8,128)S(1)} %get-tuple-element.328), channel_id=1, source_target_pairs={{0,4},{4,0},{8,12},{12,8},{16,20},{20,16},{24,28},{28,24},{1,5},{5... | collective-permute-start | bytes 3538952 | tf_op jit(solution)/shard_map/ppermute | solution.py:1064
  337.9 62.0 %collective-permute-start.43 = (f32[8,64,768]{2,1,0:T(8,128)}, f32[8,64,768]{2,1,0:T(8,128)}, u32[]{:S(2)}, u32[]{:S(2)}) collective-permute-start(f32[8,64,768]{2,1,0:T(8,128)} %get-tuple-element.346), channel_id=1, source_target_pairs={{0,1},{1,0},{2,3},{3,2},{4,5},{5,4},{6,7},{7,6},{8,9},{9,8},{10,11... | collective-permute-start | bytes 4718600 | tf_op jit(solution)/shard_map/ppermute | solution.py:1064
  347.7 52.1 %collective-permute-start.44 = (f32[8,64,768]{2,1,0:T(8,128)}, f32[8,64,768]{2,1,0:T(8,128)}, u32[]{:S(2)}, u32[]{:S(2)}) collective-permute-start(f32[8,64,768]{2,1,0:T(8,128)} %add.249), channel_id=1, source_target_pairs={{0,2},{1,3},{2,0},{3,1},{4,6},{5,7},{6,4},{7,5},{8,10},{9,11},{10,... | collective-permute-start | bytes 4718600 | tf_op jit(solution)/shard_map/ppermute | solution.py:1064
  404.7 57.0 %all-to-all-start.3 = ((f32[8,64,768]{2,1,0:T(8,128)}), f32[8,64,768]{2,1,0:T(8,128)}, u32[]{:S(2)}, u32[]{:S(2)}) async-start(f32[8,64,768]{2,1,0:T(8,128)} %bitcast.46), calls=%async_computation.3 | async-start | bytes 3145728 | tf_op jit(solution)/shard_map/all_to_all | solution.py:1093
  411.8 47.1 %collective-permute-start.48 = (f32[192,768]{1,0:T(8,128)}, f32[192,768]{1,0:T(8,128)}, u32[]{:S(2)}, u32[]{:S(2)}) collective-permute-start(f32[192,768]{1,0:T(8,128)} %constant_dynamic-slice_fusion.1), channel_id=1, source_target_pairs={{0,8},{4,12},{8,0},{12,4},{16,24},{20,28},{24,16},{28,20},{1,9},{5... | collective-permute-start | bytes 1769480 | tf_op jit(solution)/shard_map/ppermute | solution.py:1064
  414.6 42.3 %collective-permute-start.49 = (f32[96,768]{1,0:T(8,128)}, f32[96,768]{1,0:T(8,128)}, u32[]{:S(2)}, u32[]{:S(2)}) collective-permute-start(f32[96,768]{1,0:T(8,128)} %dynamic-slice_add_fusion.7), channel_id=1, source_target_pairs={{0,16},{4,20},{8,24},{12,28},{16,0},{20,4},{24,8},{28,12},{1,17},{... | collective-permute-start | bytes 884744 | tf_op jit(solution)/shard_map/ppermute | solution.py:1064
  417.0 44.7 %collective-permute-start.52 = (f32[8,64,768]{2,1,0:T(8,128)}, f32[8,64,768]{2,1,0:T(8,128)}, u32[]{:S(2)}, u32[]{:S(2)}) collective-permute-start(f32[8,64,768]{2,1,0:T(8,128)} %all-to-all-done.2.refs_0_), channel_id=1, source_target_pairs={{0,2},{1,3},{2,0},{3,1},{4,6},{5,7},{6,4},{7,5},{8,10},{9,11},{10,... | collective-permute-start | bytes 4718600 | tf_op jit(solution)/shard_map/ppermute | solution.py:1064
  462.8 40.4 %collective-permute-start.59 = (f32[8,64,768]{2,1,0:T(8,128)}, f32[8,64,768]{2,1,0:T(8,128)}, u32[]{:S(2)}, u32[]{:S(2)}) collective-permute-start(f32[8,64,768]{2,1,0:T(8,128)} %all-to-all-done.3.refs_0_), channel_id=1, source_target_pairs={{0,2},{1,3},{2,0},{3,1},{4,6},{5,7},{6,4},{7,5},{8,10},{9,11},{10,... | collective-permute-start | bytes 4718600 | tf_op jit(solution)/shard_map/ppermute | solution.py:1064
  (127 other events, 1711.2 us)
